TPU v7x, 128 devices: a whole 4x4x4 slice. The times are simulated.
128 devices in a mesh: batch: 8 (over x, core), proto: 16 (over z, y).
Axes of the slice: x: 4, y: 4, z: 4, core: 2. Of those that a mesh axis runs over, the one named last changes fastest.
Arguments:
- teacher_feats: bfloat16 [16384, 256], P(('batch', 'proto')), may hold values from -20 to 20
- student_feats: bfloat16 [16384, 256], P(('batch', 'proto')), may hold values from -20 to 20
- teacher_protos: bfloat16 [65536, 256], P(('proto', 'batch')), may hold values from -9 to 9
- student_protos: bfloat16 [65536, 256], P(('proto', 'batch')), may hold values from -9 to 9
Outputs:
- feature_grad: float32 [16384, 256], P(('batch', 'proto'))
- proto_grad: float32 [65536, 256], P(('proto', 'batch'))
All inputs are finite; a program needn't handle non-finite values.
Results may differ from a plain program's by a relative error of at most 0.0025.
Values may be sent and summed in bfloat16 or wider, within the bound.
No kernel may reach another device: no remote copies, remote signals or barrier semaphores. Data moves between devices by JAX's collectives and lax.ppermute only.
A program may use at most 192 MiB of HBM per device.

v0:
```python
import jax
import jax.numpy as jnp
from jax import lax
from jax.sharding import PartitionSpec as P

ITERS = 3


teacher_temp = 0.07
student_temp = 0.1
epsilon = 1e-06


def normalize_rows(values):
    wide = values.astype(jnp.float32)
    scale = lax.rsqrt(jnp.sum(wide * wide, -1, keepdims=True) + epsilon)
    return (wide * scale, scale)


def project_back(grad, unit_rows, scale):
    return (grad - unit_rows * jnp.sum(unit_rows * grad, -1, keepdims=True)) * scale


def score_tile(left, right, temper):
    products = lax.dot_general(
        left, right, (((1,), (1,)), ((), ())), preferred_element_type=jnp.float32
    )
    return products / temper


def shards(teacher_feats, student_feats, teacher_protos, student_protos):
    teacher_unit, _ = normalize_rows(teacher_feats)
    student_unit, student_scale = normalize_rows(student_feats)
    tproto_unit, _ = normalize_rows(teacher_protos)
    sproto_unit, sproto_scale = normalize_rows(student_protos)
    crop_teacher, crop_student = (
        lax.all_gather(teacher_unit.astype(jnp.bfloat16), "proto", axis=0, tiled=True),
        lax.all_gather(student_unit.astype(jnp.bfloat16), "proto", axis=0, tiled=True),
    )
    proto_teacher, proto_student = (
        lax.all_gather(tproto_unit.astype(jnp.bfloat16), "batch", axis=0, tiled=True),
        lax.all_gather(sproto_unit.astype(jnp.bfloat16), "batch", axis=0, tiled=True),
    )
    crop_count = crop_teacher.shape[0]
    proto_count = proto_teacher.shape[0]
    own_rows = student_feats.shape[0]
    own_protos = student_protos.shape[0]
    stored_exp = jnp.exp(score_tile(crop_teacher, proto_teacher, teacher_temp))
    crop_weight = jnp.ones((crop_count,), jnp.float32)
    proto_weight = jnp.ones((proto_count,), jnp.float32)
    for iteration in range(ITERS):
        partial_value = jnp.dot(crop_weight, stored_exp, precision=lax.Precision.HIGHEST)
        proto_weight = 1.0 / lax.psum(partial_value, "batch")
        crop_weight = 1.0 / lax.psum(
            jnp.dot(stored_exp, proto_weight, precision=lax.Precision.HIGHEST), "proto"
        )
    student_logits = score_tile(crop_student, proto_student, student_temp)
    student_exp = jnp.exp(student_logits)
    partition = lax.psum(jnp.sum(student_exp, 1), "proto")
    targets = crop_weight[:, None] * (stored_exp * proto_weight[None, :])
    probs = student_exp / partition[:, None]
    logit_grad = ((probs - targets) / student_temp).astype(jnp.bfloat16)
    feature_total = lax.psum(
        jnp.dot(logit_grad, proto_student, preferred_element_type=jnp.float32), "proto"
    )
    feature_part = lax.dynamic_slice_in_dim(
        feature_total, lax.axis_index("proto") * own_rows, own_rows, 0
    )
    proto_local = lax.dot_general(
        logit_grad, crop_student, (((0,), (0,)), ((), ())), preferred_element_type=jnp.float32
    )
    proto_total = lax.psum(proto_local, "batch")
    proto_part = lax.dynamic_slice_in_dim(
        proto_total, lax.axis_index("batch") * own_protos, own_protos, 0
    )
    feature_grad = project_back(feature_part, student_unit, student_scale)
    proto_grad = project_back(proto_part, sproto_unit, sproto_scale)
    return (feature_grad, proto_grad)


def solution(mesh):
    in_specs = (
        P(("batch", "proto"), None),
        P(("batch", "proto"), None),
        P(("proto", "batch"), None),
        P(("proto", "batch"), None),
    )
    out_specs = (P(("batch", "proto"), None), P(("proto", "batch"), None))
    return jax.shard_map(shards, mesh=mesh, in_specs=in_specs, out_specs=out_specs, check_vma=False)
```

profile of v0, /device:TPU:0, one launch (start us, length us, event | category | flops | bytes accessed | tf_op | source)
XLA Modules:
  0.0 699.3 jit_solution(11676514138707738990)
XLA Ops:
  7.2 0.0 all-gather.9.cloned.1.call-start
  7.2 0.9 fusion.17
  8.2 1.6 fusion.18
  9.7 0.0 all-gather.9.cloned.1.call-update
  9.8 0.0 all-gather.11.cloned.1.call-start
  9.8 1.1 fusion.8
  10.9 1.8 fusion.9
  12.7 0.0 all-gather.11.cloned.1.call-update
  12.7 0.0 all-gather.5.cloned.1.call-start
  12.8 0.9 fusion.16
  13.7 1.6 fusion.12
  15.3 0.0 all-gather.5.cloned.1.call-update
  15.3 0.0 all-gather.7.cloned.1.call-start
  15.4 1.1 fusion.7
  16.5 1.8 fusion.3
  18.3 0.0 all-gather.7.cloned.1.call-update
  18.3 0.0 all-reduce.6.cloned.1.call-start
  18.3 37.8 %all-gather.9.cloned.1.call-done = bf16[2048,256]{1,0:T(8,128)(2,1)} async-done(((bf16[128,256]{1,0:T(8,128)(2,1)}), bf16[2048,256]{1,0:T(8,128)(2,1)}) %all-gather.9.cloned.1.call-update) | async-done | bytes 1048592 | tf_op jit(solution)/shard_map/all_gather | solution.py:37
  56.1 26.7 %all-gather.11.cloned.1.call-done = bf16[4096,256]{1,0:T(8,128)(2,1)} async-done(((bf16[512,256]{1,0:T(8,128)(2,1)}), bf16[4096,256]{1,0:T(8,128)(2,1)}) %all-gather.11.cloned.1.call-update) | async-done | bytes 2097168 | tf_op jit(solution)/shard_map/all_gather | solution.py:41
  82.8 18.0 %multiply_exponential_fusion = f32[2048,4096]{1,0:T(8,128)} fusion(bf16[2048,256]{1,0:T(8,128)(2,1)} %all-gather.9.cloned.1.call-done, bf16[4096,256]{1,0:T(8,128)(2,1)} %all-gather.11.cloned.1.call-done), kind=kOutput, calls=%fused_computation.1 | convolution fusion | flops 4303355904 | bytes 36700160 | tf_op jit(solution)/shard_map/dot_general | solution.py:25
  100.8 19.5 %fusion.19 = f32[1,4096]{1,0:T(1,128)S(1)} fusion(f32[2048,4096]{1,0:T(8,128)} %multiply_exponential_fusion), kind=kOutput, calls=%fused_computation.33 | convolution fusion | flops 100663296 | bytes 33570816 | tf_op jit(solution)/shard_map/dot_general | solution.py:52
  120.3 25.8 %psum.64 = f32[4096]{0:T(1024)S(1)} all-reduce(f32[4096]{0:T(1024)S(1)} %bitcast.35), channel_id=1, replica_groups=mesh['batch'=8,'proto'=16] {'batch'}, use_global_device_ids=true, to_apply=%region_6.0 | all-reduce | flops 4096 | bytes 32768 | tf_op jit(solution)/shard_map/psum | solution.py:53
  146.1 31.8 %fusion.22 = f32[1,2048]{1,0:T(1,128)S(1)} fusion(f32[2048,4096]{1,0:T(8,128)} %multiply_exponential_fusion, f32[4096,1]{0,1:T(1,128)S(1)} %bitcast.31), kind=kOutput, calls=%fused_computation.43 | convolution fusion | flops 100663296 | bytes 33579008 | tf_op jit(solution)/shard_map/dot_general | solution.py:55
  177.9 41.1 %psum.65 = f32[2048]{0:T(1024)S(1)} all-reduce(f32[2048]{0:T(1024)S(1)} %bitcast.37), channel_id=1, replica_groups=mesh['batch'=8,'proto'=16] {'proto'}, use_global_device_ids=true, to_apply=%region_7.0 | all-reduce | flops 2048 | bytes 16384 | tf_op jit(solution)/shard_map/psum | solution.py:54
  219.0 19.5 %fusion.23 = f32[1,4096]{1,0:T(1,128)S(1)} fusion(f32[2048,1]{0,1:T(1,128)S(1)} %bitcast.39, f32[2048,4096]{1,0:T(8,128)} %multiply_exponential_fusion), kind=kOutput, calls=%fused_computation.44 | convolution fusion | flops 100663296 | bytes 33579008 | tf_op jit(solution)/shard_map/dot_general | solution.py:52
  238.5 24.0 %psum.66 = f32[4096]{0:T(1024)S(1)} all-reduce(f32[4096]{0:T(1024)S(1)} %bitcast.32), channel_id=1, replica_groups=mesh['batch'=8,'proto'=16] {'batch'}, use_global_device_ids=true, to_apply=%region_8.0 | all-reduce | flops 4096 | bytes 32768 | tf_op jit(solution)/shard_map/psum | solution.py:53
  262.5 31.7 %fusion.24 = f32[1,2048]{1,0:T(1,128)S(1)} fusion(f32[2048,4096]{1,0:T(8,128)} %multiply_exponential_fusion, f32[4096,1]{0,1:T(1,128)S(1)} %bitcast.33), kind=kOutput, calls=%fused_computation.45 | convolution fusion | flops 100663296 | bytes 33579008 | tf_op jit(solution)/shard_map/dot_general | solution.py:55
  294.2 36.0 %psum.67 = f32[2048]{0:T(1024)S(1)} all-reduce(f32[2048]{0:T(1024)S(1)} %bitcast.38), channel_id=1, replica_groups=mesh['batch'=8,'proto'=16] {'proto'}, use_global_device_ids=true, to_apply=%region_9.0 | all-reduce | flops 2048 | bytes 16384 | tf_op jit(solution)/shard_map/psum | solution.py:54
  330.2 19.5 %fusion.25 = f32[1,4096]{1,0:T(1,128)S(1)} fusion(f32[2048,1]{0,1:T(1,128)S(1)} %bitcast.40, f32[2048,4096]{1,0:T(8,128)} %multiply_exponential_fusion), kind=kOutput, calls=%fused_computation.46 | convolution fusion | flops 100663296 | bytes 33579008 | tf_op jit(solution)/shard_map/dot_general | solution.py:52
  349.7 23.7 %psum.68 = f32[4096]{0:T(1024)S(1)} all-reduce(f32[4096]{0:T(1024)S(1)} %bitcast.34), channel_id=1, replica_groups=mesh['batch'=8,'proto'=16] {'batch'}, use_global_device_ids=true, to_apply=%region_10.0 | all-reduce | flops 4096 | bytes 32768 | tf_op jit(solution)/shard_map/psum | solution.py:53
  373.4 31.7 %fusion.26 = f32[1,2048]{1,0:T(1,128)S(1)} fusion(f32[2048,4096]{1,0:T(8,128)} %multiply_exponential_fusion, f32[4096,1]{0,1:T(1,128)S(1)} %bitcast.30), kind=kOutput, calls=%fused_computation.47 | convolution fusion | flops 100663296 | bytes 33579008 | tf_op jit(solution)/shard_map/dot_general | solution.py:55
  405.1 0.0 all-gather.5.cloned.1.call-done
  405.1 0.0 all-gather.7.cloned.1.call-done
  405.1 14.8 %fusion = (f32[2048]{0:T(1024)S(1)}, f32[2048,4096]{1,0:T(8,128)}) fusion(bf16[2048,256]{1,0:T(8,128)(2,1)} %all-gather.5.cloned.1.call-done, bf16[4096,256]{1,0:T(8,128)(2,1)} %all-gather.7.cloned.1.call-done), kind=kOutput, calls=%fused_computation.3 | convolution fusion | flops 4311742464 | bytes 36708352 | tf_op jit(solution)/shard_map/dot_general | solution.py:25
  420.0 71.7 %all-reduce = (f32[2048]{0:T(1024)S(1)}, f32[2048]{0:T(1024)S(1)}) all-reduce(f32[2048]{0:T(1024)S(1)} %bitcast.36, f32[2048]{0:T(1024)S(1)} %get-tuple-element.4), channel_id=1, replica_groups=mesh['batch'=8,'proto'=16] {'proto'}, use_global_device_ids=true, to_apply=%region_11.0 | all-reduce | flops 4096 | bytes 32768 | tf_op jit(solution)/shard_map/psum | solution.py:54
  491.7 0.0 copy-start.2
  491.7 27.7 %multiply_convert_fusion = bf16[2048,4096]{1,0:T(8,128)(2,1)} fusion(f32[2048,4096]{1,0:T(8,128)} %multiply_exponential_fusion, f32[2048,4096]{1,0:T(8,128)} %get-tuple-element.5, f32[4096]{0:T(1024)S(1)} %broadcast_divide_fusion, f32[2048]{0:T(1024)S(1)} %broadcast_divide_fusion.5, f32[2048]{0:T(1024)S(1)} %get-tuple-element.3), kind=kLoop, calls=%fused_computation | loop fusion | flops 58720256 | bytes 83918848 | tf_op jit(solution)/shard_map/convert_element_type | solution.py:62
  519.4 0.0 copy-done.2
  519.4 0.0 copy-start.1
  519.4 0.0 copy-start
  519.4 0.0 copy-start.3
  519.4 10.4 %fusion.28 = f32[4096,256]{1,0:T(8,128)} fusion(bf16[2048,4096]{1,0:T(8,128)(2,1)} %multiply_convert_fusion, bf16[2048,256]{1,0:T(8,128)(2,1)S(1)} %copy-done.2), kind=kOutput, calls=%fused_computation.49 | convolution fusion | flops 4294967296 | bytes 22020096 | tf_op jit(solution)/shard_map/dot_general | solution.py:69
  529.8 0.0 all-reduce.6.cloned.1.call-update
  529.9 0.0 all-reduce.4.cloned.1.call-start
  529.9 0.0 copy-done.1
  529.9 9.9 %fusion.27 = f32[2048,256]{1,0:T(8,128)} fusion(bf16[2048,4096]{1,0:T(8,128)(2,1)} %multiply_convert_fusion, bf16[4096,256]{1,0:T(8,128)(2,1)S(1)} %copy-done.1), kind=kOutput, calls=%fused_computation.48 | convolution fusion | flops 4294967296 | bytes 20971520 | tf_op jit(solution)/shard_map/dot_general | solution.py:64
  539.8 0.0 all-reduce.4.cloned.1.call-update
  539.9 55.9 %all-reduce.6.cloned.1.call-done = f32[4096,256]{1,0:T(8,128)} async-done(((f32[4096,256]{1,0:T(8,128)}), f32[4096,256]{1,0:T(8,128)}) %all-reduce.6.cloned.1.call-update) | async-done | bytes 4194320 | tf_op jit(solution)/shard_map/psum | solution.py:72
  595.8 0.0 copy-done
  595.8 1.3 fusion.4
  597.1 2.0 fusion.6
  599.1 90.4 %all-reduce.4.cloned.1.call-done = f32[2048,256]{1,0:T(8,128)} async-done(((f32[2048,256]{1,0:T(8,128)}), f32[2048,256]{1,0:T(8,128)}) %all-reduce.4.cloned.1.call-update) | async-done | bytes 2097168 | tf_op jit(solution)/shard_map/psum | solution.py:63
  689.5 0.0 copy-done.3
  689.5 1.1 fusion.13
  690.6 1.7 fusion.15
  (10 shorter events, 0.1 us)
Async XLA Ops:
  7.2 48.9 %all-gather.9.cloned.1.call-start = ((), (), s32[]{:S(2)}) async-start(), calls=%async_computation.2 | async-start | bytes 1114112 | tf_op jit(solution)/shard_map/all_gather | solution.py:37
  9.8 73.0 %all-gather.11.cloned.1.call-start = ((), (), s32[]{:S(2)}) async-start(), calls=%async_computation.3 | async-start | bytes 2359296 | tf_op jit(solution)/shard_map/all_gather | solution.py:41
  12.7 392.4 %all-gather.5.cloned.1.call-start = ((), (), s32[]{:S(2)}) async-start(), calls=%async_computation | async-start | bytes 1114112 | tf_op jit(solution)/shard_map/all_gather | solution.py:38
  15.3 389.8 %all-gather.7.cloned.1.call-start = ((), (), s32[]{:S(2)}) async-start(), calls=%async_computation.1 | async-start | bytes 2359296 | tf_op jit(solution)/shard_map/all_gather | solution.py:42
  18.3 577.5 %all-reduce.6.cloned.1.call-start = ((), (), s32[]{:S(2)}) async-start(), calls=%async_computation.5 | async-start | bytes 8388608 | tf_op jit(solution)/shard_map/psum | solution.py:72
  491.7 27.7 %copy-start.2 = (bf16[2048,256]{1,0:T(8,128)(2,1)S(1)}, bf16[2048,256]{1,0:T(8,128)(2,1)}, u32[]{:S(2)}) copy-start(bf16[2048,256]{1,0:T(8,128)(2,1)} %all-gather.5.cloned.1.call-done) | copy-start | bytes 3145732
  519.4 10.5 %copy-start.1 = (bf16[4096,256]{1,0:T(8,128)(2,1)S(1)}, bf16[4096,256]{1,0:T(8,128)(2,1)}, u32[]{:S(2)}) copy-start(bf16[4096,256]{1,0:T(8,128)(2,1)} %all-gather.7.cloned.1.call-done) | copy-start | bytes 6291460
  519.4 76.4 %copy-start = (bf16[512,256]{1,0:T(8,128)(2,1)S(1)}, bf16[512,256]{1,0:T(8,128)(2,1)}, u32[]{:S(2)}) copy-start(bf16[512,256]{1,0:T(8,128)(2,1)} %param.7) | copy-start | bytes 786436
  519.4 170.1 %copy-start.3 = (bf16[128,256]{1,0:T(8,128)(2,1)S(1)}, bf16[128,256]{1,0:T(8,128)(2,1)}, u32[]{:S(2)}) copy-start(bf16[128,256]{1,0:T(8,128)(2,1)} %param.5) | copy-start | bytes 196612
  529.9 159.6 %all-reduce.4.cloned.1.call-start = ((), (), s32[]{:S(2)}) async-start(), calls=%async_computation.4 | async-start | bytes 4194304 | tf_op jit(solution)/shard_map/psum | solution.py:63
Sparse Core Ops, SparseCore 0:
  10.7 45.3 all-gather.8
  58.4 24.3 all-gather.10
  84.9 43.2 all-gather.4
  129.7 24.3 all-gather.6
  530.0 65.7 all-reduce.5
  599.0 90.4 all-reduce.3
where the time goes:
time: 707 us; the launch traced here: 699 us
  blocking collectives  222 us (31%)
  waiting for transfers between devices  211 us (30%)
  matrix products  207 us (29%)
  other arithmetic  44.6 us (6%)
  between operations  14.5 us (2%)
    psum x3, blocking collectives, shards(): lax.psum(jnp.dot(stored_exp, proto_weight, precision=lax.Precision.HIGHES...  149 us
    dot_general x3, matrix products, shards(): jnp.dot(stored_exp, proto_weight, precision=lax.Precision.HIGHEST)  95.1 us
    psum x1, waiting for transfers between devices, shards(): lax.psum(jnp.dot(logit_grad, proto_student, preferred_element_type=jnp.fl...  90.4 us
    psum x3, blocking collectives, shards(): proto_weight = 1.0 / lax.psum(partial_value, 'batch')  73.6 us
    dot_general x3, matrix products, shards(): jnp.dot(crop_weight, stored_exp, precision=lax.Precision.HIGHEST)  58.5 us
    psum x1, waiting for transfers between devices, shards(): proto_total = lax.psum(proto_local, 'batch')  55.9 us
    all_gather x1, waiting for transfers between devices, shards(): lax.all_gather(teacher_unit.astype(jnp.bfloat16), 'proto', axis=0, tiled=...  37.8 us
    dot_general x2, matrix products, score_tile(): lax.dot_general(left, right, (((1,), (1,)), ((), ())), preferred_element_...  32.8 us
  transfers between devices with their start and end apart: 6, of which 4 were waited for; matrix products, arithmetic and copies ran while one was open for 28% of the time, Pallas kernels for 0%

commit v1 on v0

v1 whole, which is shorter than its diff:
```python
import functools

import jax
import jax.numpy as jnp
from jax import lax
from jax.experimental import pallas as pl
from jax.experimental.pallas import tpu as pltpu
from jax.sharding import PartitionSpec as P

ITERS = 3
LOG2E = 1.4426950408889634
teacher_temp = 0.07
student_temp = 0.1
epsilon = 1e-06

F32 = jnp.float32
BF16 = jnp.bfloat16
MIB = 2**20
VM = pl.BlockSpec(memory_space=pltpu.VMEM)
SM = pl.BlockSpec(memory_space=pltpu.SMEM)
NT = (((1,), (1,)), ((), ()))
NN = (((1,), (0,)), ((), ()))
TN = (((0,), (0,)), ((), ()))


def normalize_rows(values):
    wide = values.astype(F32)
    scale = lax.rsqrt(jnp.sum(wide * wide, -1, keepdims=True) + epsilon)
    return (wide * scale, scale)


def project_back(grad, unit_rows, scale):
    return (grad - unit_rows * jnp.sum(unit_rows * grad, -1, keepdims=True)) * scale


def fold(x):
    return x.reshape(-1, 8, x.shape[1]).sum(0)


def spread(row, out):
    for k in range(row.shape[1] // 128):
        part = row[:, k * 128 : (k + 1) * 128]
        out[k * 128 : (k + 1) * 128, :] = jnp.broadcast_to(part, (128, 128)).T


def gather_lanes(part, out):
    for k in range(part.shape[0] // 128):
        out[:, k * 128 : (k + 1) * 128] = part[k * 128 : (k + 1) * 128, :].T.sum(0, keepdims=True)


def exp_kernel(dim, me, feats, *refs):
    pieces, (e, c, protos, own_protos) = refs[:-4], refs[-4:]
    own = pieces[0].shape[0]
    for r, piece in enumerate(pieces):
        own_protos[r] = piece[:, :dim]
        protos[r] = piece[:, dim:]

    @pl.loop(0, len(pieces))
    def _(r):
        s = lax.dot_general(feats[:, :dim], own_protos[r], NT, preferred_element_type=F32)
        x = jnp.exp2(s * (LOG2E / teacher_temp))
        e[:, pl.ds(pl.multiple_of(r * own, own), own)] = x
        c[:, pl.ds(pl.multiple_of((me[0] ^ r) * own, own), own)] = fold(x).sum(0, keepdims=True)


def total_kernel(dim, feats, protos, z, part):
    own = protos.shape[1]
    part[...] = jnp.zeros_like(part)

    @pl.loop(0, protos.shape[0])
    def _(r):
        s = lax.dot_general(feats[:, dim:], protos[r], NT, preferred_element_type=F32)
        x = jnp.exp2(s * (LOG2E / student_temp))
        acc = x[:, :128]
        for k in range(1, own // 128):
            acc += x[:, k * 128 : (k + 1) * 128]
        part[...] += acc

    gather_lanes(part, z)


def row_kernel(block, own, me, e, c0, c1, c2, c3, r, b, part):
    rows, cols = e.shape
    for k in range(cols // own):
        src = pl.ds(pl.multiple_of((me[0] ^ k) * own, own), own)
        b[:, k * own : (k + 1) * own] = 1.0 / (c0[:, src] + c1[:, src] + c2[:, src] + c3[:, src])

    @pl.loop(0, rows // block)
    def _(i):
        ii = pl.ds(pl.multiple_of(i * block, block), block)
        acc = jnp.zeros((block, 128), F32)
        for k in range(cols // 128):
            lanes = slice(k * 128, (k + 1) * 128)
            acc += e[ii, lanes] * b[:, lanes]
        part[ii, :] = acc

    gather_lanes(part, r)


def col_kernel(block, width, own, me, e, sums, c, av):
    rows, cols = e.shape
    spread(1.0 / jnp.sum(sums[...], 0, keepdims=True), av)
    for j in range(cols // width):

        def step(i, acc, j=j):
            ii = pl.ds(pl.multiple_of(i * block, block), block)
            w = av[ii, :]
            return tuple(
                acc[k] + fold(e[ii, j * width + k * 128 : j * width + (k + 1) * 128] * w)
                for k in range(width // 128)
            )

        zero = jnp.zeros((8, 128), F32)
        acc = lax.fori_loop(0, rows // block, step, (zero,) * (width // 128))
        for k in range(width // own):
            part = jnp.concatenate(acc[k * own // 128 : (k + 1) * own // 128], 1)
            to = (me[0] ^ (j * width // own + k)) * own
            c[:, pl.ds(pl.multiple_of(to, own), own)] = part.sum(0, keepdims=True)


def grad_kernel(dim, me, e, feats, b, sums, zsums, protos, f_out, keep, give, av, zv, g0, g1, f_acc):
    own = protos.shape[1]
    spread((1.0 / student_temp) / jnp.sum(sums[...], 0, keepdims=True), av)
    spread((1.0 / student_temp) / jnp.sum(zsums[...], 0, keepdims=True), zv)
    f_acc[...] = jnp.zeros_like(f_acc)
    wide = lambda m: jnp.concatenate([m] * (own // 128), 1)

    @pl.loop(0, protos.shape[0] // 2)
    def _(h):
        for k, (g, out) in enumerate(((g0, keep), (g1, give))):
            cols = pl.ds(pl.multiple_of((2 * h + k) * own, own), own)
            sp = protos[2 * h + k]
            s = lax.dot_general(feats[:, dim:], sp, NT, preferred_element_type=F32)
            p = jnp.exp2(s * (LOG2E / student_temp))
            g[...] = (p * wide(zv[...]) - wide(av[...]) * (e[:, cols] * b[:, cols])).astype(BF16)
            out[h] = lax.dot_general(g[...], feats[:, dim:], TN, preferred_element_type=F32)
            f_acc[...] += lax.dot_general(g[...], sp, NN, preferred_element_type=F32)
    f_out[...] = f_acc[...].astype(BF16).reshape(f_out.shape)


def call(kernel, name, out_shape, ops, scratch=(), limit=22, smem=0):
    many = isinstance(out_shape, (list, tuple))
    return pl.pallas_call(
        kernel,
        out_shape=out_shape,
        in_specs=[SM] * smem + [VM] * (len(ops) - smem),
        out_specs=[VM] * len(out_shape) if many else VM,
        scratch_shapes=list(scratch),
        compiler_params=pltpu.CompilerParams(vmem_limit_bytes=limit * MIB),
        name=name,
    )(*ops)


def shards(nb, npr, teacher_feats, student_feats, teacher_protos, student_protos):
    sds = jax.ShapeDtypeStruct
    swap = lambda x, k: lax.ppermute(x, "batch", [(i, i ^ k) for i in range(nb)])

    def over_proto(x):
        return lax.all_to_all(jnp.broadcast_to(x[None], (npr,) + x.shape), "proto", 0, 0)

    dim = teacher_feats.shape[1]
    own_rows, own = student_feats.shape[0], student_protos.shape[0]
    rows, cols = own_rows * npr, own * nb
    me = lax.axis_index("batch").astype(jnp.int32).reshape(1)
    teacher_unit, _ = normalize_rows(teacher_feats)
    student_unit, student_scale = normalize_rows(student_feats)
    tproto_unit, _ = normalize_rows(teacher_protos)
    sproto_unit, sproto_scale = normalize_rows(student_protos)
    mine = jnp.concatenate([tproto_unit, sproto_unit], 1).astype(BF16)
    pieces = [None] * nb
    pieces[0] = mine
    for r in range(2, nb, 2):
        pieces[r] = swap(mine, r)
    feats = over_proto(jnp.concatenate([teacher_unit, student_unit], 1).astype(BF16))
    feats = feats.reshape(rows, 2 * dim)
    for r in range(0, nb, 2):
        pieces[r + 1] = swap(pieces[r], 1)

    e, c, protos = call(
        functools.partial(exp_kernel, dim),
        "teacher_exp",
        [pltpu.VMEM((rows, cols), F32), sds((1, cols), F32), pltpu.VMEM((nb, own, dim), BF16)],
        [me, feats, *pieces],
        [pltpu.VMEM((nb, own, dim), BF16)],
        smem=1,
    )
    e = pltpu.with_memory_space_constraint(e, pltpu.VMEM)
    protos = pltpu.with_memory_space_constraint(protos, pltpu.VMEM)
    lanes = pltpu.VMEM((rows, 128), F32)
    z = call(
        functools.partial(total_kernel, dim),
        "student_total",
        sds((1, rows), F32),
        [feats, protos],
        [lanes],
    )
    for iteration in range(ITERS):
        if iteration:
            c = call(
                functools.partial(col_kernel, 128, 2048, own),
                "column_sums",
                sds((1, cols), F32),
                [me, e, sums],
                [lanes],
                smem=1,
            )
        c = c + swap(c, 1)
        cs = [c] + [swap(c, k) for k in range(2, nb, 2)]
        r, b = call(
            functools.partial(row_kernel, 128, own),
            "row_sums",
            [sds((1, rows), F32), sds((1, cols), F32)],
            [me, e, *cs],
            [lanes],
            smem=1,
        )
        if iteration == 0:
            both = over_proto(jnp.concatenate([r, z], 0))
            sums, zsums = both[:, 0], both[:, 1]
        else:
            sums = over_proto(r).reshape(npr, rows)
    half_g = pltpu.VMEM((rows, own), BF16)
    f, keep, give = call(
        functools.partial(grad_kernel, dim),
        "logit_grad",
        [
            sds((npr, own_rows, dim), BF16),
            sds((nb // 2, own, dim), F32),
            sds((nb // 2, own, dim), F32),
        ],
        [me, e, feats, b, sums, zsums, protos],
        [lanes, lanes, half_g, half_g, pltpu.VMEM((rows, dim), F32)],
        smem=1,
    )
    half = keep + swap(give, 1)
    sent = [swap(half[k].astype(BF16), 2 * k) for k in range(1, nb // 2)]
    f = lax.all_to_all(f, "proto", 0, 0)
    feature_part = jnp.sum(f.astype(F32), 0)
    proto_part = half[0] + sum(x.astype(F32) for x in sent)
    feature_grad = project_back(feature_part, student_unit, student_scale)
    proto_grad = project_back(proto_part, sproto_unit, sproto_scale)
    return (feature_grad, proto_grad)


def solution(mesh):
    nb, npr = mesh.shape["batch"], mesh.shape["proto"]
    in_specs = (
        P(("batch", "proto"), None),
        P(("batch", "proto"), None),
        P(("proto", "batch"), None),
        P(("proto", "batch"), None),
    )
    out_specs = (P(("batch", "proto"), None), P(("proto", "batch"), None))
    return jax.shard_map(
        functools.partial(shards, nb, npr),
        mesh=mesh,
        in_specs=in_specs,
        out_specs=out_specs,
        check_vma=False,
    )
```

time: 707 us -> 250 us (0.35)
  matrix products: 207 us -> 0 us
  blocking collectives: 222 us -> 46.7 us
  waiting for transfers between devices: 211 us -> 53.9 us
  Pallas kernels: 0 us -> 59.7 us
  local copies, waits for them, and re-layouts: 0.02 us -> 44.7 us
  other arithmetic: 44.6 us -> 9.09 us
  starting transfers between devices: 0.25 us -> 33.3 us
  between operations: 14.5 us -> 0.98 us
    psum x6 -> x0, blocking collectives: 222 us -> none  [the longest x3 149 us: shards(): lax.psum(jnp.dot(stored_exp, proto_weight, precision=lax.Precision.HIGHES...]
    dot_general x10 -> x0, matrix products: 207 us -> none  [the longest x3 95.1 us: shards(): jnp.dot(stored_exp, proto_weight, precision=lax.Precision.HIGHEST)]
    psum x2 -> x0, waiting for transfers between devices: 146 us -> none  [the longest x1 90.4 us: shards(): lax.psum(jnp.dot(logit_grad, proto_student, preferred_element_type=jnp.fl...]
    all_gather x4 -> x0, waiting for transfers between devices: 64.5 us -> none  [the longest x1 37.8 us: shards(): lax.all_gather(teacher_unit.astype(jnp.bfloat16), 'proto', axis=0, tiled=...]
    pallas_call x0 -> x8, Pallas kernels: none -> 59.7 us  [call(): pl.pallas_call(kernel, out_shape=out_shape, in_specs=[SM] * smem + [VM] *...]
    all_to_all x0 -> x3, blocking collectives: none -> 46.7 us  [the longest x2 24.9 us: over_proto(): lax.all_to_all(jnp.broadcast_to(x[None], (npr,) + x.shape), 'proto', 0, 0)]
    ppermute x0 -> x23, waiting for transfers between devices: none -> 45.3 us  [shards(): lax.ppermute(x, 'batch', [(i, i ^ k) for i in range(nb)])]
    unnamed x8 -> x54, local copies, waits for them, and re-layouts: 0.02 us -> 40.6 us
  transfers between devices with their start and end apart: 6 -> 25, of which waited for: 4 -> 17; matrix products, arithmetic and copies ran while one was open for 28% -> 1% of each run, Pallas kernels for 0% -> 3%
where the time goes in v1:
time: 250 us; the launch traced here: 248 us
  Pallas kernels  59.7 us (24%)
  waiting for transfers between devices  53.9 us (22%)
  blocking collectives  46.7 us (19%)
  local copies, waits for them, and re-layouts  44.7 us (18%)
  starting transfers between devices  33.3 us (13%)
  other arithmetic  9.09 us (4%)
    pallas_call x8, Pallas kernels, call(): pl.pallas_call(kernel, out_shape=out_shape, in_specs=[SM] * smem + [VM] *...  59.7 us
    ppermute x23, waiting for transfers between devices, shards(): lax.ppermute(x, 'batch', [(i, i ^ k) for i in range(nb)])  45.3 us
    unnamed x54, local copies, waits for them, and re-layouts  40.6 us
    all_to_all x2, blocking collectives, over_proto(): lax.all_to_all(jnp.broadcast_to(x[None], (npr,) + x.shape), 'proto', 0, 0)  24.9 us
    all_to_all x1, blocking collectives, shards(): f = lax.all_to_all(f, 'proto', 0, 0)  21.8 us
    ppermute x23, starting transfers between devices, shards(): lax.ppermute(x, 'batch', [(i, i ^ k) for i in range(nb)])  21.5 us
    all_to_all x2, starting transfers between devices, over_proto(): lax.all_to_all(jnp.broadcast_to(x[None], (npr,) + x.shape), 'proto', 0, 0)  11.8 us
    all_to_all x2, waiting for transfers between devices, over_proto(): lax.all_to_all(jnp.broadcast_to(x[None], (npr,) + x.shape), 'proto', 0, 0)  8.63 us
  transfers between devices with their start and end apart: 25, of which 17 were waited for; matrix products, arithmetic and copies ran while one was open for 1% of the time, Pallas kernels for 3%

profile of v1, /device:TPU:0, one launch (start us, length us, event | category | flops | bytes accessed | tf_op | source)
XLA Modules:
  0.0 248.4 jit_solution(1457019213277937119)
XLA Ops:
  0.6 0.9 fusion.13
  1.6 1.0 fusion.18
  2.6 1.0 fusion.12
  3.6 1.6 broadcast_in_dim.12
  5.1 8.3 %all-to-all-start = ((bf16[16,128,512]{2,1,0:T(8,128)(2,1)}), bf16[16,128,512]{2,1,0:T(8,128)(2,1)S(1)}, u32[]{:S(2)}, u32[]{:S(2)}) async-start(bf16[16,128,512]{2,1,0:T(8,128)(2,1)} %broadcast_in_dim.12), calls=%async_computation | async-start | bytes 4194304 | tf_op jit(solution)/shard_map/all_to_all | solution.py:159
  14.0 2.8 %collective-permute-start.5 = (bf16[512,512]{1,0:T(8,128)(2,1)S(1)}, bf16[512,512]{1,0:T(8,128)(2,1)S(1)}, u32[]{:S(2)}, u32[]{:S(2)}) collective-permute-start(bf16[512,512]{1,0:T(8,128)(2,1)S(1)} %pad_maximum_fusion.refs_0_), channel_id=1, source_target_pairs={{0,96},{16,112},{32,64},{48,80},{64,32},{80,48},{96,0},{112,16},{1... | collective-permute-start | bytes 1572872 | tf_op jit(solution)/shard_map/ppermute | solution.py:156
  16.8 0.8 collective-permute-start.3
  18.2 21.7 %collective-permute-done.5.refs_6_ = bf16[512,512]{1,0:T(8,128)(2,1)S(1)} collective-permute-done((bf16[512,512]{1,0:T(8,128)(2,1)S(1)}, bf16[512,512]{1,0:T(8,128)(2,1)S(1)}, u32[]{:S(2)}, u32[]{:S(2)}) %collective-permute-start.5) | collective-permute-done | bytes 524320 | tf_op jit(solution)/shard_map/ppermute | solution.py:156
  40.7 1.3 collective-permute-done.6.refs_7_
  42.0 1.0 collective-permute-done.4.refs_5_
  42.9 0.7 collective-permute-done.2.refs_3_
  43.7 1.4 all-to-all-done
  45.1 1.3 copy-done.3
  46.4 9.7 %teacher_exp.1 = (f32[2048,4096]{1,0:T(8,128)S(1)}, f32[1,4096]{1,0:T(1,128)}, bf16[8,512,256]{2,1,0:T(8,128)(2,1)S(1)}) custom-call(s32[1]{0:T(128)} %bitcast.me, bf16[2048,512]{1,0:T(8,128)(2,1)} %bitcast.30, bf16[512,512]{1,0:T(8,128)(2,1)} %copy-done.9, bf16[512,512]{1,0:T(8,128)(2,1)} %collective-permute-done.refs_1_, ...), custom_call_target="tpu_custom_call" | custom-call | tf_op jit(solution)/shard_map/teacher_exp/pallas_call | solution.py:143
  56.1 11.1 %copy-done = f32[2048,4096]{1,0:T(8,128)} copy-done((f32[2048,4096]{1,0:T(8,128)}, f32[2048,4096]{1,0:T(8,128)S(1)}, u32[]{:S(2)}) %copy-start) | copy-done | bytes 33554456
  67.1 1.4 collective-permute-done.7
  68.5 0.7 add.57.c0
  69.3 2.8 %collective-permute-start.10 = (f32[1,4096]{1,0:T(1,128)S(1)}, f32[1,4096]{1,0:T(1,128)S(1)}, u32[]{:S(2)}, u32[]{:S(2)}) collective-permute-start(f32[1,4096]{1,0:T(1,128)S(1)} %add.57.c0), channel_id=1, source_target_pairs={{0,96},{16,112},{32,64},{48,80},{64,32},{80,48},{96,0},{112,16},{1... | collective-permute-start | bytes 49160 | tf_op jit(solution)/shard_map/ppermute | solution.py:156
  72.1 0.8 collective-permute-start.9
  73.5 1.6 copy-done.4
  75.0 6.3 %student_total.1 = f32[1,2048]{1,0:T(1,128)S(1)} custom-call(bf16[2048,512]{1,0:T(8,128)(2,1)S(1)} %bitcast.32, bf16[8,512,256]{2,1,0:T(8,128)(2,1)S(1)} %get-tuple-element.15.protos), custom_call_target="tpu_custom_call" | custom-call | tf_op jit(solution)/shard_map/student_total/pallas_call | solution.py:143
  82.1 10.5 %copy-done.1 = f32[2048,4096]{1,0:T(8,128)S(1)} copy-done((f32[2048,4096]{1,0:T(8,128)S(1)}, f32[2048,4096]{1,0:T(8,128)}, u32[]{:S(2)}) %copy-start.1) | copy-done | bytes 33554456
  92.6 4.3 %row_sums.3 = (f32[1,2048]{1,0:T(1,128)}, f32[1,4096]{1,0:T(1,128)}) custom-call(s32[1]{0:T(128)} %bitcast.me, f32[2048,4096]{1,0:T(8,128)S(1)} %copy-done.1, f32[1,4096]{1,0:T(1,128)} %copy-done.13, f32[1,4096]{1,0:T(1,128)} %copy-done.22, f32[1,4096]{1,0:T(1,128)} %copy-done.19, f32[1,4096]{1,0:T(1,128)} %copy-done.16), custom_call_target="tpu_custom_call" | custom-call | tf_op jit(solution)/shard_map/row_sums/pallas_call | solution.py:143
  96.9 0.7 pad_maximum_fusion.2
  97.7 14.1 %all_to_all.25 = f32[16,2,2048]{2,1,0:T(2,128)S(1)} all-to-all(f32[16,2,2048]{2,1,0:T(2,128)S(1)} %broadcast_in_dim.13), channel_id=1, replica_groups=mesh['batch'=8,'proto'=16] {'proto'}, dimensions={0} | all-to-all | bytes 524288 | tf_op jit(solution)/shard_map/all_to_all | solution.py:159
  112.0 0.7 copy.17
  112.7 4.6 %column_sums.2 = f32[1,4096]{1,0:T(1,128)} custom-call(s32[1]{0:T(128)} %bitcast.me, f32[2048,4096]{1,0:T(8,128)S(1)} %copy-done.1, f32[16,2048]{1,0:T(8,128)} %bitcast.35), custom_call_target="tpu_custom_call" | custom-call | tf_op jit(solution)/shard_map/column_sums/pallas_call | solution.py:143
  117.3 1.4 collective-permute-done.11
  118.7 0.7 add.58.c0
  119.4 2.8 %collective-permute-start.14 = (f32[1,4096]{1,0:T(1,128)S(1)}, f32[1,4096]{1,0:T(1,128)S(1)}, u32[]{:S(2)}, u32[]{:S(2)}) collective-permute-start(f32[1,4096]{1,0:T(1,128)S(1)} %add.58.c0), channel_id=1, source_target_pairs={{0,96},{16,112},{32,64},{48,80},{64,32},{80,48},{96,0},{112,16},{1... | collective-permute-start | bytes 49160 | tf_op jit(solution)/shard_map/ppermute | solution.py:156
  122.3 1.3 collective-permute-start.12
  123.6 0.9 collective-permute-done.14.c3
  124.5 3.1 %collective-permute-done.13.c2 = f32[1,4096]{1,0:T(1,128)S(1)} collective-permute-done((f32[1,4096]{1,0:T(1,128)S(1)}, f32[1,4096]{1,0:T(1,128)S(1)}, u32[]{:S(2)}, u32[]{:S(2)}) %collective-permute-start.13) | collective-permute-done | bytes 16416 | tf_op jit(solution)/shard_map/ppermute | solution.py:156
  127.5 0.6 copy-done.20
  128.1 0.6 copy-done.23
  128.7 4.3 %row_sums.4 = (f32[1,2048]{1,0:T(1,128)}, f32[1,4096]{1,0:T(1,128)}) custom-call(s32[1]{0:T(128)} %bitcast.me, f32[2048,4096]{1,0:T(8,128)S(1)} %copy-done.1, f32[1,4096]{1,0:T(1,128)} %copy-done.14, f32[1,4096]{1,0:T(1,128)} %copy-done.23, f32[1,4096]{1,0:T(1,128)} %copy-done.20, f32[1,4096]{1,0:T(1,128)} %copy-done.17), custom_call_target="tpu_custom_call" | custom-call | tf_op jit(solution)/shard_map/row_sums/pallas_call | solution.py:143
  133.1 0.8 broadcast_in_dim.15
  133.8 10.9 %all_to_all.26 = f32[16,1,2048]{2,1,0:T(1,128)S(1)} all-to-all(f32[16,1,2048]{2,1,0:T(1,128)S(1)} %broadcast_in_dim.15), channel_id=1, replica_groups=mesh['batch'=8,'proto'=16] {'proto'}, dimensions={0} | all-to-all | bytes 262144 | tf_op jit(solution)/shard_map/all_to_all | solution.py:159
  144.7 0.7 copy.19
  145.4 4.6 %column_sums.3 = f32[1,4096]{1,0:T(1,128)} custom-call(s32[1]{0:T(128)} %bitcast.me, f32[2048,4096]{1,0:T(8,128)S(1)} %copy-done.1, f32[16,2048]{1,0:T(8,128)} %bitcast.36), custom_call_target="tpu_custom_call" | custom-call | tf_op jit(solution)/shard_map/column_sums/pallas_call | solution.py:143
  150.0 1.4 collective-permute-done.15
  151.4 0.7 add.59.c0
  152.2 0.6 collective-permute-start.18
  152.7 1.1 collective-permute-start.17
  153.8 2.6 %collective-permute-start.16 = (f32[1,4096]{1,0:T(1,128)S(1)}, f32[1,4096]{1,0:T(1,128)S(1)}, u32[]{:S(2)}, u32[]{:S(2)}) collective-permute-start(f32[1,4096]{1,0:T(1,128)S(1)} %add.59.c0), channel_id=1, source_target_pairs={{0,32},{16,48},{32,0},{48,16},{64,96},{80,112},{96,64},{112,80},{1... | collective-permute-start | bytes 49160 | tf_op jit(solution)/shard_map/ppermute | solution.py:156
  156.3 0.9 collective-permute-done.18.c3
  157.2 0.8 collective-permute-done.17.c2
  158.6 0.6 copy-done.24
  159.2 4.5 %row_sums.5 = (f32[1,2048]{1,0:T(1,128)}, f32[1,4096]{1,0:T(1,128)}) custom-call(s32[1]{0:T(128)} %bitcast.me, f32[2048,4096]{1,0:T(8,128)S(1)} %copy-done.1, f32[1,4096]{1,0:T(1,128)} %copy-done.15, f32[1,4096]{1,0:T(1,128)} %copy-done.24, f32[1,4096]{1,0:T(1,128)} %copy-done.21, f32[1,4096]{1,0:T(1,128)} %copy-done.18), custom_call_target="tpu_custom_call" | custom-call | tf_op jit(solution)/shard_map/row_sums/pallas_call | solution.py:143
  163.6 1.4 broadcast_in_dim.17
  165.1 3.5 %all-to-all-start.3 = ((f32[16,1,2048]{2,1,0:T(1,128)}), f32[16,1,2048]{2,1,0:T(1,128)S(1)}, u32[]{:S(2)}, u32[]{:S(2)}) async-start(f32[16,1,2048]{2,1,0:T(1,128)} %broadcast_in_dim.17), calls=%async_computation.3 | async-start | bytes 262144 | tf_op jit(solution)/shard_map/all_to_all | solution.py:159
  168.6 0.7 copy.16
  169.3 7.3 %all-to-all-done.3 = f32[16,1,2048]{2,1,0:T(1,128)S(1)} async-done(((f32[16,1,2048]{2,1,0:T(1,128)}), f32[16,1,2048]{2,1,0:T(1,128)S(1)}, u32[]{:S(2)}, u32[]{:S(2)}) %all-to-all-start.3) | async-done | bytes 131104 | tf_op jit(solution)/shard_map/all_to_all | solution.py:159
  176.5 0.7 copy.18
  177.2 10.5 %copy-done.2 = f32[2048,4096]{1,0:T(8,128)S(1)} copy-done((f32[2048,4096]{1,0:T(8,128)S(1)}, f32[2048,4096]{1,0:T(8,128)}, u32[]{:S(2)}) %copy-start.2) | copy-done | bytes 33554456
  187.8 21.3 %logit_grad.1 = (bf16[16,128,256]{2,1,0:T(8,128)(2,1)}, f32[4,512,256]{2,1,0:T(8,128)}, f32[4,512,256]{2,1,0:T(8,128)}) custom-call(s32[1]{0:T(128)} %bitcast.me, f32[2048,4096]{1,0:T(8,128)S(1)} %copy-done.2, bf16[2048,512]{1,0:T(8,128)(2,1)} %bitcast.31, f32[1,4096]{1,0:T(1,128)} %get-tuple-element.17.b, f32[16,2048]{1,0:T(8,128)} %bitcast.34, ...), custom_call_target="tpu_custom_call" | custom-call | tf_op jit(solution)/shard_map/logit_grad/pallas_call | solution.py:143
  209.1 21.8 %all_to_all.27 = bf16[16,128,256]{2,1,0:T(8,128)(2,1)S(1)} all-to-all(bf16[16,128,256]{2,1,0:T(8,128)(2,1)} %get-tuple-element.19), channel_id=1, replica_groups=mesh['batch'=8,'proto'=16] {'proto'}, dimensions={0} | all-to-all | bytes 2097152 | tf_op jit(solution)/shard_map/all_to_all | solution.py:237
  231.4 1.6 collective-permute-start.20
  233.0 1.3 collective-permute-start.22
  234.4 1.4 collective-permute-start.21
  235.9 0.8 fusion.17
  236.7 4.1 %collective-permute-done.20 = bf16[512,256]{1,0:T(8,128)(2,1)S(1)} collective-permute-done((bf16[512,256]{1,0:T(8,128)(2,1)S(1)}, bf16[512,256]{1,0:T(8,128)(2,1)S(1)}, u32[]{:S(2)}, u32[]{:S(2)}) %collective-permute-start.20) | collective-permute-done | bytes 262176 | tf_op jit(solution)/shard_map/ppermute | solution.py:156
  240.8 6.3 %collective-permute-done.22 = bf16[512,256]{1,0:T(8,128)(2,1)S(1)} collective-permute-done((bf16[512,256]{1,0:T(8,128)(2,1)S(1)}, bf16[512,256]{1,0:T(8,128)(2,1)S(1)}, u32[]{:S(2)}, u32[]{:S(2)}) %collective-permute-start.22) | collective-permute-done | bytes 262176 | tf_op jit(solution)/shard_map/ppermute | solution.py:156
  247.3 1.0 fusion.7
  (79 shorter events, 5.0 us)
Async XLA Ops:
  5.1 8.3 %copy-start.11 = (bf16[512,256]{1,0:T(8,128)(2,1)S(1)}, bf16[512,256]{1,0:T(8,128)(2,1)}, u32[]{:S(2)}) copy-start(bf16[512,256]{1,0:T(8,128)(2,1)} %param.6) | copy-start | bytes 786436
  5.1 8.4 %copy-start.7 = (bf16[512,256]{1,0:T(8,128)(2,1)S(1)}, bf16[512,256]{1,0:T(8,128)(2,1)}, u32[]{:S(2)}) copy-start(bf16[512,256]{1,0:T(8,128)(2,1)} %param.7) | copy-start | bytes 786436
  5.1 39.9 %all-to-all-start = ((bf16[16,128,512]{2,1,0:T(8,128)(2,1)}), bf16[16,128,512]{2,1,0:T(8,128)(2,1)S(1)}, u32[]{:S(2)}, u32[]{:S(2)}) async-start(bf16[16,128,512]{2,1,0:T(8,128)(2,1)} %broadcast_in_dim.12), calls=%async_computation | async-start | bytes 4194304 | tf_op jit(solution)/shard_map/all_to_all | solution.py:159
  14.0 31.1 %copy-start.9 = (bf16[512,512]{1,0:T(8,128)(2,1)}, bf16[512,512]{1,0:T(8,128)(2,1)S(1)}, u32[]{:S(2)}) copy-start(bf16[512,512]{1,0:T(8,128)(2,1)S(1)} %pad_maximum_fusion.refs_0_) | copy-start | bytes 1572868
  14.0 25.9 %collective-permute-start.5 = (bf16[512,512]{1,0:T(8,128)(2,1)S(1)}, bf16[512,512]{1,0:T(8,128)(2,1)S(1)}, u32[]{:S(2)}, u32[]{:S(2)}) collective-permute-start(bf16[512,512]{1,0:T(8,128)(2,1)S(1)} %pad_maximum_fusion.refs_0_), channel_id=1, source_target_pairs={{0,96},{16,112},{32,64},{48,80},{64,32},{80,48},{96,0},{112,16},{1... | collective-permute-start | bytes 1572872 | tf_op jit(solution)/shard_map/ppermute | solution.py:156
  16.8 23.1 %collective-permute-start.3 = (bf16[512,512]{1,0:T(8,128)(2,1)S(1)}, bf16[512,512]{1,0:T(8,128)(2,1)}, u32[]{:S(2)}, u32[]{:S(2)}) collective-permute-start(bf16[512,512]{1,0:T(8,128)(2,1)S(1)} %pad_maximum_fusion.refs_0_), channel_id=1, source_target_pairs={{0,64},{16,80},{32,96},{48,112},{64,0},{80,16},{96,32},{112,48},{1... | collective-permute-start | bytes 1572872 | tf_op jit(solution)/shard_map/ppermute | solution.py:156
  17.6 23.0 %collective-permute-start.1 = (bf16[512,512]{1,0:T(8,128)(2,1)S(1)}, bf16[512,512]{1,0:T(8,128)(2,1)}, u32[]{:S(2)}, u32[]{:S(2)}) collective-permute-start(bf16[512,512]{1,0:T(8,128)(2,1)S(1)} %pad_maximum_fusion.refs_0_), channel_id=1, source_target_pairs={{0,32},{16,48},{32,0},{48,16},{64,96},{80,112},{96,64},{112,80},{1... | collective-permute-start | bytes 1572872 | tf_op jit(solution)/shard_map/ppermute | solution.py:156
  18.2 22.5 %collective-permute-start = (bf16[512,512]{1,0:T(8,128)(2,1)S(1)}, bf16[512,512]{1,0:T(8,128)(2,1)}, u32[]{:S(2)}, u32[]{:S(2)}) collective-permute-start(bf16[512,512]{1,0:T(8,128)(2,1)S(1)} %pad_maximum_fusion.refs_0_), channel_id=1, source_target_pairs={{0,16},{16,0},{32,48},{48,32},{64,80},{80,64},{96,112},{112,96},{1... | collective-permute-start | bytes 1572872 | tf_op jit(solution)/shard_map/ppermute | solution.py:156
  39.9 5.1 %copy-start.12 = (bf16[512,512]{1,0:T(8,128)(2,1)}, bf16[512,512]{1,0:T(8,128)(2,1)S(1)}, u32[]{:S(2)}) copy-start(bf16[512,512]{1,0:T(8,128)(2,1)S(1)} %collective-permute-done.5.refs_6_) | copy-start | bytes 1572868
  39.9 2.0 collective-permute-start.6
  39.9 3.0 %collective-permute-start.4 = (bf16[512,512]{1,0:T(8,128)(2,1)}, bf16[512,512]{1,0:T(8,128)(2,1)}, u32[]{:S(2)}, u32[]{:S(2)}) collective-permute-start(bf16[512,512]{1,0:T(8,128)(2,1)} %collective-permute-done.3.refs_4_), channel_id=1, source_target_pairs={{0,16},{16,0},{32,48},{48,32},{64,80},{80,64},{96,112},{112,96},{1... | collective-permute-start | bytes 1572872 | tf_op jit(solution)/shard_map/ppermute | solution.py:156
  40.6 3.0 %collective-permute-start.2 = (bf16[512,512]{1,0:T(8,128)(2,1)}, bf16[512,512]{1,0:T(8,128)(2,1)}, u32[]{:S(2)}, u32[]{:S(2)}) collective-permute-start(bf16[512,512]{1,0:T(8,128)(2,1)} %collective-permute-done.1.refs_2_), channel_id=1, source_target_pairs={{0,16},{16,0},{32,48},{48,32},{64,80},{80,64},{96,112},{112,96},{1... | collective-permute-start | bytes 1572872 | tf_op jit(solution)/shard_map/ppermute | solution.py:156
  45.1 1.3 copy-start.3
  56.1 11.1 %copy-start = (f32[2048,4096]{1,0:T(8,128)}, f32[2048,4096]{1,0:T(8,128)S(1)}, u32[]{:S(2)}) copy-start(f32[2048,4096]{1,0:T(8,128)S(1)} %get-tuple-element.12.e) | copy-start | bytes 100663296
  67.1 14.2 %copy-start.5 = (bf16[8,512,256]{2,1,0:T(8,128)(2,1)}, bf16[8,512,256]{2,1,0:T(8,128)(2,1)S(1)}, u32[]{:S(2)}) copy-start(bf16[8,512,256]{2,1,0:T(8,128)(2,1)S(1)} %get-tuple-element.15.protos) | copy-start | bytes 6291460
  67.1 1.4 collective-permute-start.7
  69.3 12.1 %copy-start.13 = (f32[1,4096]{1,0:T(1,128)}, f32[1,4096]{1,0:T(1,128)S(1)}, u32[]{:S(2)}) copy-start(f32[1,4096]{1,0:T(1,128)S(1)} %add.57.c0) | copy-start | bytes 49156
  69.3 12.1 %collective-permute-start.10 = (f32[1,4096]{1,0:T(1,128)S(1)}, f32[1,4096]{1,0:T(1,128)S(1)}, u32[]{:S(2)}, u32[]{:S(2)}) collective-permute-start(f32[1,4096]{1,0:T(1,128)S(1)} %add.57.c0), channel_id=1, source_target_pairs={{0,96},{16,112},{32,64},{48,80},{64,32},{80,48},{96,0},{112,16},{1... | collective-permute-start | bytes 49160 | tf_op jit(solution)/shard_map/ppermute | solution.py:156
  72.1 9.3 %collective-permute-start.9 = (f32[1,4096]{1,0:T(1,128)S(1)}, f32[1,4096]{1,0:T(1,128)S(1)}, u32[]{:S(2)}, u32[]{:S(2)}) collective-permute-start(f32[1,4096]{1,0:T(1,128)S(1)} %add.57.c0), channel_id=1, source_target_pairs={{0,64},{16,80},{32,96},{48,112},{64,0},{80,16},{96,32},{112,48},{1... | collective-permute-start | bytes 49160 | tf_op jit(solution)/shard_map/ppermute | solution.py:156
  72.9 8.5 %collective-permute-start.8 = (f32[1,4096]{1,0:T(1,128)S(1)}, f32[1,4096]{1,0:T(1,128)S(1)}, u32[]{:S(2)}, u32[]{:S(2)}) collective-permute-start(f32[1,4096]{1,0:T(1,128)S(1)} %add.57.c0), channel_id=1, source_target_pairs={{0,32},{16,48},{32,0},{48,16},{64,96},{80,112},{96,64},{112,80},{1... | collective-permute-start | bytes 49160 | tf_op jit(solution)/shard_map/ppermute | solution.py:156
  73.5 1.6 copy-start.4
  81.4 0.6 copy-start.16
  81.4 0.6 copy-start.19
  81.4 0.6 copy-start.22
  82.1 10.5 %copy-start.1 = (f32[2048,4096]{1,0:T(8,128)S(1)}, f32[2048,4096]{1,0:T(8,128)}, u32[]{:S(2)}) copy-start(f32[2048,4096]{1,0:T(8,128)} %copy-done) | copy-start | bytes 100663296
  117.3 1.4 collective-permute-start.11
  119.4 8.1 %copy-start.14 = (f32[1,4096]{1,0:T(1,128)}, f32[1,4096]{1,0:T(1,128)S(1)}, u32[]{:S(2)}) copy-start(f32[1,4096]{1,0:T(1,128)S(1)} %add.58.c0) | copy-start | bytes 49156
  119.4 5.0 %collective-permute-start.14 = (f32[1,4096]{1,0:T(1,128)S(1)}, f32[1,4096]{1,0:T(1,128)S(1)}, u32[]{:S(2)}, u32[]{:S(2)}) collective-permute-start(f32[1,4096]{1,0:T(1,128)S(1)} %add.58.c0), channel_id=1, source_target_pairs={{0,96},{16,112},{32,64},{48,80},{64,32},{80,48},{96,0},{112,16},{1... | collective-permute-start | bytes 49160 | tf_op jit(solution)/shard_map/ppermute | solution.py:156
  122.3 5.2 %collective-permute-start.13 = (f32[1,4096]{1,0:T(1,128)S(1)}, f32[1,4096]{1,0:T(1,128)S(1)}, u32[]{:S(2)}, u32[]{:S(2)}) collective-permute-start(f32[1,4096]{1,0:T(1,128)S(1)} %add.58.c0), channel_id=1, source_target_pairs={{0,64},{16,80},{32,96},{48,112},{64,0},{80,16},{96,32},{112,48},{1... | collective-permute-start | bytes 49160 | tf_op jit(solution)/shard_map/ppermute | solution.py:156
  122.3 5.2 %collective-permute-start.12 = (f32[1,4096]{1,0:T(1,128)S(1)}, f32[1,4096]{1,0:T(1,128)S(1)}, u32[]{:S(2)}, u32[]{:S(2)}) collective-permute-start(f32[1,4096]{1,0:T(1,128)S(1)} %add.58.c0), channel_id=1, source_target_pairs={{0,32},{16,48},{32,0},{48,16},{64,96},{80,112},{96,64},{112,80},{1... | collective-permute-start | bytes 49160 | tf_op jit(solution)/shard_map/ppermute | solution.py:156
  124.5 3.1 %copy-start.17 = (f32[1,4096]{1,0:T(1,128)}, f32[1,4096]{1,0:T(1,128)S(1)}, u32[]{:S(2)}) copy-start(f32[1,4096]{1,0:T(1,128)S(1)} %collective-permute-done.14.c3) | copy-start | bytes 49156
  127.5 0.6 copy-start.20
  128.1 0.6 copy-start.23
  150.0 1.4 collective-permute-start.15
  152.1 6.1 %copy-start.15 = (f32[1,4096]{1,0:T(1,128)}, f32[1,4096]{1,0:T(1,128)S(1)}, u32[]{:S(2)}) copy-start(f32[1,4096]{1,0:T(1,128)S(1)} %add.59.c0) | copy-start | bytes 49156
  152.2 5.0 %collective-permute-start.18 = (f32[1,4096]{1,0:T(1,128)S(1)}, f32[1,4096]{1,0:T(1,128)S(1)}, u32[]{:S(2)}, u32[]{:S(2)}) collective-permute-start(f32[1,4096]{1,0:T(1,128)S(1)} %add.59.c0), channel_id=1, source_target_pairs={{0,96},{16,112},{32,64},{48,80},{64,32},{80,48},{96,0},{112,16},{1... | collective-permute-start | bytes 49160 | tf_op jit(solution)/shard_map/ppermute | solution.py:156
  152.7 5.2 %collective-permute-start.17 = (f32[1,4096]{1,0:T(1,128)S(1)}, f32[1,4096]{1,0:T(1,128)S(1)}, u32[]{:S(2)}, u32[]{:S(2)}) collective-permute-start(f32[1,4096]{1,0:T(1,128)S(1)} %add.59.c0), channel_id=1, source_target_pairs={{0,64},{16,80},{32,96},{48,112},{64,0},{80,16},{96,32},{112,48},{1... | collective-permute-start | bytes 49160 | tf_op jit(solution)/shard_map/ppermute | solution.py:156
  153.8 4.4 %collective-permute-start.16 = (f32[1,4096]{1,0:T(1,128)S(1)}, f32[1,4096]{1,0:T(1,128)S(1)}, u32[]{:S(2)}, u32[]{:S(2)}) collective-permute-start(f32[1,4096]{1,0:T(1,128)S(1)} %add.59.c0), channel_id=1, source_target_pairs={{0,32},{16,48},{32,0},{48,16},{64,96},{80,112},{96,64},{112,80},{1... | collective-permute-start | bytes 49160 | tf_op jit(solution)/shard_map/ppermute | solution.py:156
  157.2 1.0 copy-start.18
  158.0 0.6 copy-start.21
  158.6 0.6 copy-start.24
  159.2 18.1 %copy-start.6 = (bf16[8,512,256]{2,1,0:T(8,128)(2,1)S(1)}, bf16[8,512,256]{2,1,0:T(8,128)(2,1)}, u32[]{:S(2)}) copy-start(bf16[8,512,256]{2,1,0:T(8,128)(2,1)} %copy-done.5) | copy-start | bytes 6291460
  165.1 11.5 %all-to-all-start.3 = ((f32[16,1,2048]{2,1,0:T(1,128)}), f32[16,1,2048]{2,1,0:T(1,128)S(1)}, u32[]{:S(2)}, u32[]{:S(2)}) async-start(f32[16,1,2048]{2,1,0:T(1,128)} %broadcast_in_dim.17), calls=%async_computation.3 | async-start | bytes 262144 | tf_op jit(solution)/shard_map/all_to_all | solution.py:159
  177.2 10.5 %copy-start.2 = (f32[2048,4096]{1,0:T(8,128)S(1)}, f32[2048,4096]{1,0:T(8,128)}, u32[]{:S(2)}) copy-start(f32[2048,4096]{1,0:T(8,128)} %copy-done) | copy-start | bytes 100663296
  209.1 21.9 %copy-start.8 = (f32[4,512,256]{2,1,0:T(8,128)S(1)}, f32[4,512,256]{2,1,0:T(8,128)}, u32[]{:S(2)}) copy-start(f32[4,512,256]{2,1,0:T(8,128)} %get-tuple-element.20) | copy-start | bytes 6291460
  209.1 21.9 %collective-permute-start.19 = (f32[4,512,256]{2,1,0:T(8,128)}, f32[4,512,256]{2,1,0:T(8,128)S(1)}, u32[]{:S(2)}, u32[]{:S(2)}) collective-permute-start(f32[4,512,256]{2,1,0:T(8,128)} %get-tuple-element.21), channel_id=1, source_target_pairs={{0,16},{16,0},{32,48},{48,32},{64,80},{80,64},{96,112},{112,96},{1... | collective-permute-start | bytes 6291464 | tf_op jit(solution)/shard_map/ppermute | solution.py:156
  231.0 4.7 %copy-start.10 = (bf16[128,256]{1,0:T(8,128)(2,1)S(1)}, bf16[128,256]{1,0:T(8,128)(2,1)}, u32[]{:S(2)}) copy-start(bf16[128,256]{1,0:T(8,128)(2,1)} %param.5) | copy-start | bytes 196612
  231.4 9.3 %collective-permute-start.20 = (bf16[512,256]{1,0:T(8,128)(2,1)S(1)}, bf16[512,256]{1,0:T(8,128)(2,1)S(1)}, u32[]{:S(2)}, u32[]{:S(2)}) collective-permute-start(bf16[512,256]{1,0:T(8,128)(2,1)S(1)} %get-tuple-element.24), channel_id=1, source_target_pairs={{0,32},{16,48},{32,0},{48,16},{64,96},{80,112},{96,64},{112,80},{1... | collective-permute-start | bytes 786440 | tf_op jit(solution)/shard_map/ppermute | solution.py:156
  233.0 14.0 %collective-permute-start.22 = (bf16[512,256]{1,0:T(8,128)(2,1)S(1)}, bf16[512,256]{1,0:T(8,128)(2,1)S(1)}, u32[]{:S(2)}, u32[]{:S(2)}) collective-permute-start(bf16[512,256]{1,0:T(8,128)(2,1)S(1)} %get-tuple-element.25), channel_id=1, source_target_pairs={{0,96},{16,112},{32,64},{48,80},{64,32},{80,48},{96,0},{112,16},{1... | collective-permute-start | bytes 786440 | tf_op jit(solution)/shard_map/ppermute | solution.py:156
  234.4 12.7 %collective-permute-start.21 = (bf16[512,256]{1,0:T(8,128)(2,1)S(1)}, bf16[512,256]{1,0:T(8,128)(2,1)S(1)}, u32[]{:S(2)}, u32[]{:S(2)}) collective-permute-start(bf16[512,256]{1,0:T(8,128)(2,1)S(1)} %get-tuple-element.26), channel_id=1, source_target_pairs={{0,64},{16,80},{32,96},{48,112},{64,0},{80,16},{96,32},{112,48},{1... | collective-permute-start | bytes 786440 | tf_op jit(solution)/shard_map/ppermute | solution.py:156

commit v2 on v1

v2 whole, which is shorter than its diff:
```python
import functools

import jax
import jax.numpy as jnp
from jax import lax
from jax.experimental import pallas as pl
from jax.experimental.pallas import tpu as pltpu
from jax.sharding import PartitionSpec as P

ITERS = 3
LOG2E = 1.4426950408889634
teacher_temp = 0.07
student_temp = 0.1
epsilon = 1e-06

F32 = jnp.float32
BF16 = jnp.bfloat16
MIB = 2**20
VM = pl.BlockSpec(memory_space=pltpu.VMEM)
SM = pl.BlockSpec(memory_space=pltpu.SMEM)
NT = (((1,), (1,)), ((), ()))
NN = (((1,), (0,)), ((), ()))


def project_back(grad, unit_rows, scale):
    return (grad - unit_rows * jnp.sum(unit_rows * grad, -1, keepdims=True)) * scale


def fold(x):
    return x.reshape(-1, 8, x.shape[1]).sum(0)


def spread(row, out):
    for k in range(row.shape[1] // 128):
        part = row[:, k * 128 : (k + 1) * 128]
        out[k * 128 : (k + 1) * 128, :] = jnp.broadcast_to(part, (128, 128)).T


def gather_lanes(part, out):
    for k in range(part.shape[0] // 128):
        out[0:1, k * 128 : (k + 1) * 128] = part[k * 128 : (k + 1) * 128, :].T.sum(0, keepdims=True)


def unit_kernel(tf, sf, tp, sp, feats, protos, fscale, pscale):
    dim = tf.shape[1]
    for k, (x, y) in enumerate(((tf, tp), (sf, sp))):
        half = slice(k * dim, (k + 1) * dim)
        wide = x[...].astype(F32)
        scale = lax.rsqrt(jnp.sum(wide * wide, -1, keepdims=True) + epsilon)
        unit = (wide * scale).astype(BF16)
        for i in range(feats.shape[0]):
            feats[i, :, half] = unit
        if k:
            fscale[...] = scale
        wide = y[...].astype(F32)
        scale = lax.rsqrt(jnp.sum(wide * wide, -1, keepdims=True) + epsilon)
        protos[:, half] = (wide * scale).astype(BF16)
        if k:
            pscale[...] = scale


def exp_kernel(dim, me, feats, *refs):
    pieces, (e, c, protos) = refs[:-3], refs[-3:]
    own = pieces[0].shape[0]
    for r, piece in enumerate(pieces):
        protos[r] = piece[:, :dim]

    @pl.loop(0, len(pieces))
    def _(r):
        s = lax.dot_general(feats[:, :dim], protos[r], NT, preferred_element_type=F32)
        x = jnp.exp2(s * (LOG2E / teacher_temp))
        e[:, pl.ds(pl.multiple_of(r * own, own), own)] = x
        c[:, pl.ds(pl.multiple_of((me[0] ^ r) * own, own), own)] = fold(x).sum(0, keepdims=True)


def total_kernel(dim, feats, *refs):
    pieces, (z, protos, part) = refs[:-3], refs[-3:]
    own = pieces[0].shape[0]
    for r, piece in enumerate(pieces):
        protos[r] = piece[:, dim:]
    part[...] = jnp.zeros_like(part)

    @pl.loop(0, len(pieces))
    def _(r):
        s = lax.dot_general(feats[:, dim:], protos[r], NT, preferred_element_type=F32)
        x = jnp.exp2(s * (LOG2E / student_temp))
        acc = x[:, :128]
        for k in range(1, own // 128):
            acc += x[:, k * 128 : (k + 1) * 128]
        part[...] += acc

    gather_lanes(part, z)


def row_kernel(block, own, me, e, c0, c1, c2, c3, *refs):
    z, (r, b, part) = refs[:-3], refs[-3:]
    rows, cols = e.shape
    for k in range(cols // own):
        src = pl.ds(pl.multiple_of((me[0] ^ k) * own, own), own)
        b[:, k * own : (k + 1) * own] = 1.0 / (c0[:, src] + c1[:, src] + c2[:, src] + c3[:, src])

    @pl.loop(0, rows // block)
    def _(i):
        ii = pl.ds(pl.multiple_of(i * block, block), block)
        acc = jnp.zeros((block, 128), F32)
        for k in range(cols // 128):
            lanes = slice(k * 128, (k + 1) * 128)
            acc += e[ii, lanes] * b[:, lanes]
        part[ii, :] = acc

    gather_lanes(part, r.at[0])
    for k in range(len(z)):
        r[0, k + 1 : k + 2, :] = z[k][...]
    for k in range(1, r.shape[0]):
        r[k] = r[0]


def col_kernel(block, width, own, me, e, sums, c, av):
    rows, cols = e.shape
    spread(1.0 / jnp.sum(sums[:, 0, :], 0, keepdims=True), av)
    for j in range(cols // width):

        def step(i, acc, j=j):
            ii = pl.ds(pl.multiple_of(i * block, block), block)
            w = av[ii, :]
            return tuple(
                acc[k] + fold(e[ii, j * width + k * 128 : j * width + (k + 1) * 128] * w)
                for k in range(width // 128)
            )

        zero = jnp.zeros((8, 128), F32)
        acc = lax.fori_loop(0, rows // block, step, (zero,) * (width // 128))
        for k in range(width // own):
            part = jnp.concatenate(acc[k * own // 128 : (k + 1) * own // 128], 1)
            to = (me[0] ^ (j * width // own + k)) * own
            c[:, pl.ds(pl.multiple_of(to, own), own)] = part.sum(0, keepdims=True)


def grad_kernel(dim, me, e, feats, b, protos, sums, zsums, f, keep, give, av, zv, g0, g1, acc, turned):
    own = protos.shape[1]
    spread((1.0 / student_temp) / jnp.sum(sums[:, 0, :], 0, keepdims=True), av)
    spread((1.0 / student_temp) / jnp.sum(zsums[:, 1, :], 0, keepdims=True), zv)
    acc[...] = jnp.zeros_like(acc)
    turned[...] = feats[:, dim:].T
    wide = lambda m: jnp.concatenate([m] * (own // 128), 1)

    @pl.loop(0, protos.shape[0] // 2)
    def _(h):
        for k, (g, out) in enumerate(((g0, keep), (g1, give))):
            cols = pl.ds(pl.multiple_of((2 * h + k) * own, own), own)
            sp = protos[2 * h + k]
            s = lax.dot_general(feats[:, dim:], sp, NT, preferred_element_type=F32)
            p = jnp.exp2(s * (LOG2E / student_temp))
            g[...] = (p * wide(zv[...]) - wide(av[...]) * (e[:, cols] * b[:, cols])).astype(BF16)
            new = lax.dot_general(turned[...], g[...], NN, preferred_element_type=F32)
            out[h] = new.T.astype(out.dtype)
            acc[...] += lax.dot_general(g[...], sp, NN, preferred_element_type=F32)

    f[...] = acc[...].astype(BF16).reshape(f.shape)


def call(kernel, name, out_shape, ops, scratch=(), limit=26, smem=0, keep=()):
    many = isinstance(out_shape, (list, tuple))
    ops = list(ops[:smem]) + [
        pltpu.with_memory_space_constraint(x, pltpu.VMEM if i in keep else pltpu.HBM)
        for i, x in enumerate(ops[smem:])
    ]
    return pl.pallas_call(
        kernel,
        out_shape=out_shape,
        in_specs=[SM] * smem + [VM] * (len(ops) - smem),
        out_specs=[VM] * len(out_shape) if many else VM,
        scratch_shapes=list(scratch),
        compiler_params=pltpu.CompilerParams(vmem_limit_bytes=limit * MIB),
        name=name,
    )(*ops)


def shards(nb, npr, teacher_feats, student_feats, teacher_protos, student_protos):
    swap = lambda x, k: lax.ppermute(x, "batch", [(i, i ^ k) for i in range(nb)])

    dim = teacher_feats.shape[1]
    own_rows, own = student_feats.shape[0], student_protos.shape[0]
    rows, cols = own_rows * npr, own * nb
    me = lax.axis_index("batch").astype(jnp.int32).reshape(1)
    hbm, vmem = pltpu.HBM, pltpu.VMEM

    feats, unit, fscale, pscale = call(
        unit_kernel,
        "unit_rows",
        [
            hbm((npr, own_rows, 2 * dim), BF16),
            hbm((own, 2 * dim), BF16),
            hbm((own_rows, 1), F32),
            hbm((own, 1), F32),
        ],
        [teacher_feats, student_feats, teacher_protos, student_protos],
    )
    pieces = [unit] + [None] * (nb - 1)
    for r in range(2, nb, 2):
        pieces[r] = swap(unit, r)
    feats = lax.all_to_all(feats, "proto", 0, 0).reshape(rows, 2 * dim)
    for r in range(0, nb, 2):
        pieces[r + 1] = swap(pieces[r], 1)

    lanes = vmem((rows, 128), F32)
    all_cols = vmem((1, cols), F32)
    e, c = call(
        functools.partial(exp_kernel, dim),
        "teacher_exp",
        [vmem((rows, cols), F32), all_cols],
        [me, feats, *pieces],
        [vmem((nb, own, dim), BF16)],
        smem=1,
    )
    for iteration in range(ITERS):
        if iteration:
            c = call(
                functools.partial(col_kernel, 128, 2048, own),
                "column_sums",
                all_cols,
                [me, e, sums],
                [lanes],
                smem=1,
                keep=(0,),
            )
        c = c + swap(c, 1)
        cs = [c] + [swap(c, k) for k in range(2, nb, 2)]
        extra = [z] if iteration == 1 else []
        r, b = call(
            functools.partial(row_kernel, 128, own),
            "row_sums",
            [hbm((npr, 1 + len(extra), rows), F32), all_cols],
            [me, e, *cs, *extra],
            [lanes],
            smem=1,
            keep=(0, 1, 2, 3, 4),
        )
        if iteration == 0:
            r, feats_z = lax.optimization_barrier((r, feats))
            z, protos = call(
                functools.partial(total_kernel, dim),
                "student_total",
                [hbm((1, rows), F32), hbm((nb, own, dim), BF16)],
                [feats_z, *pieces],
                [lanes],
            )
        sums = lax.all_to_all(r, "proto", 0, 0)
        if extra:
            zsums = sums
    half_g = vmem((rows, own), BF16)
    f, keep, give = call(
        functools.partial(grad_kernel, dim),
        "logit_grad",
        [
            hbm((npr, own_rows, dim), BF16),
            hbm((nb // 2, own, dim), F32),
            hbm((nb // 2, own, dim), BF16),
        ],
        [me, e, feats, b, protos, sums, zsums],
        [lanes, lanes, half_g, half_g, vmem((rows, dim), F32), vmem((dim, rows), BF16)],
        smem=1,
        keep=(0, 2),
    )
    half = keep + swap(give, 1).astype(F32)
    sent = [swap(half[k].astype(BF16), 2 * k) for k in range(1, nb // 2)]
    f, *sent = lax.optimization_barrier((lax.all_to_all(f, "proto", 0, 0), *sent))
    feature_part = jnp.sum(f.astype(F32), 0)
    proto_part = half[0] + sum(x.astype(F32) for x in sent)
    student_unit = student_feats.astype(F32) * fscale
    sproto_unit = student_protos.astype(F32) * pscale
    feature_grad = project_back(feature_part, student_unit, fscale)
    proto_grad = project_back(proto_part, sproto_unit, pscale)
    return (feature_grad, proto_grad)


def solution(mesh):
    nb, npr = mesh.shape["batch"], mesh.shape["proto"]
    in_specs = (
        P(("batch", "proto"), None),
        P(("batch", "proto"), None),
        P(("proto", "batch"), None),
        P(("proto", "batch"), None),
    )
    out_specs = (P(("batch", "proto"), None), P(("proto", "batch"), None))
    return jax.shard_map(
        functools.partial(shards, nb, npr),
        mesh=mesh,
        in_specs=in_specs,
        out_specs=out_specs,
        check_vma=False,
    )
```

time: 250 us -> 194 us (0.78)
  local copies, waits for them, and re-layouts: 44.7 us -> 3.28 us
  blocking collectives: 46.7 us -> 38.1 us
  waiting for transfers between devices: 53.9 us -> 47.4 us
    unnamed x54 -> x14, local copies, waits for them, and re-layouts: 40.6 us -> 2.37 us
    ppermute x23, waiting for transfers between devices: 45.3 us -> 34.9 us  [shards(): lax.ppermute(x, 'batch', [(i, i ^ k) for i in range(nb)])]
    all_to_all x3, blocking collectives: 46.7 us -> 38.1 us  [shards(): sums = lax.all_to_all(r, 'proto', 0, 0)]
    all_to_all x2, waiting for transfers between devices: 8.63 us -> 12.5 us  [the longest x1 10.5 us: shards(): lax.all_to_all(f, 'proto', 0, 0)]
    broadcast_in_dim x4 -> x0, local copies, waits for them, and re-layouts: 3.84 us -> none  [over_proto(): jnp.broadcast_to(x[None], (npr,) + x.shape)]
    pallas_call x8 -> x9, Pallas kernels: 59.7 us -> 61.4 us  [call(): pl.pallas_call(kernel, out_shape=out_shape, in_specs=[SM] * smem + [VM] *...]
  transfers between devices with their start and end apart: 25 -> 25, of which waited for: 17 -> 15; matrix products, arithmetic and copies ran while one was open for 1% -> 2% of each run, Pallas kernels for 3% -> 5%
where the time goes in v2:
time: 194 us; the launch traced here: 193 us
  Pallas kernels  61.4 us (32%)
  waiting for transfers between devices  47.4 us (24%)
  blocking collectives  38.1 us (20%)
  starting transfers between devices  33.5 us (17%)
  other arithmetic  8.02 us (4%)
  local copies, waits for them, and re-layouts  3.28 us (2%)
    pallas_call x9, Pallas kernels, call(): pl.pallas_call(kernel, out_shape=out_shape, in_specs=[SM] * smem + [VM] *...  61.4 us
    all_to_all x3, blocking collectives, shards(): sums = lax.all_to_all(r, 'proto', 0, 0)  38.1 us
    ppermute x23, waiting for transfers between devices, shards(): lax.ppermute(x, 'batch', [(i, i ^ k) for i in range(nb)])  34.9 us
    ppermute x23, starting transfers between devices, shards(): lax.ppermute(x, 'batch', [(i, i ^ k) for i in range(nb)])  21.6 us
    all_to_all x1, waiting for transfers between devices, shards(): lax.all_to_all(f, 'proto', 0, 0)  10.5 us
    all_to_all x1, starting transfers between devices, shards(): feats = lax.all_to_all(feats, 'proto', 0, 0).reshape(rows, 2 * dim)  8.26 us
  transfers between devices with their start and end apart: 25, of which 15 were waited for; matrix products, arithmetic and copies ran while one was open for 2% of the time, Pallas kernels for 5%

profile of v2, /device:TPU:0, one launch (start us, length us, event | category | flops | bytes accessed | tf_op | source)
XLA Modules:
  0.0 192.5 jit_solution(13192563597881700687)
XLA Ops:
  0.6 3.1 %unit_rows.1 = (bf16[16,128,512]{2,1,0:T(8,128)(2,1)}, bf16[512,512]{1,0:T(8,128)(2,1)}, f32[128,1]{1,0:T(8,128)}, f32[512,1]{1,0:T(8,128)}) custom-call(bf16[128,256]{1,0:T(8,128)(2,1)} %tf.1, bf16[128,256]{1,0:T(8,128)(2,1)} %sf.1, bf16[512,256]{1,0:T(8,128)(2,1)} %tp.1, bf16[512,256]{1,0:T(8,128)(2,1)} %sp.1), custom_call_target="tpu_custom_call" | custom-call | tf_op jit(solution)/shard_map/unit_rows/pallas_call | solution.py:168
  3.7 8.3 %all-to-all-start = ((bf16[16,128,512]{2,1,0:T(8,128)(2,1)}), bf16[16,128,512]{2,1,0:T(8,128)(2,1)S(1)}, u32[]{:S(2)}, u32[]{:S(2)}) async-start(bf16[16,128,512]{2,1,0:T(8,128)(2,1)} %get-tuple-element.23), calls=%async_computation | async-start | bytes 4194304 | tf_op jit(solution)/shard_map/all_to_all | solution.py:202
  12.0 2.8 %collective-permute-start.5 = (bf16[512,512]{1,0:T(8,128)(2,1)S(1)}, bf16[512,512]{1,0:T(8,128)(2,1)S(1)}, u32[]{:S(2)}, u32[]{:S(2)}) collective-permute-start(bf16[512,512]{1,0:T(8,128)(2,1)S(1)} %copy-done.2), channel_id=1, source_target_pairs={{0,96},{16,112},{32,64},{48,80},{64,32},{80,48},{96,0},{112,16},{1... | collective-permute-start | bytes 1572872 | tf_op jit(solution)/shard_map/ppermute | solution.py:180
  14.8 0.8 collective-permute-start.3
  15.6 0.5 collective-permute-start.1
  16.1 0.0 collective-permute-start
  16.2 21.7 %collective-permute-done.5.refs_6_ = bf16[512,512]{1,0:T(8,128)(2,1)S(1)} collective-permute-done((bf16[512,512]{1,0:T(8,128)(2,1)S(1)}, bf16[512,512]{1,0:T(8,128)(2,1)S(1)}, u32[]{:S(2)}, u32[]{:S(2)}) %collective-permute-start.5) | collective-permute-done | bytes 524320 | tf_op jit(solution)/shard_map/ppermute | solution.py:180
  37.9 0.0 collective-permute-start.6
  37.9 0.5 collective-permute-start.4
  38.4 0.2 collective-permute-done.1.refs_2_
  38.6 1.3 collective-permute-done.6.refs_7_
  39.9 1.0 collective-permute-done.4.refs_5_
  40.9 0.7 collective-permute-done.2.refs_3_
  41.6 2.0 %all-to-all-done = bf16[16,128,512]{2,1,0:T(8,128)(2,1)S(1)} async-done(((bf16[16,128,512]{2,1,0:T(8,128)(2,1)}), bf16[16,128,512]{2,1,0:T(8,128)(2,1)S(1)}, u32[]{:S(2)}, u32[]{:S(2)}) %all-to-all-start) | async-done | bytes 2097184 | tf_op jit(solution)/shard_map/all_to_all | solution.py:202
  43.6 1.3 copy-done
  45.0 8.9 %teacher_exp.1 = (f32[2048,4096]{1,0:T(8,128)S(1)}, f32[1,4096]{1,0:T(1,128)S(1)}) custom-call(s32[1]{0:T(128)} %bitcast.me, bf16[2048,512]{1,0:T(8,128)(2,1)} %bitcast.16, bf16[512,512]{1,0:T(8,128)(2,1)} %get-tuple-element.24.refs_0_, bf16[512,512]{1,0:T(8,128)(2,1)} %collective-permute-done.refs_1_, bf16[512,512]{1,0:T(8,128)(2,1)} %collective-permute-done.1.refs_2_, ...), custom_call_target="tpu_custom_call" | custom-call | tf_op jit(solution)/shard_map/teacher_exp/pallas_call | solution.py:168
  53.9 0.1 collective-permute-start.7
  54.0 1.2 collective-permute-done.7
  55.2 2.8 %collective-permute-start.10 = (f32[1,4096]{1,0:T(1,128)S(1)}, f32[1,4096]{1,0:T(1,128)S(1)}, u32[]{:S(2)}, u32[]{:S(2)}) collective-permute-start(f32[1,4096]{1,0:T(1,128)S(1)} %add.21.c0), channel_id=1, source_target_pairs={{0,96},{16,112},{32,64},{48,80},{64,32},{80,48},{96,0},{112,16},{1... | collective-permute-start | bytes 49160 | tf_op jit(solution)/shard_map/ppermute | solution.py:180
  58.0 0.8 collective-permute-start.9
  58.8 0.5 collective-permute-start.8
  59.4 0.9 collective-permute-done.10.c3
  60.2 3.1 %collective-permute-done.9.c2 = f32[1,4096]{1,0:T(1,128)S(1)} collective-permute-done((f32[1,4096]{1,0:T(1,128)S(1)}, f32[1,4096]{1,0:T(1,128)S(1)}, u32[]{:S(2)}, u32[]{:S(2)}) %collective-permute-start.9) | collective-permute-done | bytes 16416 | tf_op jit(solution)/shard_map/ppermute | solution.py:180
  63.3 3.6 %row_sums.3 = (f32[16,1,2048]{2,1,0:T(1,128)}, f32[1,4096]{1,0:T(1,128)}) custom-call(s32[1]{0:T(128)} %bitcast.me, f32[2048,4096]{1,0:T(8,128)S(1)} %get-tuple-element.25.e, f32[1,4096]{1,0:T(1,128)S(1)} %add.21.c0, f32[1,4096]{1,0:T(1,128)S(1)} %collective-permute-done.8.c1, f32[1,4096]{1,0:T(1,128)S(1)} %collective-permute-done.9.c2, ...), custom_call_target="tpu_custom_call" | custom-call | tf_op jit(solution)/shard_map/row_sums/pallas_call | solution.py:168
  66.9 13.1 %all_to_all.25.sums = f32[16,1,2048]{2,1,0:T(1,128)} all-to-all(f32[16,1,2048]{2,1,0:T(1,128)} %get-tuple-element.28), channel_id=1, replica_groups=mesh['batch'=8,'proto'=16] {'proto'}, dimensions={0} | all-to-all | bytes 262144 | tf_op jit(solution)/shard_map/all_to_all | solution.py:248
  80.0 4.0 %column_sums.2 = f32[1,4096]{1,0:T(1,128)S(1)} custom-call(s32[1]{0:T(128)} %bitcast.me, f32[2048,4096]{1,0:T(8,128)S(1)} %get-tuple-element.25.e, f32[16,1,2048]{2,1,0:T(1,128)} %all_to_all.25.sums), custom_call_target="tpu_custom_call" | custom-call | tf_op jit(solution)/shard_map/column_sums/pallas_call | solution.py:168
  84.0 0.1 collective-permute-start.11
  84.1 1.2 collective-permute-done.11
  85.3 0.8 collective-permute-start.14
  86.1 1.4 collective-permute-start.13
  87.5 2.0 %collective-permute-start.12 = (f32[1,4096]{1,0:T(1,128)S(1)}, f32[1,4096]{1,0:T(1,128)S(1)}, u32[]{:S(2)}, u32[]{:S(2)}) collective-permute-start(f32[1,4096]{1,0:T(1,128)S(1)} %add.22.c0), channel_id=1, source_target_pairs={{0,32},{16,48},{32,0},{48,16},{64,96},{80,112},{96,64},{112,80},{1... | collective-permute-start | bytes 49160 | tf_op jit(solution)/shard_map/ppermute | solution.py:180
  89.4 9.9 %student_total.1 = (f32[1,2048]{1,0:T(1,128)}, bf16[8,512,256]{2,1,0:T(8,128)(2,1)}) custom-call(bf16[2048,512]{1,0:T(8,128)(2,1)} %bitcast.17, bf16[512,512]{1,0:T(8,128)(2,1)} %get-tuple-element.24.refs_0_, bf16[512,512]{1,0:T(8,128)(2,1)} %collective-permute-done.refs_1_, bf16[512,512]{1,0:T(8,128)(2,1)} %collective-permute-done.1.refs_2_, ...), custom_call_target="tpu_custom_call" | custom-call | tf_op jit(solution)/shard_map/student_total/pallas_call | solution.py:168
  99.3 4.4 %row_sums.4 = (f32[16,2,2048]{2,1,0:T(2,128)}, f32[1,4096]{1,0:T(1,128)}) custom-call(s32[1]{0:T(128)} %bitcast.me, f32[2048,4096]{1,0:T(8,128)S(1)} %get-tuple-element.25.e, f32[1,4096]{1,0:T(1,128)S(1)} %add.22.c0, f32[1,4096]{1,0:T(1,128)S(1)} %collective-permute-done.12.c1, f32[1,4096]{1,0:T(1,128)S(1)} %collective-permute-done.13.c2, ...), custom_call_target="tpu_custom_call" | custom-call | tf_op jit(solution)/shard_map/row_sums/pallas_call | solution.py:168
  103.7 12.9 %all_to_all.26.sums.zsums = f32[16,2,2048]{2,1,0:T(2,128)} all-to-all(f32[16,2,2048]{2,1,0:T(2,128)} %get-tuple-element.31), channel_id=1, replica_groups=mesh['batch'=8,'proto'=16] {'proto'}, dimensions={0} | all-to-all | bytes 524288 | tf_op jit(solution)/shard_map/all_to_all | solution.py:248
  116.6 4.0 %column_sums.3 = f32[1,4096]{1,0:T(1,128)S(1)} custom-call(s32[1]{0:T(128)} %bitcast.me, f32[2048,4096]{1,0:T(8,128)S(1)} %get-tuple-element.25.e, f32[16,2,2048]{2,1,0:T(2,128)} %all_to_all.26.sums.zsums), custom_call_target="tpu_custom_call" | custom-call | tf_op jit(solution)/shard_map/column_sums/pallas_call | solution.py:168
  120.7 0.1 collective-permute-start.15
  120.7 1.2 collective-permute-done.15
  121.9 0.8 collective-permute-start.18
  122.8 1.4 collective-permute-start.17
  124.2 1.9 %collective-permute-start.16 = (f32[1,4096]{1,0:T(1,128)S(1)}, f32[1,4096]{1,0:T(1,128)S(1)}, u32[]{:S(2)}, u32[]{:S(2)}) collective-permute-start(f32[1,4096]{1,0:T(1,128)S(1)} %add.23.c0), channel_id=1, source_target_pairs={{0,32},{16,48},{32,0},{48,16},{64,96},{80,112},{96,64},{112,80},{1... | collective-permute-start | bytes 49160 | tf_op jit(solution)/shard_map/ppermute | solution.py:180
  126.1 1.0 collective-permute-done.18.c3
  127.1 0.9 collective-permute-done.17.c2
  128.0 3.6 %row_sums.5 = (f32[16,1,2048]{2,1,0:T(1,128)}, f32[1,4096]{1,0:T(1,128)S(1)}) custom-call(s32[1]{0:T(128)} %bitcast.me, f32[2048,4096]{1,0:T(8,128)S(1)} %get-tuple-element.25.e, f32[1,4096]{1,0:T(1,128)S(1)} %add.23.c0, f32[1,4096]{1,0:T(1,128)S(1)} %collective-permute-done.16.c1, f32[1,4096]{1,0:T(1,128)S(1)} %collective-permute-done.17.c2, ...), custom_call_target="tpu_custom_call" | custom-call | tf_op jit(solution)/shard_map/row_sums/pallas_call | solution.py:168
  131.6 12.2 %all_to_all.27.sums = f32[16,1,2048]{2,1,0:T(1,128)} all-to-all(f32[16,1,2048]{2,1,0:T(1,128)} %get-tuple-element.34), channel_id=1, replica_groups=mesh['batch'=8,'proto'=16] {'proto'}, dimensions={0} | all-to-all | bytes 262144 | tf_op jit(solution)/shard_map/all_to_all | solution.py:248
  143.8 19.8 %logit_grad.1 = (bf16[16,128,256]{2,1,0:T(8,128)(2,1)}, f32[4,512,256]{2,1,0:T(8,128)}, bf16[4,512,256]{2,1,0:T(8,128)(2,1)}) custom-call(s32[1]{0:T(128)} %bitcast.me, f32[2048,4096]{1,0:T(8,128)S(1)} %get-tuple-element.25.e, bf16[2048,512]{1,0:T(8,128)(2,1)} %bitcast.18, f32[1,4096]{1,0:T(1,128)S(1)} %get-tuple-element.32.b, ...), custom_call_target="tpu_custom_call" | custom-call | tf_op jit(solution)/shard_map/logit_grad/pallas_call | solution.py:168
  163.6 3.7 %all-to-all-start.4 = ((bf16[16,128,256]{2,1,0:T(8,128)(2,1)}), bf16[16,128,256]{2,1,0:T(8,128)(2,1)S(1)}, u32[]{:S(2)}, u32[]{:S(2)}) async-start(bf16[16,128,256]{2,1,0:T(8,128)(2,1)} %get-tuple-element.35), calls=%async_computation.4 | async-start | bytes 2097152 | tf_op jit(solution)/shard_map/all_to_all | solution.py:267
  167.3 1.0 copy-done.4
  168.3 2.2 %fusion.1 = (bf16[4,512,256]{2,1,0:T(8,128)(2,1)S(1)}, f32[4,512,256]{2,1,0:T(8,128)S(1)}) fusion(f32[4,512,256]{2,1,0:T(8,128)} %get-tuple-element.36, bf16[4,512,256]{2,1,0:T(8,128)(2,1)} %copy-done.4), kind=kLoop, calls=%fused_computation.13 | loop fusion | flops 1572864 | bytes 6291456 | tf_op jit(solution)/shard_map/convert.2
  170.5 0.0 copy-start.5
  170.5 0.0 copy-start.1
  170.5 0.9 slice_bitcast_fusion.1
  171.4 2.5 %collective-permute-start.22 = (bf16[512,256]{1,0:T(8,128)(2,1)}, bf16[512,256]{1,0:T(8,128)(2,1)}, u32[]{:S(2)}, u32[]{:S(2)}) collective-permute-start(bf16[512,256]{1,0:T(8,128)(2,1)} %get-tuple-element.46), channel_id=1, source_target_pairs={{0,96},{16,112},{32,64},{48,80},{64,32},{80,48},{96,0},{112,16},{1... | collective-permute-start | bytes 786440 | tf_op jit(solution)/shard_map/ppermute | solution.py:180
  173.9 1.4 collective-permute-start.21
  175.3 0.2 collective-permute-start.20
  175.5 0.1 reduce
  175.6 1.1 reduce.1
  176.7 10.5 %all-to-all-done.4 = bf16[16,128,256]{2,1,0:T(8,128)(2,1)S(1)} async-done(((bf16[16,128,256]{2,1,0:T(8,128)(2,1)}), bf16[16,128,256]{2,1,0:T(8,128)(2,1)S(1)}, u32[]{:S(2)}, u32[]{:S(2)}) %all-to-all-start.4) | async-done | bytes 1048608 | tf_op jit(solution)/shard_map/all_to_all | solution.py:267
  187.3 0.0 collective-permute-done.22
  187.3 0.6 collective-permute-done.20
  187.9 0.1 convert_reduce_fusion
  188.1 0.2 multiply_reduce_fusion.1
  188.2 0.8 subtract_multiply_fusion.1
  189.0 1.4 multiply_reduce_fusion
  190.4 2.1 %subtract_multiply_fusion = f32[512,256]{1,0:T(8,128)} fusion(bf16[512,256]{1,0:T(8,128)(2,1)S(1)} %copy-done.1, f32[512]{0:T(512)S(1)} %multiply_reduce_fusion, f32[512]{0:T(512)S(1)} %reduce.1, bf16[512,256]{1,0:T(8,128)(2,1)} %collective-permute-done.22, bf16[512,256]{1,0:T(8,128)(2,1)} %collective-permute-done.21, ...), kind=kLoop, calls=%fused_computation.4 | loop fusion | flops 1441792 | bytes 2101248 | tf_op jit(solution)/shard_map/mul | solution.py:26
  (24 shorter events, 0.1 us)
Async XLA Ops:
  3.7 8.3 %copy-start.2 = (bf16[512,512]{1,0:T(8,128)(2,1)S(1)}, bf16[512,512]{1,0:T(8,128)(2,1)}, u32[]{:S(2)}) copy-start(bf16[512,512]{1,0:T(8,128)(2,1)} %get-tuple-element.24.refs_0_) | copy-start | bytes 1572868
  3.7 39.9 %all-to-all-start = ((bf16[16,128,512]{2,1,0:T(8,128)(2,1)}), bf16[16,128,512]{2,1,0:T(8,128)(2,1)S(1)}, u32[]{:S(2)}, u32[]{:S(2)}) async-start(bf16[16,128,512]{2,1,0:T(8,128)(2,1)} %get-tuple-element.23), calls=%async_computation | async-start | bytes 4194304 | tf_op jit(solution)/shard_map/all_to_all | solution.py:202
  12.0 25.9 %collective-permute-start.5 = (bf16[512,512]{1,0:T(8,128)(2,1)S(1)}, bf16[512,512]{1,0:T(8,128)(2,1)S(1)}, u32[]{:S(2)}, u32[]{:S(2)}) collective-permute-start(bf16[512,512]{1,0:T(8,128)(2,1)S(1)} %copy-done.2), channel_id=1, source_target_pairs={{0,96},{16,112},{32,64},{48,80},{64,32},{80,48},{96,0},{112,16},{1... | collective-permute-start | bytes 1572872 | tf_op jit(solution)/shard_map/ppermute | solution.py:180
  14.8 23.1 %collective-permute-start.3 = (bf16[512,512]{1,0:T(8,128)(2,1)S(1)}, bf16[512,512]{1,0:T(8,128)(2,1)}, u32[]{:S(2)}, u32[]{:S(2)}) collective-permute-start(bf16[512,512]{1,0:T(8,128)(2,1)S(1)} %copy-done.2), channel_id=1, source_target_pairs={{0,64},{16,80},{32,96},{48,112},{64,0},{80,16},{96,32},{112,48},{1... | collective-permute-start | bytes 1572872 | tf_op jit(solution)/shard_map/ppermute | solution.py:180
  15.6 23.0 %collective-permute-start.1 = (bf16[512,512]{1,0:T(8,128)(2,1)S(1)}, bf16[512,512]{1,0:T(8,128)(2,1)}, u32[]{:S(2)}, u32[]{:S(2)}) collective-permute-start(bf16[512,512]{1,0:T(8,128)(2,1)S(1)} %copy-done.2), channel_id=1, source_target_pairs={{0,32},{16,48},{32,0},{48,16},{64,96},{80,112},{96,64},{112,80},{1... | collective-permute-start | bytes 1572872 | tf_op jit(solution)/shard_map/ppermute | solution.py:180
  16.1 22.5 %collective-permute-start = (bf16[512,512]{1,0:T(8,128)(2,1)S(1)}, bf16[512,512]{1,0:T(8,128)(2,1)}, u32[]{:S(2)}, u32[]{:S(2)}) collective-permute-start(bf16[512,512]{1,0:T(8,128)(2,1)S(1)} %copy-done.2), channel_id=1, source_target_pairs={{0,16},{16,0},{32,48},{48,32},{64,80},{80,64},{96,112},{112,96},{1... | collective-permute-start | bytes 1572872 | tf_op jit(solution)/shard_map/ppermute | solution.py:180
  37.9 5.7 %copy-start.3 = (bf16[512,512]{1,0:T(8,128)(2,1)}, bf16[512,512]{1,0:T(8,128)(2,1)S(1)}, u32[]{:S(2)}) copy-start(bf16[512,512]{1,0:T(8,128)(2,1)S(1)} %collective-permute-done.5.refs_6_) | copy-start | bytes 1572868
  37.9 2.0 %collective-permute-start.6 = (bf16[512,512]{1,0:T(8,128)(2,1)S(1)}, bf16[512,512]{1,0:T(8,128)(2,1)}, u32[]{:S(2)}, u32[]{:S(2)}) collective-permute-start(bf16[512,512]{1,0:T(8,128)(2,1)S(1)} %collective-permute-done.5.refs_6_), channel_id=1, source_target_pairs={{0,16},{16,0},{32,48},{48,32},{64,80},{80,64},{96,112},{112,96},{1... | collective-permute-start | bytes 1572872 | tf_op jit(solution)/shard_map/ppermute | solution.py:180
  37.9 3.0 %collective-permute-start.4 = (bf16[512,512]{1,0:T(8,128)(2,1)}, bf16[512,512]{1,0:T(8,128)(2,1)}, u32[]{:S(2)}, u32[]{:S(2)}) collective-permute-start(bf16[512,512]{1,0:T(8,128)(2,1)} %collective-permute-done.3.refs_4_), channel_id=1, source_target_pairs={{0,16},{16,0},{32,48},{48,32},{64,80},{80,64},{96,112},{112,96},{1... | collective-permute-start | bytes 1572872 | tf_op jit(solution)/shard_map/ppermute | solution.py:180
  38.6 3.0 %collective-permute-start.2 = (bf16[512,512]{1,0:T(8,128)(2,1)}, bf16[512,512]{1,0:T(8,128)(2,1)}, u32[]{:S(2)}, u32[]{:S(2)}) collective-permute-start(bf16[512,512]{1,0:T(8,128)(2,1)} %collective-permute-done.1.refs_2_), channel_id=1, source_target_pairs={{0,16},{16,0},{32,48},{48,32},{64,80},{80,64},{96,112},{112,96},{1... | collective-permute-start | bytes 1572872 | tf_op jit(solution)/shard_map/ppermute | solution.py:180
  43.6 1.3 copy-start
  53.9 1.3 collective-permute-start.7
  55.2 5.0 %collective-permute-start.10 = (f32[1,4096]{1,0:T(1,128)S(1)}, f32[1,4096]{1,0:T(1,128)S(1)}, u32[]{:S(2)}, u32[]{:S(2)}) collective-permute-start(f32[1,4096]{1,0:T(1,128)S(1)} %add.21.c0), channel_id=1, source_target_pairs={{0,96},{16,112},{32,64},{48,80},{64,32},{80,48},{96,0},{112,16},{1... | collective-permute-start | bytes 49160 | tf_op jit(solution)/shard_map/ppermute | solution.py:180
  58.0 5.2 %collective-permute-start.9 = (f32[1,4096]{1,0:T(1,128)S(1)}, f32[1,4096]{1,0:T(1,128)S(1)}, u32[]{:S(2)}, u32[]{:S(2)}) collective-permute-start(f32[1,4096]{1,0:T(1,128)S(1)} %add.21.c0), channel_id=1, source_target_pairs={{0,64},{16,80},{32,96},{48,112},{64,0},{80,16},{96,32},{112,48},{1... | collective-permute-start | bytes 49160 | tf_op jit(solution)/shard_map/ppermute | solution.py:180
  58.8 4.4 %collective-permute-start.8 = (f32[1,4096]{1,0:T(1,128)S(1)}, f32[1,4096]{1,0:T(1,128)S(1)}, u32[]{:S(2)}, u32[]{:S(2)}) collective-permute-start(f32[1,4096]{1,0:T(1,128)S(1)} %add.21.c0), channel_id=1, source_target_pairs={{0,32},{16,48},{32,0},{48,16},{64,96},{80,112},{96,64},{112,80},{1... | collective-permute-start | bytes 49160 | tf_op jit(solution)/shard_map/ppermute | solution.py:180
  84.0 1.3 collective-permute-start.11
  85.3 14.1 %collective-permute-start.14 = (f32[1,4096]{1,0:T(1,128)S(1)}, f32[1,4096]{1,0:T(1,128)S(1)}, u32[]{:S(2)}, u32[]{:S(2)}) collective-permute-start(f32[1,4096]{1,0:T(1,128)S(1)} %add.22.c0), channel_id=1, source_target_pairs={{0,96},{16,112},{32,64},{48,80},{64,32},{80,48},{96,0},{112,16},{1... | collective-permute-start | bytes 49160 | tf_op jit(solution)/shard_map/ppermute | solution.py:180
  86.1 13.2 %collective-permute-start.13 = (f32[1,4096]{1,0:T(1,128)S(1)}, f32[1,4096]{1,0:T(1,128)S(1)}, u32[]{:S(2)}, u32[]{:S(2)}) collective-permute-start(f32[1,4096]{1,0:T(1,128)S(1)} %add.22.c0), channel_id=1, source_target_pairs={{0,64},{16,80},{32,96},{48,112},{64,0},{80,16},{96,32},{112,48},{1... | collective-permute-start | bytes 49160 | tf_op jit(solution)/shard_map/ppermute | solution.py:180
  87.5 11.9 %collective-permute-start.12 = (f32[1,4096]{1,0:T(1,128)S(1)}, f32[1,4096]{1,0:T(1,128)S(1)}, u32[]{:S(2)}, u32[]{:S(2)}) collective-permute-start(f32[1,4096]{1,0:T(1,128)S(1)} %add.22.c0), channel_id=1, source_target_pairs={{0,32},{16,48},{32,0},{48,16},{64,96},{80,112},{96,64},{112,80},{1... | collective-permute-start | bytes 49160 | tf_op jit(solution)/shard_map/ppermute | solution.py:180
  120.7 1.3 collective-permute-start.15
  121.9 5.2 %collective-permute-start.18 = (f32[1,4096]{1,0:T(1,128)S(1)}, f32[1,4096]{1,0:T(1,128)S(1)}, u32[]{:S(2)}, u32[]{:S(2)}) collective-permute-start(f32[1,4096]{1,0:T(1,128)S(1)} %add.23.c0), channel_id=1, source_target_pairs={{0,96},{16,112},{32,64},{48,80},{64,32},{80,48},{96,0},{112,16},{1... | collective-permute-start | bytes 49160 | tf_op jit(solution)/shard_map/ppermute | solution.py:180
  122.8 5.2 %collective-permute-start.17 = (f32[1,4096]{1,0:T(1,128)S(1)}, f32[1,4096]{1,0:T(1,128)S(1)}, u32[]{:S(2)}, u32[]{:S(2)}) collective-permute-start(f32[1,4096]{1,0:T(1,128)S(1)} %add.23.c0), channel_id=1, source_target_pairs={{0,64},{16,80},{32,96},{48,112},{64,0},{80,16},{96,32},{112,48},{1... | collective-permute-start | bytes 49160 | tf_op jit(solution)/shard_map/ppermute | solution.py:180
  124.2 3.8 %collective-permute-start.16 = (f32[1,4096]{1,0:T(1,128)S(1)}, f32[1,4096]{1,0:T(1,128)S(1)}, u32[]{:S(2)}, u32[]{:S(2)}) collective-permute-start(f32[1,4096]{1,0:T(1,128)S(1)} %add.23.c0), channel_id=1, source_target_pairs={{0,32},{16,48},{32,0},{48,16},{64,96},{80,112},{96,64},{112,80},{1... | collective-permute-start | bytes 49160 | tf_op jit(solution)/shard_map/ppermute | solution.py:180
  163.6 3.7 %collective-permute-start.19 = (bf16[4,512,256]{2,1,0:T(8,128)(2,1)}, bf16[4,512,256]{2,1,0:T(8,128)(2,1)S(1)}, u32[]{:S(2)}, u32[]{:S(2)}) collective-permute-start(bf16[4,512,256]{2,1,0:T(8,128)(2,1)} %get-tuple-element.37), channel_id=1, source_target_pairs={{0,16},{16,0},{32,48},{48,32},{64,80},{80,64},{96,112},{112,96},{1... | collective-permute-start | bytes 3145736 | tf_op jit(solution)/shard_map/ppermute | solution.py:180
  163.6 23.7 %all-to-all-start.4 = ((bf16[16,128,256]{2,1,0:T(8,128)(2,1)}), bf16[16,128,256]{2,1,0:T(8,128)(2,1)S(1)}, u32[]{:S(2)}, u32[]{:S(2)}) async-start(bf16[16,128,256]{2,1,0:T(8,128)(2,1)} %get-tuple-element.35), calls=%async_computation.4 | async-start | bytes 2097152 | tf_op jit(solution)/shard_map/all_to_all | solution.py:267
  167.3 1.0 copy-start.4
  168.3 7.2 %copy-start.6 = (f32[128,1]{1,0:T(8,128)S(1)}, f32[128,1]{1,0:T(8,128)}, u32[]{:S(2)}) copy-start(f32[128,1]{1,0:T(8,128)} %get-tuple-element.39) | copy-start | bytes 1540
  170.5 17.6 %copy-start.5 = (bf16[128,256]{1,0:T(8,128)(2,1)S(1)}, bf16[128,256]{1,0:T(8,128)(2,1)}, u32[]{:S(2)}) copy-start(bf16[128,256]{1,0:T(8,128)(2,1)} %sf.1) | copy-start | bytes 196612
  170.5 18.5 %copy-start.1 = (bf16[512,256]{1,0:T(8,128)(2,1)S(1)}, bf16[512,256]{1,0:T(8,128)(2,1)}, u32[]{:S(2)}) copy-start(bf16[512,256]{1,0:T(8,128)(2,1)} %sp.1) | copy-start | bytes 786436
  171.4 15.9 %collective-permute-start.22 = (bf16[512,256]{1,0:T(8,128)(2,1)}, bf16[512,256]{1,0:T(8,128)(2,1)}, u32[]{:S(2)}, u32[]{:S(2)}) collective-permute-start(bf16[512,256]{1,0:T(8,128)(2,1)} %get-tuple-element.46), channel_id=1, source_target_pairs={{0,96},{16,112},{32,64},{48,80},{64,32},{80,48},{96,0},{112,16},{1... | collective-permute-start | bytes 786440 | tf_op jit(solution)/shard_map/ppermute | solution.py:180
  173.9 13.4 %collective-permute-start.21 = (bf16[512,256]{1,0:T(8,128)(2,1)}, bf16[512,256]{1,0:T(8,128)(2,1)}, u32[]{:S(2)}, u32[]{:S(2)}) collective-permute-start(bf16[512,256]{1,0:T(8,128)(2,1)} %get-tuple-element.47), channel_id=1, source_target_pairs={{0,64},{16,80},{32,96},{48,112},{64,0},{80,16},{96,32},{112,48},{1... | collective-permute-start | bytes 786440 | tf_op jit(solution)/shard_map/ppermute | solution.py:180
  175.3 12.6 %collective-permute-start.20 = (bf16[512,256]{1,0:T(8,128)(2,1)}, bf16[512,256]{1,0:T(8,128)(2,1)}, u32[]{:S(2)}, u32[]{:S(2)}) collective-permute-start(bf16[512,256]{1,0:T(8,128)(2,1)} %get-tuple-element.48), channel_id=1, source_target_pairs={{0,32},{16,48},{32,0},{48,16},{64,96},{80,112},{96,64},{112,80},{1... | collective-permute-start | bytes 786440 | tf_op jit(solution)/shard_map/ppermute | solution.py:180

commit v3 on v2

v3 whole, which is shorter than its diff:
```python
import functools

import jax
import jax.numpy as jnp
from jax import lax
from jax.experimental import pallas as pl
from jax.experimental.pallas import tpu as pltpu
from jax.sharding import PartitionSpec as P

ITERS = 3
LOG2E = 1.4426950408889634
teacher_temp = 0.07
student_temp = 0.1
epsilon = 1e-06

F32 = jnp.float32
BF16 = jnp.bfloat16
MIB = 2**20
VM = pl.BlockSpec(memory_space=pltpu.VMEM)
SM = pl.BlockSpec(memory_space=pltpu.SMEM)
NT = (((1,), (1,)), ((), ()))
NN = (((1,), (0,)), ((), ()))


def unit_rows(x):
    wide = x.astype(F32)
    scale = lax.rsqrt(jnp.sum(wide * wide, -1, keepdims=True) + epsilon)
    return (wide * scale, scale)


def project_back(grad, x):
    unit, scale = unit_rows(x)
    return (grad - unit * jnp.sum(unit * grad, -1, keepdims=True)) * scale


def fold(x):
    return x.reshape(-1, 8, x.shape[1]).sum(0)


def spread(row, out):
    for k in range(row.shape[1] // 128):
        part = row[:, k * 128 : (k + 1) * 128]
        out[k * 128 : (k + 1) * 128, :] = jnp.broadcast_to(part, (128, 128)).T


def gather_lanes(part, out):
    for k in range(part.shape[0] // 128):
        out[0:1, k * 128 : (k + 1) * 128] = part[k * 128 : (k + 1) * 128, :].T.sum(0, keepdims=True)


def unit_kernel(tf, sf, tp, sp, feats, protos):
    dim = tf.shape[1]
    for k, (x, y) in enumerate(((tf, tp), (sf, sp))):
        half = slice(k * dim, (k + 1) * dim)
        unit = unit_rows(x[...])[0].astype(BF16)
        for i in range(feats.shape[0]):
            feats[i, :, half] = unit
        protos[:, half] = unit_rows(y[...])[0].astype(BF16)


def load_half(half, feats, pieces, ft, pt, sem):
    dim = ft.shape[1]
    cols = pl.ds(half * dim, dim)
    first = pltpu.make_async_copy(feats.at[:, cols], ft, sem.at[len(pieces)])
    first.start()
    for r, piece in enumerate(pieces):
        pltpu.make_async_copy(piece.at[:, cols], pt.at[r], sem.at[r]).start()

    def wait_piece(r):
        pltpu.make_async_copy(pieces[0].at[:, cols], pt.at[r], sem.at[r]).wait()

    return first.wait, wait_piece


def exp_kernel(me, feats, *refs):
    pieces, (e, c, ft, pt, sem) = refs[:-5], refs[-5:]
    own = pt.shape[1]
    wait_feats, wait_piece = load_half(0, feats, pieces, ft, pt, sem)
    wait_feats()

    @pl.loop(0, len(pieces))
    def _(r):
        wait_piece(r)
        s = lax.dot_general(ft[...], pt[r], NT, preferred_element_type=F32)
        x = jnp.exp2(s * (LOG2E / teacher_temp))
        e[:, pl.ds(pl.multiple_of(r * own, own), own)] = x
        c[:, pl.ds(pl.multiple_of((me[0] ^ r) * own, own), own)] = fold(x).sum(0, keepdims=True)


def total_kernel(feats, *refs):
    pieces, (z, ft, pt, sem, part) = refs[:-5], refs[-5:]
    own = pt.shape[1]
    wait_feats, wait_piece = load_half(1, feats, pieces, ft, pt, sem)
    part[...] = jnp.zeros_like(part)
    wait_feats()

    @pl.loop(0, len(pieces))
    def _(r):
        wait_piece(r)
        s = lax.dot_general(ft[...], pt[r], NT, preferred_element_type=F32)
        x = jnp.exp2(s * (LOG2E / student_temp))
        acc = x[:, :128]
        for k in range(1, own // 128):
            acc += x[:, k * 128 : (k + 1) * 128]
        part[...] += acc

    gather_lanes(part, z)


def row_kernel(block, own, me, e, c0, c1, c2, c3, *refs):
    z, (r, b, part) = refs[:-3], refs[-3:]
    rows, cols = e.shape
    for k in range(cols // own):
        src = pl.ds(pl.multiple_of((me[0] ^ k) * own, own), own)
        b[:, k * own : (k + 1) * own] = 1.0 / (c0[:, src] + c1[:, src] + c2[:, src] + c3[:, src])

    @pl.loop(0, rows // block)
    def _(i):
        ii = pl.ds(pl.multiple_of(i * block, block), block)
        acc = jnp.zeros((block, 128), F32)
        for k in range(cols // 128):
            lanes = slice(k * 128, (k + 1) * 128)
            acc += e[ii, lanes] * b[:, lanes]
        part[ii, :] = acc

    gather_lanes(part, r.at[0])
    if z:
        r[0, 1:2, :] = z[0][...]
    for k in range(1, r.shape[0]):
        r[k] = r[0]


def col_kernel(block, width, own, me, e, sums, c, av):
    rows, cols = e.shape
    spread(1.0 / jnp.sum(sums[:, 0, :], 0, keepdims=True), av)
    for j in range(cols // width):

        def step(i, acc, j=j):
            ii = pl.ds(pl.multiple_of(i * block, block), block)
            w = av[ii, :]
            return tuple(
                acc[k] + fold(e[ii, j * width + k * 128 : j * width + (k + 1) * 128] * w)
                for k in range(width // 128)
            )

        zero = jnp.zeros((8, 128), F32)
        acc = lax.fori_loop(0, rows // block, step, (zero,) * (width // 128))
        for k in range(width // own):
            part = jnp.concatenate(acc[k * own // 128 : (k + 1) * own // 128], 1)
            to = (me[0] ^ (j * width // own + k)) * own
            c[:, pl.ds(pl.multiple_of(to, own), own)] = part.sum(0, keepdims=True)


def grad_kernel(count, e, feats, b, sums, zsums, *refs):
    pieces, refs = refs[:count], refs[count:]
    f, keep, give, ft, pt, sem, av, zv, g0, g1, acc, turned, kept, given, out_sem = refs
    own = pt.shape[1]
    wait_feats, wait_piece = load_half(1, feats, pieces, ft, pt, sem)
    spread((1.0 / student_temp) / jnp.sum(sums[:, 0, :], 0, keepdims=True), av)
    spread((1.0 / student_temp) / jnp.sum(zsums[:, 1, :], 0, keepdims=True), zv)
    acc[...] = jnp.zeros_like(acc)
    wait_feats()
    turned[...] = ft[...].T
    wide = lambda m: jnp.concatenate([m] * (own // 128), 1)

    def put(h, k):
        src, dst = ((kept, keep), (given, give))[k]
        return pltpu.make_async_copy(src.at[h], dst.at[h], out_sem.at[h, k])

    @pl.loop(0, count // 2)
    def _(h):
        new = []
        wait_piece(2 * h)
        wait_piece(2 * h + 1)
        for k, (g, out) in enumerate(((g0, kept), (g1, given))):
            cols = pl.ds(pl.multiple_of((2 * h + k) * own, own), own)
            sp = pt[2 * h + k]
            s = lax.dot_general(ft[...], sp, NT, preferred_element_type=F32)
            p = jnp.exp2(s * (LOG2E / student_temp))
            g[...] = (p * wide(zv[...]) - wide(av[...]) * (e[:, cols] * b[:, cols])).astype(BF16)
            out[h] = lax.dot_general(turned[...], g[...], NN, preferred_element_type=F32).T.astype(out.dtype)
            new.append(lax.dot_general(g[...], sp, NN, preferred_element_type=F32))
        acc[...] += new[0] + new[1]
        put(h, 0).start()
        put(h, 1).start()

    f[...] = acc[...].astype(BF16).reshape(f.shape)
    for h in range(count // 2):
        put(h, 0).wait()
        put(h, 1).wait()


def merge_kernel(keep, got, first, *rest):
    first[...] = keep[0] + got[0].astype(F32)
    for k, out in enumerate(rest):
        out[...] = (keep[k + 1] + got[k + 1].astype(F32)).astype(BF16)


def final_kernel(f, sf, sp, half, *refs):
    got, (f_out, p_out) = refs[:-2], refs[-2:]
    f_out[...] = project_back(jnp.sum(f[...].astype(F32), 0), sf[...])
    p = half[...]
    for x in got:
        p += x[...].astype(F32)
    p_out[...] = project_back(p, sp[...])


def call(kernel, name, out_shape, ops, scratch=(), limit=26, smem=0, keep=(), raw=(), raw_out=()):
    many = isinstance(out_shape, (list, tuple))
    ops = list(ops[:smem]) + [
        pltpu.with_memory_space_constraint(x, pltpu.VMEM if i in keep else pltpu.HBM)
        for i, x in enumerate(ops[smem:])
    ]
    whole = pl.BlockSpec(memory_space=pl.ANY)
    return pl.pallas_call(
        kernel,
        out_shape=out_shape,
        in_specs=[SM] * smem + [whole if i in raw else VM for i in range(len(ops) - smem)],
        out_specs=[whole if i in raw_out else VM for i in range(len(out_shape))] if many else VM,
        scratch_shapes=list(scratch),
        compiler_params=pltpu.CompilerParams(vmem_limit_bytes=limit * MIB),
        name=name,
    )(*ops)


def shards(nb, npr, teacher_feats, student_feats, teacher_protos, student_protos):
    swap = lambda x, k: lax.ppermute(x, "batch", [(i, i ^ k) for i in range(nb)])

    dim = teacher_feats.shape[1]
    own_rows, own = student_feats.shape[0], student_protos.shape[0]
    rows, cols = own_rows * npr, own * nb
    me = lax.axis_index("batch").astype(jnp.int32).reshape(1)
    hbm, vmem = pltpu.HBM, pltpu.VMEM

    feats, unit = call(
        unit_kernel,
        "unit_rows",
        [hbm((npr, own_rows, 2 * dim), BF16), hbm((own, 2 * dim), BF16)],
        [teacher_feats, student_feats, teacher_protos, student_protos],
    )
    pieces = [unit] + [None] * (nb - 1)
    for r in range(2, nb, 2):
        pieces[r] = swap(unit, r)
    feats = lax.all_to_all(feats, "proto", 0, 0).reshape(rows, 2 * dim)
    for r in range(0, nb, 2):
        pieces[r + 1] = swap(pieces[r], 1)

    lanes = vmem((rows, 128), F32)
    all_cols = vmem((1, cols), F32)
    halves = [vmem((rows, dim), BF16), vmem((nb, own, dim), BF16), pltpu.SemaphoreType.DMA((nb + 1,))]
    e, c = call(
        exp_kernel,
        "teacher_exp",
        [vmem((rows, cols), F32), all_cols],
        [me, feats, *pieces],
        halves,
        smem=1,
        raw=range(nb + 1),
    )
    for iteration in range(ITERS):
        if iteration:
            c = call(
                functools.partial(col_kernel, 128, 2048, own),
                "column_sums",
                all_cols,
                [me, e, sums],
                [lanes],
                smem=1,
                keep=(0, 1),
            )
        c = c + swap(c, 1)
        cs = [c] + [swap(c, k) for k in range(2, nb, 2)]
        if iteration == 1:
            z = call(
                total_kernel,
                "student_total",
                hbm((1, rows), F32),
                [feats, *pieces],
                halves + [lanes],
                raw=range(nb + 1),
            )
        extra = [z] if iteration == 1 else []
        r, b = call(
            functools.partial(row_kernel, 128, own),
            "row_sums",
            [vmem((npr, 1 + len(extra), rows), F32), all_cols],
            [me, e, *cs, *extra],
            [lanes],
            smem=1,
            keep=(0, 1, 2, 3, 4),
        )
        sums = lax.all_to_all(r, "proto", 0, 0)
        if extra:
            zsums = sums
    half_g = vmem((rows, own), BF16)
    f, keep, give = call(
        functools.partial(grad_kernel, nb),
        "logit_grad",
        [
            hbm((npr, own_rows, dim), BF16),
            hbm((nb // 2, own, dim), F32),
            hbm((nb // 2, own, dim), BF16),
        ],
        [e, feats, b, sums, zsums, *pieces],
        halves
        + [lanes, lanes, half_g, half_g, vmem((rows, dim), F32), vmem((dim, rows), BF16)]
        + [vmem((nb // 2, own, dim), F32), vmem((nb // 2, own, dim), BF16)]
        + [pltpu.SemaphoreType.DMA((nb // 2, 2))],
        keep=(0, 2, 3, 4),
        raw=(1, *range(5, 5 + nb)),
        raw_out=(1, 2),
    )
    half = call(
        merge_kernel,
        "merge_cores",
        [hbm((own, dim), F32)] + [vmem((own, dim), BF16)] * (nb // 2 - 1),
        [keep, swap(give, 1)],
        keep=(1,),
    )
    got = [swap(x, 2 * k + 2) for k, x in enumerate(half[1:])]
    f, *got = lax.optimization_barrier((lax.all_to_all(f, "proto", 0, 0), *got))
    return call(
        final_kernel,
        "project_back",
        [jax.ShapeDtypeStruct((own_rows, dim), F32), jax.ShapeDtypeStruct((own, dim), F32)],
        [f, student_feats, student_protos, half[0], *got],
        keep=(0, *range(4, 3 + nb // 2)),
    )


def solution(mesh):
    nb, npr = mesh.shape["batch"], mesh.shape["proto"]
    in_specs = (
        P(("batch", "proto"), None),
        P(("batch", "proto"), None),
        P(("proto", "batch"), None),
        P(("proto", "batch"), None),
    )
    out_specs = (P(("batch", "proto"), None), P(("proto", "batch"), None))
    return jax.shard_map(
        functools.partial(shards, nb, npr),
        mesh=mesh,
        in_specs=in_specs,
        out_specs=out_specs,
        check_vma=False,
    )
```

time: 194 us -> 182 us (0.938)
  other arithmetic: 8.02 us -> 0.06 us
  waiting for transfers between devices: 47.4 us -> 50.5 us
  blocking collectives: 38.1 us -> 35.4 us
  Pallas kernels: 61.4 us -> 59.2 us
    mul x2 -> x0, other arithmetic: 2.9 us -> none  [project_back(): (grad - unit_rows * jnp.sum(unit_rows * grad, -1, keepdims=True)) * scale]
    all_to_all x3, blocking collectives: 38.1 us -> 35.4 us  [shards(): sums = lax.all_to_all(r, 'proto', 0, 0)]
    another operation x1 -> x0, other arithmetic: 2.19 us -> none
    all_to_all x1, waiting for transfers between devices: 10.5 us -> 12.7 us  [shards(): f, *got = lax.optimization_barrier((lax.all_to_all(f, 'proto', 0, 0), *got))]
    pallas_call x9 -> x11, Pallas kernels: 61.4 us -> 59.2 us  [call(): pl.pallas_call(kernel, out_shape=out_shape, in_specs=[SM] * smem + [whole...]
  transfers between devices with their start and end apart: 25 -> 25, of which waited for: 15 -> 15; matrix products, arithmetic and copies ran while one was open for 2% -> 0% of each run, Pallas kernels for 5% -> 6%
where the time goes in v3:
time: 182 us; the launch traced here: 181 us
  Pallas kernels  59.2 us (33%)
  waiting for transfers between devices  50.5 us (28%)
  blocking collectives  35.4 us (19%)
  starting transfers between devices  34.2 us (19%)
    pallas_call x11, Pallas kernels, call(): pl.pallas_call(kernel, out_shape=out_shape, in_specs=[SM] * smem + [whole...  59.2 us
    ppermute x23, waiting for transfers between devices, shards(): lax.ppermute(x, 'batch', [(i, i ^ k) for i in range(nb)])  35.8 us
    all_to_all x3, blocking collectives, shards(): sums = lax.all_to_all(r, 'proto', 0, 0)  35.4 us
    ppermute x23, starting transfers between devices, shards(): lax.ppermute(x, 'batch', [(i, i ^ k) for i in range(nb)])  22.2 us
    all_to_all x1, waiting for transfers between devices, shards(): f, *got = lax.optimization_barrier((lax.all_to_all(f, 'proto', 0, 0), *got))  12.7 us
    all_to_all x1, starting transfers between devices, shards(): feats = lax.all_to_all(feats, 'proto', 0, 0).reshape(rows, 2 * dim)  8.26 us
    all_to_all x1, starting transfers between devices, shards(): f, *got = lax.optimization_barrier((lax.all_to_all(f, 'proto', 0, 0), *got))  3.66 us
  transfers between devices with their start and end apart: 25, of which 15 were waited for; matrix products, arithmetic and copies ran while one was open for 0% of the time, Pallas kernels for 6%

profile of v3, /device:TPU:0, one launch (start us, length us, event | category | flops | bytes accessed | tf_op | source)
XLA Modules:
  0.0 181.5 jit_solution(8379232595623353529)
XLA Ops:
  0.6 3.0 %unit_rows.1 = (bf16[16,128,512]{2,1,0:T(8,128)(2,1)}, bf16[512,512]{1,0:T(8,128)(2,1)}) custom-call(bf16[128,256]{1,0:T(8,128)(2,1)} %tf.1, bf16[128,256]{1,0:T(8,128)(2,1)} %sf.3, bf16[512,256]{1,0:T(8,128)(2,1)} %tp.1, bf16[512,256]{1,0:T(8,128)(2,1)} %sp.3), custom_call_target="tpu_custom_call" | custom-call | tf_op jit(solution)/shard_map/unit_rows/pallas_call | solution.py:215
  3.6 8.3 %all-to-all-start = ((bf16[16,128,512]{2,1,0:T(8,128)(2,1)}), bf16[16,128,512]{2,1,0:T(8,128)(2,1)S(1)}, u32[]{:S(2)}, u32[]{:S(2)}) async-start(bf16[16,128,512]{2,1,0:T(8,128)(2,1)} %get-tuple-element.21), calls=%async_computation | async-start | bytes 4194304 | tf_op jit(solution)/shard_map/all_to_all | solution.py:244
  11.9 2.8 %collective-permute-start.5 = (bf16[512,512]{1,0:T(8,128)(2,1)S(1)}, bf16[512,512]{1,0:T(8,128)(2,1)S(1)}, u32[]{:S(2)}, u32[]{:S(2)}) collective-permute-start(bf16[512,512]{1,0:T(8,128)(2,1)S(1)} %copy-done.1), channel_id=1, source_target_pairs={{0,96},{16,112},{32,64},{48,80},{64,32},{80,48},{96,0},{112,16},{1... | collective-permute-start | bytes 1572872 | tf_op jit(solution)/shard_map/ppermute | solution.py:227
  14.7 0.8 collective-permute-start.3
  15.5 0.5 collective-permute-start.1
  16.1 0.0 collective-permute-start
  16.1 21.7 %collective-permute-done.5.refs_6_ = bf16[512,512]{1,0:T(8,128)(2,1)S(1)} collective-permute-done((bf16[512,512]{1,0:T(8,128)(2,1)S(1)}, bf16[512,512]{1,0:T(8,128)(2,1)S(1)}, u32[]{:S(2)}, u32[]{:S(2)}) %collective-permute-start.5) | collective-permute-done | bytes 524320 | tf_op jit(solution)/shard_map/ppermute | solution.py:227
  37.8 0.0 collective-permute-start.6
  37.8 0.0 collective-permute-done.3.refs_4_
  37.8 0.5 collective-permute-start.4
  38.3 0.2 collective-permute-done.1.refs_2_
  38.5 0.0 collective-permute-start.2
  38.5 0.0 collective-permute-done.refs_1_
  38.5 1.3 collective-permute-done.6.refs_7_
  39.8 1.0 collective-permute-done.4.refs_5_
  40.8 0.7 collective-permute-done.2.refs_3_
  41.5 2.0 %all-to-all-done = bf16[16,128,512]{2,1,0:T(8,128)(2,1)S(1)} async-done(((bf16[16,128,512]{2,1,0:T(8,128)(2,1)}), bf16[16,128,512]{2,1,0:T(8,128)(2,1)S(1)}, u32[]{:S(2)}, u32[]{:S(2)}) %all-to-all-start) | async-done | bytes 2097184 | tf_op jit(solution)/shard_map/all_to_all | solution.py:244
  43.5 1.3 copy-done
  44.9 7.4 %teacher_exp.1 = (f32[2048,4096]{1,0:T(8,128)S(1)}, f32[1,4096]{1,0:T(1,128)S(1)}) custom-call(s32[1]{0:T(128)} %bitcast.me, bf16[2048,512]{1,0:T(8,128)(2,1)} %bitcast.2, bf16[512,512]{1,0:T(8,128)(2,1)} %get-tuple-element.22.refs_0_, bf16[512,512]{1,0:T(8,128)(2,1)} %collective-permute-done.refs_1_, bf16[512,512]{1,0:T(8,128)(2,1)} %collective-permute-done.1.refs_2_, ...), custom_call_target="tpu_custom_call" | custom-call | tf_op jit(solution)/shard_map/teacher_exp/pallas_call | solution.py:215
  52.2 0.1 collective-permute-start.7
  52.3 1.2 collective-permute-done.7
  53.5 2.8 %collective-permute-start.10 = (f32[1,4096]{1,0:T(1,128)S(1)}, f32[1,4096]{1,0:T(1,128)S(1)}, u32[]{:S(2)}, u32[]{:S(2)}) collective-permute-start(f32[1,4096]{1,0:T(1,128)S(1)} %add.9.c0), channel_id=1, source_target_pairs={{0,96},{16,112},{32,64},{48,80},{64,32},{80,48},{96,0},{112,16},{1... | collective-permute-start | bytes 49160 | tf_op jit(solution)/shard_map/ppermute | solution.py:227
  56.4 0.8 collective-permute-start.9
  57.2 0.5 collective-permute-start.8
  57.7 0.9 collective-permute-done.10.c3
  58.6 3.0 %collective-permute-done.9.c2 = f32[1,4096]{1,0:T(1,128)S(1)} collective-permute-done((f32[1,4096]{1,0:T(1,128)S(1)}, f32[1,4096]{1,0:T(1,128)S(1)}, u32[]{:S(2)}, u32[]{:S(2)}) %collective-permute-start.9) | collective-permute-done | bytes 16416 | tf_op jit(solution)/shard_map/ppermute | solution.py:227
  61.6 0.0 collective-permute-done.8.c1
  61.6 3.2 %row_sums.3 = (f32[16,1,2048]{2,1,0:T(1,128)S(1)}, f32[1,4096]{1,0:T(1,128)}) custom-call(s32[1]{0:T(128)} %bitcast.me, f32[2048,4096]{1,0:T(8,128)S(1)} %get-tuple-element.23.e, f32[1,4096]{1,0:T(1,128)S(1)} %add.9.c0, f32[1,4096]{1,0:T(1,128)S(1)} %collective-permute-done.8.c1, f32[1,4096]{1,0:T(1,128)S(1)} %collective-permute-done.9.c2, ...), custom_call_target="tpu_custom_call" | custom-call | tf_op jit(solution)/shard_map/row_sums/pallas_call | solution.py:215
  64.8 12.7 %all_to_all.25.sums = f32[16,1,2048]{2,1,0:T(1,128)S(1)} all-to-all(f32[16,1,2048]{2,1,0:T(1,128)S(1)} %get-tuple-element.25), channel_id=1, replica_groups=mesh['batch'=8,'proto'=16] {'proto'}, dimensions={0} | all-to-all | bytes 262144 | tf_op jit(solution)/shard_map/all_to_all | solution.py:292
  77.6 3.1 %column_sums.2 = f32[1,4096]{1,0:T(1,128)S(1)} custom-call(s32[1]{0:T(128)} %bitcast.me, f32[2048,4096]{1,0:T(8,128)S(1)} %get-tuple-element.23.e, f32[16,1,2048]{2,1,0:T(1,128)S(1)} %all_to_all.25.sums), custom_call_target="tpu_custom_call" | custom-call | tf_op jit(solution)/shard_map/column_sums/pallas_call | solution.py:215
  80.7 0.1 collective-permute-start.11
  80.8 1.2 collective-permute-done.11
  82.0 0.8 collective-permute-start.14
  82.8 1.4 collective-permute-start.13
  84.2 2.0 %collective-permute-start.12 = (f32[1,4096]{1,0:T(1,128)S(1)}, f32[1,4096]{1,0:T(1,128)S(1)}, u32[]{:S(2)}, u32[]{:S(2)}) collective-permute-start(f32[1,4096]{1,0:T(1,128)S(1)} %add.10.c0), channel_id=1, source_target_pairs={{0,32},{16,48},{32,0},{48,16},{64,96},{80,112},{96,64},{112,80},{1... | collective-permute-start | bytes 49160 | tf_op jit(solution)/shard_map/ppermute | solution.py:227
  86.1 8.2 %student_total.1.refs_0_ = f32[1,2048]{1,0:T(1,128)} custom-call(bf16[2048,512]{1,0:T(8,128)(2,1)} %bitcast.3, bf16[512,512]{1,0:T(8,128)(2,1)} %get-tuple-element.22.refs_0_, bf16[512,512]{1,0:T(8,128)(2,1)} %collective-permute-done.refs_1_, bf16[512,512]{1,0:T(8,128)(2,1)} %collective-permute-done.1.refs_2_, ...), custom_call_target="tpu_custom_call" | custom-call | tf_op jit(solution)/shard_map/student_total/pallas_call | solution.py:215
  94.4 0.0 collective-permute-done.14.c3
  94.4 0.0 collective-permute-done.12.c1
  94.4 3.8 %row_sums.4 = (f32[16,2,2048]{2,1,0:T(2,128)S(1)}, f32[1,4096]{1,0:T(1,128)}) custom-call(s32[1]{0:T(128)} %bitcast.me, f32[2048,4096]{1,0:T(8,128)S(1)} %get-tuple-element.23.e, f32[1,4096]{1,0:T(1,128)S(1)} %add.10.c0, f32[1,4096]{1,0:T(1,128)S(1)} %collective-permute-done.12.c1, f32[1,4096]{1,0:T(1,128)S(1)} %collective-permute-done.13.c2, ...), custom_call_target="tpu_custom_call" | custom-call | tf_op jit(solution)/shard_map/row_sums/pallas_call | solution.py:215
  98.2 11.8 %all_to_all.26.sums.zsums = f32[16,2,2048]{2,1,0:T(2,128)S(1)} all-to-all(f32[16,2,2048]{2,1,0:T(2,128)S(1)} %get-tuple-element.26), channel_id=1, replica_groups=mesh['batch'=8,'proto'=16] {'proto'}, dimensions={0} | all-to-all | bytes 524288 | tf_op jit(solution)/shard_map/all_to_all | solution.py:292
  110.0 3.1 %column_sums.3 = f32[1,4096]{1,0:T(1,128)S(1)} custom-call(s32[1]{0:T(128)} %bitcast.me, f32[2048,4096]{1,0:T(8,128)S(1)} %get-tuple-element.23.e, f32[16,2,2048]{2,1,0:T(2,128)S(1)} %all_to_all.26.sums.zsums), custom_call_target="tpu_custom_call" | custom-call | tf_op jit(solution)/shard_map/column_sums/pallas_call | solution.py:215
  113.1 0.1 collective-permute-start.15
  113.2 1.2 collective-permute-done.15
  114.3 0.8 collective-permute-start.18
  115.2 1.4 collective-permute-start.17
  116.5 2.0 %collective-permute-start.16 = (f32[1,4096]{1,0:T(1,128)S(1)}, f32[1,4096]{1,0:T(1,128)S(1)}, u32[]{:S(2)}, u32[]{:S(2)}) collective-permute-start(f32[1,4096]{1,0:T(1,128)S(1)} %add.11.c0), channel_id=1, source_target_pairs={{0,32},{16,48},{32,0},{48,16},{64,96},{80,112},{96,64},{112,80},{1... | collective-permute-start | bytes 49160 | tf_op jit(solution)/shard_map/ppermute | solution.py:227
  118.5 1.0 collective-permute-done.18.c3
  119.5 0.9 collective-permute-done.17.c2
  120.4 0.0 collective-permute-done.16.c1
  120.4 3.0 %row_sums.5 = (f32[16,1,2048]{2,1,0:T(1,128)S(1)}, f32[1,4096]{1,0:T(1,128)S(1)}) custom-call(s32[1]{0:T(128)} %bitcast.me, f32[2048,4096]{1,0:T(8,128)S(1)} %get-tuple-element.23.e, f32[1,4096]{1,0:T(1,128)S(1)} %add.11.c0, f32[1,4096]{1,0:T(1,128)S(1)} %collective-permute-done.16.c1, f32[1,4096]{1,0:T(1,128)S(1)} %collective-permute-done.17.c2, ...), custom_call_target="tpu_custom_call" | custom-call | tf_op jit(solution)/shard_map/row_sums/pallas_call | solution.py:215
  123.4 10.9 %all_to_all.27.sums = f32[16,1,2048]{2,1,0:T(1,128)S(1)} all-to-all(f32[16,1,2048]{2,1,0:T(1,128)S(1)} %get-tuple-element.28), channel_id=1, replica_groups=mesh['batch'=8,'proto'=16] {'proto'}, dimensions={0} | all-to-all | bytes 262144 | tf_op jit(solution)/shard_map/all_to_all | solution.py:292
  134.3 19.6 %logit_grad.1 = (bf16[16,128,256]{2,1,0:T(8,128)(2,1)}, f32[4,512,256]{2,1,0:T(8,128)}, bf16[4,512,256]{2,1,0:T(8,128)(2,1)}) custom-call(f32[2048,4096]{1,0:T(8,128)S(1)} %get-tuple-element.23.e, bf16[2048,512]{1,0:T(8,128)(2,1)} %bitcast.4, f32[1,4096]{1,0:T(1,128)S(1)} %get-tuple-element.27.b, f32[16,1,2048]{2,1,0:T(1,128)S(1)} %all_to_all.27.sums, ...), custom_call_target="tpu_custom_call" | custom-call | tf_op jit(solution)/shard_map/logit_grad/pallas_call | solution.py:215
  153.9 0.1 collective-permute-start.19
  154.0 3.7 %all-to-all-start.4 = ((bf16[16,128,256]{2,1,0:T(8,128)(2,1)}), bf16[16,128,256]{2,1,0:T(8,128)(2,1)S(1)}, u32[]{:S(2)}, u32[]{:S(2)}) async-start(bf16[16,128,256]{2,1,0:T(8,128)(2,1)} %get-tuple-element.29), calls=%async_computation.4 | async-start | bytes 2097152 | tf_op jit(solution)/shard_map/all_to_all | solution.py:321
  157.7 0.0 collective-permute-done.19.got
  157.7 2.4 %merge_cores.1 = (f32[512,256]{1,0:T(8,128)}, bf16[512,256]{1,0:T(8,128)(2,1)S(1)}, bf16[512,256]{1,0:T(8,128)(2,1)S(1)}, bf16[512,256]{1,0:T(8,128)(2,1)S(1)}) custom-call(f32[4,512,256]{2,1,0:T(8,128)} %get-tuple-element.30.keep, bf16[4,512,256]{2,1,0:T(8,128)(2,1)S(1)} %collective-permute-done.19.got), custom_call_target="tpu_custom_call" | custom-call | tf_op jit(solution)/shard_map/merge_cores/pallas_call | solution.py:215
  160.1 1.8 %collective-permute-start.20 = (bf16[512,256]{1,0:T(8,128)(2,1)S(1)}, bf16[512,256]{1,0:T(8,128)(2,1)S(1)}, u32[]{:S(2)}, u32[]{:S(2)}) collective-permute-start(bf16[512,256]{1,0:T(8,128)(2,1)S(1)} %get-tuple-element.32), channel_id=1, source_target_pairs={{0,32},{16,48},{32,0},{48,16},{64,96},{80,112},{96,64},{112,80},{1... | collective-permute-start | bytes 786440 | tf_op jit(solution)/shard_map/ppermute | solution.py:227
  161.9 2.1 %collective-permute-start.21 = (bf16[512,256]{1,0:T(8,128)(2,1)S(1)}, bf16[512,256]{1,0:T(8,128)(2,1)S(1)}, u32[]{:S(2)}, u32[]{:S(2)}) collective-permute-start(bf16[512,256]{1,0:T(8,128)(2,1)S(1)} %get-tuple-element.33), channel_id=1, source_target_pairs={{0,64},{16,80},{32,96},{48,112},{64,0},{80,16},{96,32},{112,48},{1... | collective-permute-start | bytes 786440 | tf_op jit(solution)/shard_map/ppermute | solution.py:227
  164.1 0.7 collective-permute-start.22
  164.8 12.7 %all-to-all-done.4.f = bf16[16,128,256]{2,1,0:T(8,128)(2,1)S(1)} async-done(((bf16[16,128,256]{2,1,0:T(8,128)(2,1)}), bf16[16,128,256]{2,1,0:T(8,128)(2,1)S(1)}, u32[]{:S(2)}, u32[]{:S(2)}) %all-to-all-start.4) | async-done | bytes 1048608 | tf_op jit(solution)/shard_map/all_to_all | solution.py:321
  177.5 0.0 collective-permute-done.20.refs_0_
  177.5 0.0 collective-permute-done.21.refs_1_
  177.5 1.5 collective-permute-done.22.refs_2_
  179.0 2.4 %project_back.1 = (f32[128,256]{1,0:T(8,128)}, f32[512,256]{1,0:T(8,128)}) custom-call(bf16[16,128,256]{2,1,0:T(8,128)(2,1)S(1)} %all-to-all-done.4.f, bf16[128,256]{1,0:T(8,128)(2,1)} %sf.3, bf16[512,256]{1,0:T(8,128)(2,1)} %sp.3, f32[512,256]{1,0:T(8,128)} %get-tuple-element.36.half, bf16[512,256]{1,0:T(8,128)(2,1)S(1)} %collective-permute-done.20.refs_0_, ...), custom_call_target="tpu_custom_call" | custom-call | tf_op jit(solution)/shard_map/project_back/pallas_call | solution.py:215
  (9 shorter events, 0.1 us)
Async XLA Ops:
  3.6 8.3 %copy-start.1 = (bf16[512,512]{1,0:T(8,128)(2,1)S(1)}, bf16[512,512]{1,0:T(8,128)(2,1)}, u32[]{:S(2)}) copy-start(bf16[512,512]{1,0:T(8,128)(2,1)} %get-tuple-element.22.refs_0_) | copy-start | bytes 1572868
  3.6 39.9 %all-to-all-start = ((bf16[16,128,512]{2,1,0:T(8,128)(2,1)}), bf16[16,128,512]{2,1,0:T(8,128)(2,1)S(1)}, u32[]{:S(2)}, u32[]{:S(2)}) async-start(bf16[16,128,512]{2,1,0:T(8,128)(2,1)} %get-tuple-element.21), calls=%async_computation | async-start | bytes 4194304 | tf_op jit(solution)/shard_map/all_to_all | solution.py:244
  11.9 25.9 %collective-permute-start.5 = (bf16[512,512]{1,0:T(8,128)(2,1)S(1)}, bf16[512,512]{1,0:T(8,128)(2,1)S(1)}, u32[]{:S(2)}, u32[]{:S(2)}) collective-permute-start(bf16[512,512]{1,0:T(8,128)(2,1)S(1)} %copy-done.1), channel_id=1, source_target_pairs={{0,96},{16,112},{32,64},{48,80},{64,32},{80,48},{96,0},{112,16},{1... | collective-permute-start | bytes 1572872 | tf_op jit(solution)/shard_map/ppermute | solution.py:227
  14.7 23.1 %collective-permute-start.3 = (bf16[512,512]{1,0:T(8,128)(2,1)S(1)}, bf16[512,512]{1,0:T(8,128)(2,1)}, u32[]{:S(2)}, u32[]{:S(2)}) collective-permute-start(bf16[512,512]{1,0:T(8,128)(2,1)S(1)} %copy-done.1), channel_id=1, source_target_pairs={{0,64},{16,80},{32,96},{48,112},{64,0},{80,16},{96,32},{112,48},{1... | collective-permute-start | bytes 1572872 | tf_op jit(solution)/shard_map/ppermute | solution.py:227
  15.5 23.0 %collective-permute-start.1 = (bf16[512,512]{1,0:T(8,128)(2,1)S(1)}, bf16[512,512]{1,0:T(8,128)(2,1)}, u32[]{:S(2)}, u32[]{:S(2)}) collective-permute-start(bf16[512,512]{1,0:T(8,128)(2,1)S(1)} %copy-done.1), channel_id=1, source_target_pairs={{0,32},{16,48},{32,0},{48,16},{64,96},{80,112},{96,64},{112,80},{1... | collective-permute-start | bytes 1572872 | tf_op jit(solution)/shard_map/ppermute | solution.py:227
  16.1 22.5 %collective-permute-start = (bf16[512,512]{1,0:T(8,128)(2,1)S(1)}, bf16[512,512]{1,0:T(8,128)(2,1)}, u32[]{:S(2)}, u32[]{:S(2)}) collective-permute-start(bf16[512,512]{1,0:T(8,128)(2,1)S(1)} %copy-done.1), channel_id=1, source_target_pairs={{0,16},{16,0},{32,48},{48,32},{64,80},{80,64},{96,112},{112,96},{1... | collective-permute-start | bytes 1572872 | tf_op jit(solution)/shard_map/ppermute | solution.py:227
  37.8 5.7 %copy-start.2 = (bf16[512,512]{1,0:T(8,128)(2,1)}, bf16[512,512]{1,0:T(8,128)(2,1)S(1)}, u32[]{:S(2)}) copy-start(bf16[512,512]{1,0:T(8,128)(2,1)S(1)} %collective-permute-done.5.refs_6_) | copy-start | bytes 1572868
  37.8 2.0 %collective-permute-start.6 = (bf16[512,512]{1,0:T(8,128)(2,1)S(1)}, bf16[512,512]{1,0:T(8,128)(2,1)}, u32[]{:S(2)}, u32[]{:S(2)}) collective-permute-start(bf16[512,512]{1,0:T(8,128)(2,1)S(1)} %collective-permute-done.5.refs_6_), channel_id=1, source_target_pairs={{0,16},{16,0},{32,48},{48,32},{64,80},{80,64},{96,112},{112,96},{1... | collective-permute-start | bytes 1572872 | tf_op jit(solution)/shard_map/ppermute | solution.py:227
  37.8 3.0 %collective-permute-start.4 = (bf16[512,512]{1,0:T(8,128)(2,1)}, bf16[512,512]{1,0:T(8,128)(2,1)}, u32[]{:S(2)}, u32[]{:S(2)}) collective-permute-start(bf16[512,512]{1,0:T(8,128)(2,1)} %collective-permute-done.3.refs_4_), channel_id=1, source_target_pairs={{0,16},{16,0},{32,48},{48,32},{64,80},{80,64},{96,112},{112,96},{1... | collective-permute-start | bytes 1572872 | tf_op jit(solution)/shard_map/ppermute | solution.py:227
  38.5 3.0 %collective-permute-start.2 = (bf16[512,512]{1,0:T(8,128)(2,1)}, bf16[512,512]{1,0:T(8,128)(2,1)}, u32[]{:S(2)}, u32[]{:S(2)}) collective-permute-start(bf16[512,512]{1,0:T(8,128)(2,1)} %collective-permute-done.1.refs_2_), channel_id=1, source_target_pairs={{0,16},{16,0},{32,48},{48,32},{64,80},{80,64},{96,112},{112,96},{1... | collective-permute-start | bytes 1572872 | tf_op jit(solution)/shard_map/ppermute | solution.py:227
  43.5 1.3 copy-start
  52.2 1.3 collective-permute-start.7
  53.5 5.0 %collective-permute-start.10 = (f32[1,4096]{1,0:T(1,128)S(1)}, f32[1,4096]{1,0:T(1,128)S(1)}, u32[]{:S(2)}, u32[]{:S(2)}) collective-permute-start(f32[1,4096]{1,0:T(1,128)S(1)} %add.9.c0), channel_id=1, source_target_pairs={{0,96},{16,112},{32,64},{48,80},{64,32},{80,48},{96,0},{112,16},{1... | collective-permute-start | bytes 49160 | tf_op jit(solution)/shard_map/ppermute | solution.py:227
  56.4 5.2 %collective-permute-start.9 = (f32[1,4096]{1,0:T(1,128)S(1)}, f32[1,4096]{1,0:T(1,128)S(1)}, u32[]{:S(2)}, u32[]{:S(2)}) collective-permute-start(f32[1,4096]{1,0:T(1,128)S(1)} %add.9.c0), channel_id=1, source_target_pairs={{0,64},{16,80},{32,96},{48,112},{64,0},{80,16},{96,32},{112,48},{1... | collective-permute-start | bytes 49160 | tf_op jit(solution)/shard_map/ppermute | solution.py:227
  57.2 4.5 %collective-permute-start.8 = (f32[1,4096]{1,0:T(1,128)S(1)}, f32[1,4096]{1,0:T(1,128)S(1)}, u32[]{:S(2)}, u32[]{:S(2)}) collective-permute-start(f32[1,4096]{1,0:T(1,128)S(1)} %add.9.c0), channel_id=1, source_target_pairs={{0,32},{16,48},{32,0},{48,16},{64,96},{80,112},{96,64},{112,80},{1... | collective-permute-start | bytes 49160 | tf_op jit(solution)/shard_map/ppermute | solution.py:227
  80.7 1.3 collective-permute-start.11
  82.0 12.4 %collective-permute-start.14 = (f32[1,4096]{1,0:T(1,128)S(1)}, f32[1,4096]{1,0:T(1,128)S(1)}, u32[]{:S(2)}, u32[]{:S(2)}) collective-permute-start(f32[1,4096]{1,0:T(1,128)S(1)} %add.10.c0), channel_id=1, source_target_pairs={{0,96},{16,112},{32,64},{48,80},{64,32},{80,48},{96,0},{112,16},{1... | collective-permute-start | bytes 49160 | tf_op jit(solution)/shard_map/ppermute | solution.py:227
  82.8 11.6 %collective-permute-start.13 = (f32[1,4096]{1,0:T(1,128)S(1)}, f32[1,4096]{1,0:T(1,128)S(1)}, u32[]{:S(2)}, u32[]{:S(2)}) collective-permute-start(f32[1,4096]{1,0:T(1,128)S(1)} %add.10.c0), channel_id=1, source_target_pairs={{0,64},{16,80},{32,96},{48,112},{64,0},{80,16},{96,32},{112,48},{1... | collective-permute-start | bytes 49160 | tf_op jit(solution)/shard_map/ppermute | solution.py:227
  84.2 10.3 %collective-permute-start.12 = (f32[1,4096]{1,0:T(1,128)S(1)}, f32[1,4096]{1,0:T(1,128)S(1)}, u32[]{:S(2)}, u32[]{:S(2)}) collective-permute-start(f32[1,4096]{1,0:T(1,128)S(1)} %add.10.c0), channel_id=1, source_target_pairs={{0,32},{16,48},{32,0},{48,16},{64,96},{80,112},{96,64},{112,80},{1... | collective-permute-start | bytes 49160 | tf_op jit(solution)/shard_map/ppermute | solution.py:227
  113.1 1.3 collective-permute-start.15
  114.3 5.1 %collective-permute-start.18 = (f32[1,4096]{1,0:T(1,128)S(1)}, f32[1,4096]{1,0:T(1,128)S(1)}, u32[]{:S(2)}, u32[]{:S(2)}) collective-permute-start(f32[1,4096]{1,0:T(1,128)S(1)} %add.11.c0), channel_id=1, source_target_pairs={{0,96},{16,112},{32,64},{48,80},{64,32},{80,48},{96,0},{112,16},{1... | collective-permute-start | bytes 49160 | tf_op jit(solution)/shard_map/ppermute | solution.py:227
  115.2 5.2 %collective-permute-start.17 = (f32[1,4096]{1,0:T(1,128)S(1)}, f32[1,4096]{1,0:T(1,128)S(1)}, u32[]{:S(2)}, u32[]{:S(2)}) collective-permute-start(f32[1,4096]{1,0:T(1,128)S(1)} %add.11.c0), channel_id=1, source_target_pairs={{0,64},{16,80},{32,96},{48,112},{64,0},{80,16},{96,32},{112,48},{1... | collective-permute-start | bytes 49160 | tf_op jit(solution)/shard_map/ppermute | solution.py:227
  116.5 3.9 %collective-permute-start.16 = (f32[1,4096]{1,0:T(1,128)S(1)}, f32[1,4096]{1,0:T(1,128)S(1)}, u32[]{:S(2)}, u32[]{:S(2)}) collective-permute-start(f32[1,4096]{1,0:T(1,128)S(1)} %add.11.c0), channel_id=1, source_target_pairs={{0,32},{16,48},{32,0},{48,16},{64,96},{80,112},{96,64},{112,80},{1... | collective-permute-start | bytes 49160 | tf_op jit(solution)/shard_map/ppermute | solution.py:227
  153.9 3.8 %collective-permute-start.19 = (bf16[4,512,256]{2,1,0:T(8,128)(2,1)}, bf16[4,512,256]{2,1,0:T(8,128)(2,1)S(1)}, u32[]{:S(2)}, u32[]{:S(2)}) collective-permute-start(bf16[4,512,256]{2,1,0:T(8,128)(2,1)} %get-tuple-element.31), channel_id=1, source_target_pairs={{0,16},{16,0},{32,48},{48,32},{64,80},{80,64},{96,112},{112,96},{1... | collective-permute-start | bytes 3145736 | tf_op jit(solution)/shard_map/ppermute | solution.py:227
  154.0 23.5 %all-to-all-start.4 = ((bf16[16,128,256]{2,1,0:T(8,128)(2,1)}), bf16[16,128,256]{2,1,0:T(8,128)(2,1)S(1)}, u32[]{:S(2)}, u32[]{:S(2)}) async-start(bf16[16,128,256]{2,1,0:T(8,128)(2,1)} %get-tuple-element.29), calls=%async_computation.4 | async-start | bytes 2097152 | tf_op jit(solution)/shard_map/all_to_all | solution.py:321
  160.1 17.4 %collective-permute-start.20 = (bf16[512,256]{1,0:T(8,128)(2,1)S(1)}, bf16[512,256]{1,0:T(8,128)(2,1)S(1)}, u32[]{:S(2)}, u32[]{:S(2)}) collective-permute-start(bf16[512,256]{1,0:T(8,128)(2,1)S(1)} %get-tuple-element.32), channel_id=1, source_target_pairs={{0,32},{16,48},{32,0},{48,16},{64,96},{80,112},{96,64},{112,80},{1... | collective-permute-start | bytes 786440 | tf_op jit(solution)/shard_map/ppermute | solution.py:227
  161.9 15.6 %collective-permute-start.21 = (bf16[512,256]{1,0:T(8,128)(2,1)S(1)}, bf16[512,256]{1,0:T(8,128)(2,1)S(1)}, u32[]{:S(2)}, u32[]{:S(2)}) collective-permute-start(bf16[512,256]{1,0:T(8,128)(2,1)S(1)} %get-tuple-element.33), channel_id=1, source_target_pairs={{0,64},{16,80},{32,96},{48,112},{64,0},{80,16},{96,32},{112,48},{1... | collective-permute-start | bytes 786440 | tf_op jit(solution)/shard_map/ppermute | solution.py:227
  164.1 15.0 %collective-permute-start.22 = (bf16[512,256]{1,0:T(8,128)(2,1)S(1)}, bf16[512,256]{1,0:T(8,128)(2,1)S(1)}, u32[]{:S(2)}, u32[]{:S(2)}) collective-permute-start(bf16[512,256]{1,0:T(8,128)(2,1)S(1)} %get-tuple-element.34), channel_id=1, source_target_pairs={{0,96},{16,112},{32,64},{48,80},{64,32},{80,48},{96,0},{112,16},{1... | collective-permute-start | bytes 786440 | tf_op jit(solution)/shard_map/ppermute | solution.py:227

commit v4 on v3

--- a/solution.py
+++ b/solution.py
@@ -274,9 +274,10 @@
             z = call(
                 total_kernel,
                 "student_total",
-                hbm((1, rows), F32),
+                vmem((1, rows), F32),
                 [feats, *pieces],
                 halves + [lanes],
+                limit=12,
                 raw=range(nb + 1),
             )
         extra = [z] if iteration == 1 else []
@@ -287,7 +288,7 @@
             [me, e, *cs, *extra],
             [lanes],
             smem=1,
-            keep=(0, 1, 2, 3, 4),
+            keep=(0, 1, 2, 3, 4, *([5] if extra else [])),
         )
         sums = lax.all_to_all(r, "proto", 0, 0)
         if extra:

time: 182 us -> 181 us (level)
  no operation moved by 1% of the time
where the time goes in v4:
time: 181 us; the launch traced here: 180 us
  Pallas kernels  57.9 us (32%)
  waiting for transfers between devices  50.5 us (28%)
  blocking collectives  35.4 us (20%)
  starting transfers between devices  34.2 us (19%)
    pallas_call x11, Pallas kernels, call(): pl.pallas_call(kernel, out_shape=out_shape, in_specs=[SM] * smem + [whole...  57.9 us
    ppermute x23, waiting for transfers between devices, shards(): lax.ppermute(x, 'batch', [(i, i ^ k) for i in range(nb)])  35.8 us
    all_to_all x3, blocking collectives, shards(): sums = lax.all_to_all(r, 'proto', 0, 0)  35.4 us
    ppermute x23, starting transfers between devices, shards(): lax.ppermute(x, 'batch', [(i, i ^ k) for i in range(nb)])  22.2 us
    all_to_all x1, waiting for transfers between devices, shards(): f, *got = lax.optimization_barrier((lax.all_to_all(f, 'proto', 0, 0), *got))  12.7 us
    all_to_all x1, starting transfers between devices, shards(): feats = lax.all_to_all(feats, 'proto', 0, 0).reshape(rows, 2 * dim)  8.26 us
    all_to_all x1, starting transfers between devices, shards(): f, *got = lax.optimization_barrier((lax.all_to_all(f, 'proto', 0, 0), *got))  3.66 us
  transfers between devices with their start and end apart: 25, of which 15 were waited for; matrix products, arithmetic and copies ran while one was open for 0% of the time, Pallas kernels for 6%

profile of v4, /device:TPU:0, one launch (start us, length us, event | category | flops | bytes accessed | tf_op | source)
XLA Modules:
  0.0 180.2 jit_solution(14896056964702860566)
XLA Ops:
  0.6 3.0 %unit_rows.1 = (bf16[16,128,512]{2,1,0:T(8,128)(2,1)}, bf16[512,512]{1,0:T(8,128)(2,1)}) custom-call(bf16[128,256]{1,0:T(8,128)(2,1)} %tf.1, bf16[128,256]{1,0:T(8,128)(2,1)} %sf.3, bf16[512,256]{1,0:T(8,128)(2,1)} %tp.1, bf16[512,256]{1,0:T(8,128)(2,1)} %sp.3), custom_call_target="tpu_custom_call" | custom-call | tf_op jit(solution)/shard_map/unit_rows/pallas_call | solution.py:215
  3.6 8.3 %all-to-all-start = ((bf16[16,128,512]{2,1,0:T(8,128)(2,1)}), bf16[16,128,512]{2,1,0:T(8,128)(2,1)S(1)}, u32[]{:S(2)}, u32[]{:S(2)}) async-start(bf16[16,128,512]{2,1,0:T(8,128)(2,1)} %get-tuple-element.21), calls=%async_computation | async-start | bytes 4194304 | tf_op jit(solution)/shard_map/all_to_all | solution.py:244
  11.9 2.8 %collective-permute-start.5 = (bf16[512,512]{1,0:T(8,128)(2,1)S(1)}, bf16[512,512]{1,0:T(8,128)(2,1)S(1)}, u32[]{:S(2)}, u32[]{:S(2)}) collective-permute-start(bf16[512,512]{1,0:T(8,128)(2,1)S(1)} %copy-done.1), channel_id=1, source_target_pairs={{0,96},{16,112},{32,64},{48,80},{64,32},{80,48},{96,0},{112,16},{1... | collective-permute-start | bytes 1572872 | tf_op jit(solution)/shard_map/ppermute | solution.py:227
  14.7 0.8 collective-permute-start.3
  15.5 0.5 collective-permute-start.1
  16.1 0.0 collective-permute-start
  16.1 21.7 %collective-permute-done.5.refs_6_ = bf16[512,512]{1,0:T(8,128)(2,1)S(1)} collective-permute-done((bf16[512,512]{1,0:T(8,128)(2,1)S(1)}, bf16[512,512]{1,0:T(8,128)(2,1)S(1)}, u32[]{:S(2)}, u32[]{:S(2)}) %collective-permute-start.5) | collective-permute-done | bytes 524320 | tf_op jit(solution)/shard_map/ppermute | solution.py:227
  37.8 0.0 collective-permute-start.6
  37.8 0.0 collective-permute-done.3.refs_4_
  37.8 0.5 collective-permute-start.4
  38.3 0.2 collective-permute-done.1.refs_2_
  38.5 0.0 collective-permute-start.2
  38.5 0.0 collective-permute-done.refs_1_
  38.5 1.3 collective-permute-done.6.refs_7_
  39.8 1.0 collective-permute-done.4.refs_5_
  40.8 0.7 collective-permute-done.2.refs_3_
  41.5 2.0 %all-to-all-done = bf16[16,128,512]{2,1,0:T(8,128)(2,1)S(1)} async-done(((bf16[16,128,512]{2,1,0:T(8,128)(2,1)}), bf16[16,128,512]{2,1,0:T(8,128)(2,1)S(1)}, u32[]{:S(2)}, u32[]{:S(2)}) %all-to-all-start) | async-done | bytes 2097184 | tf_op jit(solution)/shard_map/all_to_all | solution.py:244
  43.5 1.3 copy-done
  44.9 7.4 %teacher_exp.1 = (f32[2048,4096]{1,0:T(8,128)S(1)}, f32[1,4096]{1,0:T(1,128)S(1)}) custom-call(s32[1]{0:T(128)} %bitcast.me, bf16[2048,512]{1,0:T(8,128)(2,1)} %bitcast.2, bf16[512,512]{1,0:T(8,128)(2,1)} %get-tuple-element.22.refs_0_, bf16[512,512]{1,0:T(8,128)(2,1)} %collective-permute-done.refs_1_, bf16[512,512]{1,0:T(8,128)(2,1)} %collective-permute-done.1.refs_2_, ...), custom_call_target="tpu_custom_call" | custom-call | tf_op jit(solution)/shard_map/teacher_exp/pallas_call | solution.py:215
  52.2 0.1 collective-permute-start.7
  52.3 1.2 collective-permute-done.7
  53.5 2.8 %collective-permute-start.10 = (f32[1,4096]{1,0:T(1,128)S(1)}, f32[1,4096]{1,0:T(1,128)S(1)}, u32[]{:S(2)}, u32[]{:S(2)}) collective-permute-start(f32[1,4096]{1,0:T(1,128)S(1)} %add.9.c0), channel_id=1, source_target_pairs={{0,96},{16,112},{32,64},{48,80},{64,32},{80,48},{96,0},{112,16},{1... | collective-permute-start | bytes 49160 | tf_op jit(solution)/shard_map/ppermute | solution.py:227
  56.4 0.8 collective-permute-start.9
  57.2 0.5 collective-permute-start.8
  57.7 0.9 collective-permute-done.10.c3
  58.6 3.0 %collective-permute-done.9.c2 = f32[1,4096]{1,0:T(1,128)S(1)} collective-permute-done((f32[1,4096]{1,0:T(1,128)S(1)}, f32[1,4096]{1,0:T(1,128)S(1)}, u32[]{:S(2)}, u32[]{:S(2)}) %collective-permute-start.9) | collective-permute-done | bytes 16416 | tf_op jit(solution)/shard_map/ppermute | solution.py:227
  61.6 0.0 collective-permute-done.8.c1
  61.6 3.2 %row_sums.3 = (f32[16,1,2048]{2,1,0:T(1,128)S(1)}, f32[1,4096]{1,0:T(1,128)}) custom-call(s32[1]{0:T(128)} %bitcast.me, f32[2048,4096]{1,0:T(8,128)S(1)} %get-tuple-element.23.e, f32[1,4096]{1,0:T(1,128)S(1)} %add.9.c0, f32[1,4096]{1,0:T(1,128)S(1)} %collective-permute-done.8.c1, f32[1,4096]{1,0:T(1,128)S(1)} %collective-permute-done.9.c2, ...), custom_call_target="tpu_custom_call" | custom-call | tf_op jit(solution)/shard_map/row_sums/pallas_call | solution.py:215
  64.8 12.7 %all_to_all.25.sums = f32[16,1,2048]{2,1,0:T(1,128)S(1)} all-to-all(f32[16,1,2048]{2,1,0:T(1,128)S(1)} %get-tuple-element.25), channel_id=1, replica_groups=mesh['batch'=8,'proto'=16] {'proto'}, dimensions={0} | all-to-all | bytes 262144 | tf_op jit(solution)/shard_map/all_to_all | solution.py:293
  77.6 3.1 %column_sums.2 = f32[1,4096]{1,0:T(1,128)S(1)} custom-call(s32[1]{0:T(128)} %bitcast.me, f32[2048,4096]{1,0:T(8,128)S(1)} %get-tuple-element.23.e, f32[16,1,2048]{2,1,0:T(1,128)S(1)} %all_to_all.25.sums), custom_call_target="tpu_custom_call" | custom-call | tf_op jit(solution)/shard_map/column_sums/pallas_call | solution.py:215
  80.7 0.1 collective-permute-start.11
  80.8 1.2 collective-permute-done.11
  82.0 0.8 collective-permute-start.14
  82.8 1.4 collective-permute-start.13
  84.2 2.0 %collective-permute-start.12 = (f32[1,4096]{1,0:T(1,128)S(1)}, f32[1,4096]{1,0:T(1,128)S(1)}, u32[]{:S(2)}, u32[]{:S(2)}) collective-permute-start(f32[1,4096]{1,0:T(1,128)S(1)} %add.10.c0), channel_id=1, source_target_pairs={{0,32},{16,48},{32,0},{48,16},{64,96},{80,112},{96,64},{112,80},{1... | collective-permute-start | bytes 49160 | tf_op jit(solution)/shard_map/ppermute | solution.py:227
  86.1 7.7 %student_total.1.refs_0_ = f32[1,2048]{1,0:T(1,128)S(1)} custom-call(bf16[2048,512]{1,0:T(8,128)(2,1)} %bitcast.3, bf16[512,512]{1,0:T(8,128)(2,1)} %get-tuple-element.22.refs_0_, bf16[512,512]{1,0:T(8,128)(2,1)} %collective-permute-done.refs_1_, bf16[512,512]{1,0:T(8,128)(2,1)} %collective-permute-done.1.refs_2_, ...), custom_call_target="tpu_custom_call" | custom-call | tf_op jit(solution)/shard_map/student_total/pallas_call | solution.py:215
  93.8 0.0 collective-permute-done.14.c3
  93.8 0.0 collective-permute-done.13.c2
  93.8 0.0 collective-permute-done.12.c1
  93.8 3.1 %row_sums.4 = (f32[16,2,2048]{2,1,0:T(2,128)S(1)}, f32[1,4096]{1,0:T(1,128)}) custom-call(s32[1]{0:T(128)} %bitcast.me, f32[2048,4096]{1,0:T(8,128)S(1)} %get-tuple-element.23.e, f32[1,4096]{1,0:T(1,128)S(1)} %add.10.c0, f32[1,4096]{1,0:T(1,128)S(1)} %collective-permute-done.12.c1, f32[1,4096]{1,0:T(1,128)S(1)} %collective-permute-done.13.c2, ...), custom_call_target="tpu_custom_call" | custom-call | tf_op jit(solution)/shard_map/row_sums/pallas_call | solution.py:215
  96.9 11.8 %all_to_all.26.sums.zsums = f32[16,2,2048]{2,1,0:T(2,128)S(1)} all-to-all(f32[16,2,2048]{2,1,0:T(2,128)S(1)} %get-tuple-element.26), channel_id=1, replica_groups=mesh['batch'=8,'proto'=16] {'proto'}, dimensions={0} | all-to-all | bytes 524288 | tf_op jit(solution)/shard_map/all_to_all | solution.py:293
  108.7 3.1 %column_sums.3 = f32[1,4096]{1,0:T(1,128)S(1)} custom-call(s32[1]{0:T(128)} %bitcast.me, f32[2048,4096]{1,0:T(8,128)S(1)} %get-tuple-element.23.e, f32[16,2,2048]{2,1,0:T(2,128)S(1)} %all_to_all.26.sums.zsums), custom_call_target="tpu_custom_call" | custom-call | tf_op jit(solution)/shard_map/column_sums/pallas_call | solution.py:215
  111.8 0.1 collective-permute-start.15
  111.9 1.2 collective-permute-done.15
  113.1 0.8 collective-permute-start.18
  113.9 1.4 collective-permute-start.17
  115.2 2.0 %collective-permute-start.16 = (f32[1,4096]{1,0:T(1,128)S(1)}, f32[1,4096]{1,0:T(1,128)S(1)}, u32[]{:S(2)}, u32[]{:S(2)}) collective-permute-start(f32[1,4096]{1,0:T(1,128)S(1)} %add.11.c0), channel_id=1, source_target_pairs={{0,32},{16,48},{32,0},{48,16},{64,96},{80,112},{96,64},{112,80},{1... | collective-permute-start | bytes 49160 | tf_op jit(solution)/shard_map/ppermute | solution.py:227
  117.2 1.0 collective-permute-done.18.c3
  118.2 0.9 collective-permute-done.17.c2
  119.1 0.0 collective-permute-done.16.c1
  119.1 3.0 %row_sums.5 = (f32[16,1,2048]{2,1,0:T(1,128)S(1)}, f32[1,4096]{1,0:T(1,128)S(1)}) custom-call(s32[1]{0:T(128)} %bitcast.me, f32[2048,4096]{1,0:T(8,128)S(1)} %get-tuple-element.23.e, f32[1,4096]{1,0:T(1,128)S(1)} %add.11.c0, f32[1,4096]{1,0:T(1,128)S(1)} %collective-permute-done.16.c1, f32[1,4096]{1,0:T(1,128)S(1)} %collective-permute-done.17.c2, ...), custom_call_target="tpu_custom_call" | custom-call | tf_op jit(solution)/shard_map/row_sums/pallas_call | solution.py:215
  122.1 10.9 %all_to_all.27.sums = f32[16,1,2048]{2,1,0:T(1,128)S(1)} all-to-all(f32[16,1,2048]{2,1,0:T(1,128)S(1)} %get-tuple-element.28), channel_id=1, replica_groups=mesh['batch'=8,'proto'=16] {'proto'}, dimensions={0} | all-to-all | bytes 262144 | tf_op jit(solution)/shard_map/all_to_all | solution.py:293
  133.0 19.6 %logit_grad.1 = (bf16[16,128,256]{2,1,0:T(8,128)(2,1)}, f32[4,512,256]{2,1,0:T(8,128)}, bf16[4,512,256]{2,1,0:T(8,128)(2,1)}) custom-call(f32[2048,4096]{1,0:T(8,128)S(1)} %get-tuple-element.23.e, bf16[2048,512]{1,0:T(8,128)(2,1)} %bitcast.4, f32[1,4096]{1,0:T(1,128)S(1)} %get-tuple-element.27.b, f32[16,1,2048]{2,1,0:T(1,128)S(1)} %all_to_all.27.sums, ...), custom_call_target="tpu_custom_call" | custom-call | tf_op jit(solution)/shard_map/logit_grad/pallas_call | solution.py:215
  152.6 0.1 collective-permute-start.19
  152.7 3.7 %all-to-all-start.4 = ((bf16[16,128,256]{2,1,0:T(8,128)(2,1)}), bf16[16,128,256]{2,1,0:T(8,128)(2,1)S(1)}, u32[]{:S(2)}, u32[]{:S(2)}) async-start(bf16[16,128,256]{2,1,0:T(8,128)(2,1)} %get-tuple-element.29), calls=%async_computation.4 | async-start | bytes 2097152 | tf_op jit(solution)/shard_map/all_to_all | solution.py:322
  156.4 0.0 collective-permute-done.19.got
  156.4 2.4 %merge_cores.1 = (f32[512,256]{1,0:T(8,128)}, bf16[512,256]{1,0:T(8,128)(2,1)S(1)}, bf16[512,256]{1,0:T(8,128)(2,1)S(1)}, bf16[512,256]{1,0:T(8,128)(2,1)S(1)}) custom-call(f32[4,512,256]{2,1,0:T(8,128)} %get-tuple-element.30.keep, bf16[4,512,256]{2,1,0:T(8,128)(2,1)S(1)} %collective-permute-done.19.got), custom_call_target="tpu_custom_call" | custom-call | tf_op jit(solution)/shard_map/merge_cores/pallas_call | solution.py:215
  158.8 1.9 %collective-permute-start.20 = (bf16[512,256]{1,0:T(8,128)(2,1)S(1)}, bf16[512,256]{1,0:T(8,128)(2,1)S(1)}, u32[]{:S(2)}, u32[]{:S(2)}) collective-permute-start(bf16[512,256]{1,0:T(8,128)(2,1)S(1)} %get-tuple-element.32), channel_id=1, source_target_pairs={{0,32},{16,48},{32,0},{48,16},{64,96},{80,112},{96,64},{112,80},{1... | collective-permute-start | bytes 786440 | tf_op jit(solution)/shard_map/ppermute | solution.py:227
  160.7 2.1 %collective-permute-start.21 = (bf16[512,256]{1,0:T(8,128)(2,1)S(1)}, bf16[512,256]{1,0:T(8,128)(2,1)S(1)}, u32[]{:S(2)}, u32[]{:S(2)}) collective-permute-start(bf16[512,256]{1,0:T(8,128)(2,1)S(1)} %get-tuple-element.33), channel_id=1, source_target_pairs={{0,64},{16,80},{32,96},{48,112},{64,0},{80,16},{96,32},{112,48},{1... | collective-permute-start | bytes 786440 | tf_op jit(solution)/shard_map/ppermute | solution.py:227
  162.8 0.7 collective-permute-start.22
  163.5 12.7 %all-to-all-done.4.f = bf16[16,128,256]{2,1,0:T(8,128)(2,1)S(1)} async-done(((bf16[16,128,256]{2,1,0:T(8,128)(2,1)}), bf16[16,128,256]{2,1,0:T(8,128)(2,1)S(1)}, u32[]{:S(2)}, u32[]{:S(2)}) %all-to-all-start.4) | async-done | bytes 1048608 | tf_op jit(solution)/shard_map/all_to_all | solution.py:322
  176.2 0.0 collective-permute-done.20.refs_0_
  176.2 1.5 collective-permute-done.22.refs_2_
  177.7 2.4 %project_back.1 = (f32[128,256]{1,0:T(8,128)}, f32[512,256]{1,0:T(8,128)}) custom-call(bf16[16,128,256]{2,1,0:T(8,128)(2,1)S(1)} %all-to-all-done.4.f, bf16[128,256]{1,0:T(8,128)(2,1)} %sf.3, bf16[512,256]{1,0:T(8,128)(2,1)} %sp.3, f32[512,256]{1,0:T(8,128)} %get-tuple-element.36.half, bf16[512,256]{1,0:T(8,128)(2,1)S(1)} %collective-permute-done.20.refs_0_, ...), custom_call_target="tpu_custom_call" | custom-call | tf_op jit(solution)/shard_map/project_back/pallas_call | solution.py:215
  (9 shorter events, 0.1 us)
Async XLA Ops:
  3.6 8.3 %copy-start.1 = (bf16[512,512]{1,0:T(8,128)(2,1)S(1)}, bf16[512,512]{1,0:T(8,128)(2,1)}, u32[]{:S(2)}) copy-start(bf16[512,512]{1,0:T(8,128)(2,1)} %get-tuple-element.22.refs_0_) | copy-start | bytes 1572868
  3.6 39.9 %all-to-all-start = ((bf16[16,128,512]{2,1,0:T(8,128)(2,1)}), bf16[16,128,512]{2,1,0:T(8,128)(2,1)S(1)}, u32[]{:S(2)}, u32[]{:S(2)}) async-start(bf16[16,128,512]{2,1,0:T(8,128)(2,1)} %get-tuple-element.21), calls=%async_computation | async-start | bytes 4194304 | tf_op jit(solution)/shard_map/all_to_all | solution.py:244
  11.9 25.9 %collective-permute-start.5 = (bf16[512,512]{1,0:T(8,128)(2,1)S(1)}, bf16[512,512]{1,0:T(8,128)(2,1)S(1)}, u32[]{:S(2)}, u32[]{:S(2)}) collective-permute-start(bf16[512,512]{1,0:T(8,128)(2,1)S(1)} %copy-done.1), channel_id=1, source_target_pairs={{0,96},{16,112},{32,64},{48,80},{64,32},{80,48},{96,0},{112,16},{1... | collective-permute-start | bytes 1572872 | tf_op jit(solution)/shard_map/ppermute | solution.py:227
  14.7 23.1 %collective-permute-start.3 = (bf16[512,512]{1,0:T(8,128)(2,1)S(1)}, bf16[512,512]{1,0:T(8,128)(2,1)}, u32[]{:S(2)}, u32[]{:S(2)}) collective-permute-start(bf16[512,512]{1,0:T(8,128)(2,1)S(1)} %copy-done.1), channel_id=1, source_target_pairs={{0,64},{16,80},{32,96},{48,112},{64,0},{80,16},{96,32},{112,48},{1... | collective-permute-start | bytes 1572872 | tf_op jit(solution)/shard_map/ppermute | solution.py:227
  15.5 23.0 %collective-permute-start.1 = (bf16[512,512]{1,0:T(8,128)(2,1)S(1)}, bf16[512,512]{1,0:T(8,128)(2,1)}, u32[]{:S(2)}, u32[]{:S(2)}) collective-permute-start(bf16[512,512]{1,0:T(8,128)(2,1)S(1)} %copy-done.1), channel_id=1, source_target_pairs={{0,32},{16,48},{32,0},{48,16},{64,96},{80,112},{96,64},{112,80},{1... | collective-permute-start | bytes 1572872 | tf_op jit(solution)/shard_map/ppermute | solution.py:227
  16.1 22.5 %collective-permute-start = (bf16[512,512]{1,0:T(8,128)(2,1)S(1)}, bf16[512,512]{1,0:T(8,128)(2,1)}, u32[]{:S(2)}, u32[]{:S(2)}) collective-permute-start(bf16[512,512]{1,0:T(8,128)(2,1)S(1)} %copy-done.1), channel_id=1, source_target_pairs={{0,16},{16,0},{32,48},{48,32},{64,80},{80,64},{96,112},{112,96},{1... | collective-permute-start | bytes 1572872 | tf_op jit(solution)/shard_map/ppermute | solution.py:227
  37.8 5.7 %copy-start.2 = (bf16[512,512]{1,0:T(8,128)(2,1)}, bf16[512,512]{1,0:T(8,128)(2,1)S(1)}, u32[]{:S(2)}) copy-start(bf16[512,512]{1,0:T(8,128)(2,1)S(1)} %collective-permute-done.5.refs_6_) | copy-start | bytes 1572868
  37.8 2.0 %collective-permute-start.6 = (bf16[512,512]{1,0:T(8,128)(2,1)S(1)}, bf16[512,512]{1,0:T(8,128)(2,1)}, u32[]{:S(2)}, u32[]{:S(2)}) collective-permute-start(bf16[512,512]{1,0:T(8,128)(2,1)S(1)} %collective-permute-done.5.refs_6_), channel_id=1, source_target_pairs={{0,16},{16,0},{32,48},{48,32},{64,80},{80,64},{96,112},{112,96},{1... | collective-permute-start | bytes 1572872 | tf_op jit(solution)/shard_map/ppermute | solution.py:227
  37.8 3.0 %collective-permute-start.4 = (bf16[512,512]{1,0:T(8,128)(2,1)}, bf16[512,512]{1,0:T(8,128)(2,1)}, u32[]{:S(2)}, u32[]{:S(2)}) collective-permute-start(bf16[512,512]{1,0:T(8,128)(2,1)} %collective-permute-done.3.refs_4_), channel_id=1, source_target_pairs={{0,16},{16,0},{32,48},{48,32},{64,80},{80,64},{96,112},{112,96},{1... | collective-permute-start | bytes 1572872 | tf_op jit(solution)/shard_map/ppermute | solution.py:227
  38.5 3.0 %collective-permute-start.2 = (bf16[512,512]{1,0:T(8,128)(2,1)}, bf16[512,512]{1,0:T(8,128)(2,1)}, u32[]{:S(2)}, u32[]{:S(2)}) collective-permute-start(bf16[512,512]{1,0:T(8,128)(2,1)} %collective-permute-done.1.refs_2_), channel_id=1, source_target_pairs={{0,16},{16,0},{32,48},{48,32},{64,80},{80,64},{96,112},{112,96},{1... | collective-permute-start | bytes 1572872 | tf_op jit(solution)/shard_map/ppermute | solution.py:227
  43.5 1.3 copy-start
  52.2 1.3 collective-permute-start.7
  53.5 5.0 %collective-permute-start.10 = (f32[1,4096]{1,0:T(1,128)S(1)}, f32[1,4096]{1,0:T(1,128)S(1)}, u32[]{:S(2)}, u32[]{:S(2)}) collective-permute-start(f32[1,4096]{1,0:T(1,128)S(1)} %add.9.c0), channel_id=1, source_target_pairs={{0,96},{16,112},{32,64},{48,80},{64,32},{80,48},{96,0},{112,16},{1... | collective-permute-start | bytes 49160 | tf_op jit(solution)/shard_map/ppermute | solution.py:227
  56.4 5.2 %collective-permute-start.9 = (f32[1,4096]{1,0:T(1,128)S(1)}, f32[1,4096]{1,0:T(1,128)S(1)}, u32[]{:S(2)}, u32[]{:S(2)}) collective-permute-start(f32[1,4096]{1,0:T(1,128)S(1)} %add.9.c0), channel_id=1, source_target_pairs={{0,64},{16,80},{32,96},{48,112},{64,0},{80,16},{96,32},{112,48},{1... | collective-permute-start | bytes 49160 | tf_op jit(solution)/shard_map/ppermute | solution.py:227
  57.2 4.5 %collective-permute-start.8 = (f32[1,4096]{1,0:T(1,128)S(1)}, f32[1,4096]{1,0:T(1,128)S(1)}, u32[]{:S(2)}, u32[]{:S(2)}) collective-permute-start(f32[1,4096]{1,0:T(1,128)S(1)} %add.9.c0), channel_id=1, source_target_pairs={{0,32},{16,48},{32,0},{48,16},{64,96},{80,112},{96,64},{112,80},{1... | collective-permute-start | bytes 49160 | tf_op jit(solution)/shard_map/ppermute | solution.py:227
  80.7 1.3 collective-permute-start.11
  82.0 11.8 %collective-permute-start.14 = (f32[1,4096]{1,0:T(1,128)S(1)}, f32[1,4096]{1,0:T(1,128)S(1)}, u32[]{:S(2)}, u32[]{:S(2)}) collective-permute-start(f32[1,4096]{1,0:T(1,128)S(1)} %add.10.c0), channel_id=1, source_target_pairs={{0,96},{16,112},{32,64},{48,80},{64,32},{80,48},{96,0},{112,16},{1... | collective-permute-start | bytes 49160 | tf_op jit(solution)/shard_map/ppermute | solution.py:227
  82.8 11.0 %collective-permute-start.13 = (f32[1,4096]{1,0:T(1,128)S(1)}, f32[1,4096]{1,0:T(1,128)S(1)}, u32[]{:S(2)}, u32[]{:S(2)}) collective-permute-start(f32[1,4096]{1,0:T(1,128)S(1)} %add.10.c0), channel_id=1, source_target_pairs={{0,64},{16,80},{32,96},{48,112},{64,0},{80,16},{96,32},{112,48},{1... | collective-permute-start | bytes 49160 | tf_op jit(solution)/shard_map/ppermute | solution.py:227
  84.2 9.7 %collective-permute-start.12 = (f32[1,4096]{1,0:T(1,128)S(1)}, f32[1,4096]{1,0:T(1,128)S(1)}, u32[]{:S(2)}, u32[]{:S(2)}) collective-permute-start(f32[1,4096]{1,0:T(1,128)S(1)} %add.10.c0), channel_id=1, source_target_pairs={{0,32},{16,48},{32,0},{48,16},{64,96},{80,112},{96,64},{112,80},{1... | collective-permute-start | bytes 49160 | tf_op jit(solution)/shard_map/ppermute | solution.py:227
  111.8 1.3 collective-permute-start.15
  113.1 5.1 %collective-permute-start.18 = (f32[1,4096]{1,0:T(1,128)S(1)}, f32[1,4096]{1,0:T(1,128)S(1)}, u32[]{:S(2)}, u32[]{:S(2)}) collective-permute-start(f32[1,4096]{1,0:T(1,128)S(1)} %add.11.c0), channel_id=1, source_target_pairs={{0,96},{16,112},{32,64},{48,80},{64,32},{80,48},{96,0},{112,16},{1... | collective-permute-start | bytes 49160 | tf_op jit(solution)/shard_map/ppermute | solution.py:227
  113.9 5.2 %collective-permute-start.17 = (f32[1,4096]{1,0:T(1,128)S(1)}, f32[1,4096]{1,0:T(1,128)S(1)}, u32[]{:S(2)}, u32[]{:S(2)}) collective-permute-start(f32[1,4096]{1,0:T(1,128)S(1)} %add.11.c0), channel_id=1, source_target_pairs={{0,64},{16,80},{32,96},{48,112},{64,0},{80,16},{96,32},{112,48},{1... | collective-permute-start | bytes 49160 | tf_op jit(solution)/shard_map/ppermute | solution.py:227
  115.2 3.9 %collective-permute-start.16 = (f32[1,4096]{1,0:T(1,128)S(1)}, f32[1,4096]{1,0:T(1,128)S(1)}, u32[]{:S(2)}, u32[]{:S(2)}) collective-permute-start(f32[1,4096]{1,0:T(1,128)S(1)} %add.11.c0), channel_id=1, source_target_pairs={{0,32},{16,48},{32,0},{48,16},{64,96},{80,112},{96,64},{112,80},{1... | collective-permute-start | bytes 49160 | tf_op jit(solution)/shard_map/ppermute | solution.py:227
  152.6 3.8 %collective-permute-start.19 = (bf16[4,512,256]{2,1,0:T(8,128)(2,1)}, bf16[4,512,256]{2,1,0:T(8,128)(2,1)S(1)}, u32[]{:S(2)}, u32[]{:S(2)}) collective-permute-start(bf16[4,512,256]{2,1,0:T(8,128)(2,1)} %get-tuple-element.31), channel_id=1, source_target_pairs={{0,16},{16,0},{32,48},{48,32},{64,80},{80,64},{96,112},{112,96},{1... | collective-permute-start | bytes 3145736 | tf_op jit(solution)/shard_map/ppermute | solution.py:227
  152.7 23.5 %all-to-all-start.4 = ((bf16[16,128,256]{2,1,0:T(8,128)(2,1)}), bf16[16,128,256]{2,1,0:T(8,128)(2,1)S(1)}, u32[]{:S(2)}, u32[]{:S(2)}) async-start(bf16[16,128,256]{2,1,0:T(8,128)(2,1)} %get-tuple-element.29), calls=%async_computation.4 | async-start | bytes 2097152 | tf_op jit(solution)/shard_map/all_to_all | solution.py:322
  158.8 17.4 %collective-permute-start.20 = (bf16[512,256]{1,0:T(8,128)(2,1)S(1)}, bf16[512,256]{1,0:T(8,128)(2,1)S(1)}, u32[]{:S(2)}, u32[]{:S(2)}) collective-permute-start(bf16[512,256]{1,0:T(8,128)(2,1)S(1)} %get-tuple-element.32), channel_id=1, source_target_pairs={{0,32},{16,48},{32,0},{48,16},{64,96},{80,112},{96,64},{112,80},{1... | collective-permute-start | bytes 786440 | tf_op jit(solution)/shard_map/ppermute | solution.py:227
  160.7 15.6 %collective-permute-start.21 = (bf16[512,256]{1,0:T(8,128)(2,1)S(1)}, bf16[512,256]{1,0:T(8,128)(2,1)S(1)}, u32[]{:S(2)}, u32[]{:S(2)}) collective-permute-start(bf16[512,256]{1,0:T(8,128)(2,1)S(1)} %get-tuple-element.33), channel_id=1, source_target_pairs={{0,64},{16,80},{32,96},{48,112},{64,0},{80,16},{96,32},{112,48},{1... | collective-permute-start | bytes 786440 | tf_op jit(solution)/shard_map/ppermute | solution.py:227
  162.8 15.0 %collective-permute-start.22 = (bf16[512,256]{1,0:T(8,128)(2,1)S(1)}, bf16[512,256]{1,0:T(8,128)(2,1)S(1)}, u32[]{:S(2)}, u32[]{:S(2)}) collective-permute-start(bf16[512,256]{1,0:T(8,128)(2,1)S(1)} %get-tuple-element.34), channel_id=1, source_target_pairs={{0,96},{16,112},{32,64},{48,80},{64,32},{80,48},{96,0},{112,16},{1... | collective-permute-start | bytes 786440 | tf_op jit(solution)/shard_map/ppermute | solution.py:227

commit v5 on v4

--- a/solution.py
+++ b/solution.py
@@ -282,7 +282,7 @@
             )
         extra = [z] if iteration == 1 else []
         r, b = call(
-            functools.partial(row_kernel, 128, own),
+            functools.partial(row_kernel, 256, own),
             "row_sums",
             [vmem((npr, 1 + len(extra), rows), F32), all_cols],
             [me, e, *cs, *extra],

time: 181 us -> 180 us (level)
  no operation moved by 1% of the time
where the time goes in v5:
time: 180 us; the launch traced here: 179 us
  Pallas kernels  57.1 us (32%)
  waiting for transfers between devices  50.5 us (28%)
  blocking collectives  35.4 us (20%)
  starting transfers between devices  34.2 us (19%)
    pallas_call x11, Pallas kernels, call(): pl.pallas_call(kernel, out_shape=out_shape, in_specs=[SM] * smem + [whole...  57.1 us
    ppermute x23, waiting for transfers between devices, shards(): lax.ppermute(x, 'batch', [(i, i ^ k) for i in range(nb)])  35.8 us
    all_to_all x3, blocking collectives, shards(): sums = lax.all_to_all(r, 'proto', 0, 0)  35.4 us
    ppermute x23, starting transfers between devices, shards(): lax.ppermute(x, 'batch', [(i, i ^ k) for i in range(nb)])  22.2 us
    all_to_all x1, waiting for transfers between devices, shards(): f, *got = lax.optimization_barrier((lax.all_to_all(f, 'proto', 0, 0), *got))  12.7 us
    all_to_all x1, starting transfers between devices, shards(): feats = lax.all_to_all(feats, 'proto', 0, 0).reshape(rows, 2 * dim)  8.26 us
    all_to_all x1, starting transfers between devices, shards(): f, *got = lax.optimization_barrier((lax.all_to_all(f, 'proto', 0, 0), *got))  3.66 us
  transfers between devices with their start and end apart: 25, of which 15 were waited for; matrix products, arithmetic and copies ran while one was open for 0% of the time, Pallas kernels for 6%

profile of v5, /device:TPU:0, one launch (start us, length us, event | category | flops | bytes accessed | tf_op | source)
XLA Modules:
  0.0 179.4 jit_solution(1979697424867541312)
XLA Ops:
  0.6 3.0 %unit_rows.1 = (bf16[16,128,512]{2,1,0:T(8,128)(2,1)}, bf16[512,512]{1,0:T(8,128)(2,1)}) custom-call(bf16[128,256]{1,0:T(8,128)(2,1)} %tf.1, bf16[128,256]{1,0:T(8,128)(2,1)} %sf.3, bf16[512,256]{1,0:T(8,128)(2,1)} %tp.1, bf16[512,256]{1,0:T(8,128)(2,1)} %sp.3), custom_call_target="tpu_custom_call" | custom-call | tf_op jit(solution)/shard_map/unit_rows/pallas_call | solution.py:215
  3.6 8.3 %all-to-all-start = ((bf16[16,128,512]{2,1,0:T(8,128)(2,1)}), bf16[16,128,512]{2,1,0:T(8,128)(2,1)S(1)}, u32[]{:S(2)}, u32[]{:S(2)}) async-start(bf16[16,128,512]{2,1,0:T(8,128)(2,1)} %get-tuple-element.21), calls=%async_computation | async-start | bytes 4194304 | tf_op jit(solution)/shard_map/all_to_all | solution.py:244
  11.9 2.8 %collective-permute-start.5 = (bf16[512,512]{1,0:T(8,128)(2,1)S(1)}, bf16[512,512]{1,0:T(8,128)(2,1)S(1)}, u32[]{:S(2)}, u32[]{:S(2)}) collective-permute-start(bf16[512,512]{1,0:T(8,128)(2,1)S(1)} %copy-done.1), channel_id=1, source_target_pairs={{0,96},{16,112},{32,64},{48,80},{64,32},{80,48},{96,0},{112,16},{1... | collective-permute-start | bytes 1572872 | tf_op jit(solution)/shard_map/ppermute | solution.py:227
  14.7 0.8 collective-permute-start.3
  15.5 0.5 collective-permute-start.1
  16.1 0.0 collective-permute-start
  16.1 21.7 %collective-permute-done.5.refs_6_ = bf16[512,512]{1,0:T(8,128)(2,1)S(1)} collective-permute-done((bf16[512,512]{1,0:T(8,128)(2,1)S(1)}, bf16[512,512]{1,0:T(8,128)(2,1)S(1)}, u32[]{:S(2)}, u32[]{:S(2)}) %collective-permute-start.5) | collective-permute-done | bytes 524320 | tf_op jit(solution)/shard_map/ppermute | solution.py:227
  37.8 0.0 collective-permute-start.6
  37.8 0.0 collective-permute-done.3.refs_4_
  37.8 0.5 collective-permute-start.4
  38.3 0.2 collective-permute-done.1.refs_2_
  38.5 0.0 collective-permute-start.2
  38.5 0.0 collective-permute-done.refs_1_
  38.5 1.3 collective-permute-done.6.refs_7_
  39.8 1.0 collective-permute-done.4.refs_5_
  40.8 0.7 collective-permute-done.2.refs_3_
  41.5 2.0 %all-to-all-done = bf16[16,128,512]{2,1,0:T(8,128)(2,1)S(1)} async-done(((bf16[16,128,512]{2,1,0:T(8,128)(2,1)}), bf16[16,128,512]{2,1,0:T(8,128)(2,1)S(1)}, u32[]{:S(2)}, u32[]{:S(2)}) %all-to-all-start) | async-done | bytes 2097184 | tf_op jit(solution)/shard_map/all_to_all | solution.py:244
  43.5 1.3 copy-done
  44.9 7.4 %teacher_exp.1 = (f32[2048,4096]{1,0:T(8,128)S(1)}, f32[1,4096]{1,0:T(1,128)S(1)}) custom-call(s32[1]{0:T(128)} %bitcast.me, bf16[2048,512]{1,0:T(8,128)(2,1)} %bitcast.2, bf16[512,512]{1,0:T(8,128)(2,1)} %get-tuple-element.22.refs_0_, bf16[512,512]{1,0:T(8,128)(2,1)} %collective-permute-done.refs_1_, bf16[512,512]{1,0:T(8,128)(2,1)} %collective-permute-done.1.refs_2_, ...), custom_call_target="tpu_custom_call" | custom-call | tf_op jit(solution)/shard_map/teacher_exp/pallas_call | solution.py:215
  52.2 0.1 collective-permute-start.7
  52.3 1.2 collective-permute-done.7
  53.5 2.8 %collective-permute-start.10 = (f32[1,4096]{1,0:T(1,128)S(1)}, f32[1,4096]{1,0:T(1,128)S(1)}, u32[]{:S(2)}, u32[]{:S(2)}) collective-permute-start(f32[1,4096]{1,0:T(1,128)S(1)} %add.9.c0), channel_id=1, source_target_pairs={{0,96},{16,112},{32,64},{48,80},{64,32},{80,48},{96,0},{112,16},{1... | collective-permute-start | bytes 49160 | tf_op jit(solution)/shard_map/ppermute | solution.py:227
  56.4 0.8 collective-permute-start.9
  57.2 0.5 collective-permute-start.8
  57.7 0.9 collective-permute-done.10.c3
  58.6 3.0 %collective-permute-done.9.c2 = f32[1,4096]{1,0:T(1,128)S(1)} collective-permute-done((f32[1,4096]{1,0:T(1,128)S(1)}, f32[1,4096]{1,0:T(1,128)S(1)}, u32[]{:S(2)}, u32[]{:S(2)}) %collective-permute-start.9) | collective-permute-done | bytes 16416 | tf_op jit(solution)/shard_map/ppermute | solution.py:227
  61.6 0.0 collective-permute-done.8.c1
  61.6 3.0 %row_sums.3 = (f32[16,1,2048]{2,1,0:T(1,128)S(1)}, f32[1,4096]{1,0:T(1,128)}) custom-call(s32[1]{0:T(128)} %bitcast.me, f32[2048,4096]{1,0:T(8,128)S(1)} %get-tuple-element.23.e, f32[1,4096]{1,0:T(1,128)S(1)} %add.9.c0, f32[1,4096]{1,0:T(1,128)S(1)} %collective-permute-done.8.c1, f32[1,4096]{1,0:T(1,128)S(1)} %collective-permute-done.9.c2, ...), custom_call_target="tpu_custom_call" | custom-call | tf_op jit(solution)/shard_map/row_sums/pallas_call | solution.py:215
  64.6 12.7 %all_to_all.25.sums = f32[16,1,2048]{2,1,0:T(1,128)S(1)} all-to-all(f32[16,1,2048]{2,1,0:T(1,128)S(1)} %get-tuple-element.25), channel_id=1, replica_groups=mesh['batch'=8,'proto'=16] {'proto'}, dimensions={0} | all-to-all | bytes 262144 | tf_op jit(solution)/shard_map/all_to_all | solution.py:293
  77.3 3.1 %column_sums.2 = f32[1,4096]{1,0:T(1,128)S(1)} custom-call(s32[1]{0:T(128)} %bitcast.me, f32[2048,4096]{1,0:T(8,128)S(1)} %get-tuple-element.23.e, f32[16,1,2048]{2,1,0:T(1,128)S(1)} %all_to_all.25.sums), custom_call_target="tpu_custom_call" | custom-call | tf_op jit(solution)/shard_map/column_sums/pallas_call | solution.py:215
  80.5 0.1 collective-permute-start.11
  80.5 1.2 collective-permute-done.11
  81.7 0.8 collective-permute-start.14
  82.6 1.4 collective-permute-start.13
  83.9 2.0 %collective-permute-start.12 = (f32[1,4096]{1,0:T(1,128)S(1)}, f32[1,4096]{1,0:T(1,128)S(1)}, u32[]{:S(2)}, u32[]{:S(2)}) collective-permute-start(f32[1,4096]{1,0:T(1,128)S(1)} %add.10.c0), channel_id=1, source_target_pairs={{0,32},{16,48},{32,0},{48,16},{64,96},{80,112},{96,64},{112,80},{1... | collective-permute-start | bytes 49160 | tf_op jit(solution)/shard_map/ppermute | solution.py:227
  85.9 7.7 %student_total.1.refs_0_ = f32[1,2048]{1,0:T(1,128)S(1)} custom-call(bf16[2048,512]{1,0:T(8,128)(2,1)} %bitcast.3, bf16[512,512]{1,0:T(8,128)(2,1)} %get-tuple-element.22.refs_0_, bf16[512,512]{1,0:T(8,128)(2,1)} %collective-permute-done.refs_1_, bf16[512,512]{1,0:T(8,128)(2,1)} %collective-permute-done.1.refs_2_, ...), custom_call_target="tpu_custom_call" | custom-call | tf_op jit(solution)/shard_map/student_total/pallas_call | solution.py:215
  93.6 0.0 collective-permute-done.14.c3
  93.6 0.0 collective-permute-done.13.c2
  93.6 0.0 collective-permute-done.12.c1
  93.6 2.8 %row_sums.4 = (f32[16,2,2048]{2,1,0:T(2,128)S(1)}, f32[1,4096]{1,0:T(1,128)}) custom-call(s32[1]{0:T(128)} %bitcast.me, f32[2048,4096]{1,0:T(8,128)S(1)} %get-tuple-element.23.e, f32[1,4096]{1,0:T(1,128)S(1)} %add.10.c0, f32[1,4096]{1,0:T(1,128)S(1)} %collective-permute-done.12.c1, f32[1,4096]{1,0:T(1,128)S(1)} %collective-permute-done.13.c2, ...), custom_call_target="tpu_custom_call" | custom-call | tf_op jit(solution)/shard_map/row_sums/pallas_call | solution.py:215
  96.4 11.8 %all_to_all.26.sums.zsums = f32[16,2,2048]{2,1,0:T(2,128)S(1)} all-to-all(f32[16,2,2048]{2,1,0:T(2,128)S(1)} %get-tuple-element.26), channel_id=1, replica_groups=mesh['batch'=8,'proto'=16] {'proto'}, dimensions={0} | all-to-all | bytes 524288 | tf_op jit(solution)/shard_map/all_to_all | solution.py:293
  108.1 3.1 %column_sums.3 = f32[1,4096]{1,0:T(1,128)S(1)} custom-call(s32[1]{0:T(128)} %bitcast.me, f32[2048,4096]{1,0:T(8,128)S(1)} %get-tuple-element.23.e, f32[16,2,2048]{2,1,0:T(2,128)S(1)} %all_to_all.26.sums.zsums), custom_call_target="tpu_custom_call" | custom-call | tf_op jit(solution)/shard_map/column_sums/pallas_call | solution.py:215
  111.2 0.1 collective-permute-start.15
  111.3 1.2 collective-permute-done.15
  112.5 0.8 collective-permute-start.18
  113.3 1.4 collective-permute-start.17
  114.7 2.0 %collective-permute-start.16 = (f32[1,4096]{1,0:T(1,128)S(1)}, f32[1,4096]{1,0:T(1,128)S(1)}, u32[]{:S(2)}, u32[]{:S(2)}) collective-permute-start(f32[1,4096]{1,0:T(1,128)S(1)} %add.11.c0), channel_id=1, source_target_pairs={{0,32},{16,48},{32,0},{48,16},{64,96},{80,112},{96,64},{112,80},{1... | collective-permute-start | bytes 49160 | tf_op jit(solution)/shard_map/ppermute | solution.py:227
  116.7 1.0 collective-permute-done.18.c3
  117.7 0.9 collective-permute-done.17.c2
  118.6 0.0 collective-permute-done.16.c1
  118.6 2.7 %row_sums.5 = (f32[16,1,2048]{2,1,0:T(1,128)S(1)}, f32[1,4096]{1,0:T(1,128)S(1)}) custom-call(s32[1]{0:T(128)} %bitcast.me, f32[2048,4096]{1,0:T(8,128)S(1)} %get-tuple-element.23.e, f32[1,4096]{1,0:T(1,128)S(1)} %add.11.c0, f32[1,4096]{1,0:T(1,128)S(1)} %collective-permute-done.16.c1, f32[1,4096]{1,0:T(1,128)S(1)} %collective-permute-done.17.c2, ...), custom_call_target="tpu_custom_call" | custom-call | tf_op jit(solution)/shard_map/row_sums/pallas_call | solution.py:215
  121.3 10.9 %all_to_all.27.sums = f32[16,1,2048]{2,1,0:T(1,128)S(1)} all-to-all(f32[16,1,2048]{2,1,0:T(1,128)S(1)} %get-tuple-element.28), channel_id=1, replica_groups=mesh['batch'=8,'proto'=16] {'proto'}, dimensions={0} | all-to-all | bytes 262144 | tf_op jit(solution)/shard_map/all_to_all | solution.py:293
  132.2 19.6 %logit_grad.1 = (bf16[16,128,256]{2,1,0:T(8,128)(2,1)}, f32[4,512,256]{2,1,0:T(8,128)}, bf16[4,512,256]{2,1,0:T(8,128)(2,1)}) custom-call(f32[2048,4096]{1,0:T(8,128)S(1)} %get-tuple-element.23.e, bf16[2048,512]{1,0:T(8,128)(2,1)} %bitcast.4, f32[1,4096]{1,0:T(1,128)S(1)} %get-tuple-element.27.b, f32[16,1,2048]{2,1,0:T(1,128)S(1)} %all_to_all.27.sums, ...), custom_call_target="tpu_custom_call" | custom-call | tf_op jit(solution)/shard_map/logit_grad/pallas_call | solution.py:215
  151.8 0.1 collective-permute-start.19
  151.9 3.7 %all-to-all-start.4 = ((bf16[16,128,256]{2,1,0:T(8,128)(2,1)}), bf16[16,128,256]{2,1,0:T(8,128)(2,1)S(1)}, u32[]{:S(2)}, u32[]{:S(2)}) async-start(bf16[16,128,256]{2,1,0:T(8,128)(2,1)} %get-tuple-element.29), calls=%async_computation.4 | async-start | bytes 2097152 | tf_op jit(solution)/shard_map/all_to_all | solution.py:322
  155.6 0.0 collective-permute-done.19.got
  155.6 2.4 %merge_cores.1 = (f32[512,256]{1,0:T(8,128)}, bf16[512,256]{1,0:T(8,128)(2,1)S(1)}, bf16[512,256]{1,0:T(8,128)(2,1)S(1)}, bf16[512,256]{1,0:T(8,128)(2,1)S(1)}) custom-call(f32[4,512,256]{2,1,0:T(8,128)} %get-tuple-element.30.keep, bf16[4,512,256]{2,1,0:T(8,128)(2,1)S(1)} %collective-permute-done.19.got), custom_call_target="tpu_custom_call" | custom-call | tf_op jit(solution)/shard_map/merge_cores/pallas_call | solution.py:215
  158.0 1.9 %collective-permute-start.20 = (bf16[512,256]{1,0:T(8,128)(2,1)S(1)}, bf16[512,256]{1,0:T(8,128)(2,1)S(1)}, u32[]{:S(2)}, u32[]{:S(2)}) collective-permute-start(bf16[512,256]{1,0:T(8,128)(2,1)S(1)} %get-tuple-element.32), channel_id=1, source_target_pairs={{0,32},{16,48},{32,0},{48,16},{64,96},{80,112},{96,64},{112,80},{1... | collective-permute-start | bytes 786440 | tf_op jit(solution)/shard_map/ppermute | solution.py:227
  159.9 2.1 %collective-permute-start.21 = (bf16[512,256]{1,0:T(8,128)(2,1)S(1)}, bf16[512,256]{1,0:T(8,128)(2,1)S(1)}, u32[]{:S(2)}, u32[]{:S(2)}) collective-permute-start(bf16[512,256]{1,0:T(8,128)(2,1)S(1)} %get-tuple-element.33), channel_id=1, source_target_pairs={{0,64},{16,80},{32,96},{48,112},{64,0},{80,16},{96,32},{112,48},{1... | collective-permute-start | bytes 786440 | tf_op jit(solution)/shard_map/ppermute | solution.py:227
  162.0 0.7 collective-permute-start.22
  162.7 12.7 %all-to-all-done.4.f = bf16[16,128,256]{2,1,0:T(8,128)(2,1)S(1)} async-done(((bf16[16,128,256]{2,1,0:T(8,128)(2,1)}), bf16[16,128,256]{2,1,0:T(8,128)(2,1)S(1)}, u32[]{:S(2)}, u32[]{:S(2)}) %all-to-all-start.4) | async-done | bytes 1048608 | tf_op jit(solution)/shard_map/all_to_all | solution.py:322
  175.4 0.0 collective-permute-done.20.refs_0_
  175.5 1.5 collective-permute-done.22.refs_2_
  177.0 2.4 %project_back.1 = (f32[128,256]{1,0:T(8,128)}, f32[512,256]{1,0:T(8,128)}) custom-call(bf16[16,128,256]{2,1,0:T(8,128)(2,1)S(1)} %all-to-all-done.4.f, bf16[128,256]{1,0:T(8,128)(2,1)} %sf.3, bf16[512,256]{1,0:T(8,128)(2,1)} %sp.3, f32[512,256]{1,0:T(8,128)} %get-tuple-element.36.half, bf16[512,256]{1,0:T(8,128)(2,1)S(1)} %collective-permute-done.20.refs_0_, ...), custom_call_target="tpu_custom_call" | custom-call | tf_op jit(solution)/shard_map/project_back/pallas_call | solution.py:215
  (9 shorter events, 0.1 us)
Async XLA Ops:
  3.6 8.3 %copy-start.1 = (bf16[512,512]{1,0:T(8,128)(2,1)S(1)}, bf16[512,512]{1,0:T(8,128)(2,1)}, u32[]{:S(2)}) copy-start(bf16[512,512]{1,0:T(8,128)(2,1)} %get-tuple-element.22.refs_0_) | copy-start | bytes 1572868
  3.6 39.9 %all-to-all-start = ((bf16[16,128,512]{2,1,0:T(8,128)(2,1)}), bf16[16,128,512]{2,1,0:T(8,128)(2,1)S(1)}, u32[]{:S(2)}, u32[]{:S(2)}) async-start(bf16[16,128,512]{2,1,0:T(8,128)(2,1)} %get-tuple-element.21), calls=%async_computation | async-start | bytes 4194304 | tf_op jit(solution)/shard_map/all_to_all | solution.py:244
  11.9 25.9 %collective-permute-start.5 = (bf16[512,512]{1,0:T(8,128)(2,1)S(1)}, bf16[512,512]{1,0:T(8,128)(2,1)S(1)}, u32[]{:S(2)}, u32[]{:S(2)}) collective-permute-start(bf16[512,512]{1,0:T(8,128)(2,1)S(1)} %copy-done.1), channel_id=1, source_target_pairs={{0,96},{16,112},{32,64},{48,80},{64,32},{80,48},{96,0},{112,16},{1... | collective-permute-start | bytes 1572872 | tf_op jit(solution)/shard_map/ppermute | solution.py:227
  14.7 23.1 %collective-permute-start.3 = (bf16[512,512]{1,0:T(8,128)(2,1)S(1)}, bf16[512,512]{1,0:T(8,128)(2,1)}, u32[]{:S(2)}, u32[]{:S(2)}) collective-permute-start(bf16[512,512]{1,0:T(8,128)(2,1)S(1)} %copy-done.1), channel_id=1, source_target_pairs={{0,64},{16,80},{32,96},{48,112},{64,0},{80,16},{96,32},{112,48},{1... | collective-permute-start | bytes 1572872 | tf_op jit(solution)/shard_map/ppermute | solution.py:227
  15.5 23.0 %collective-permute-start.1 = (bf16[512,512]{1,0:T(8,128)(2,1)S(1)}, bf16[512,512]{1,0:T(8,128)(2,1)}, u32[]{:S(2)}, u32[]{:S(2)}) collective-permute-start(bf16[512,512]{1,0:T(8,128)(2,1)S(1)} %copy-done.1), channel_id=1, source_target_pairs={{0,32},{16,48},{32,0},{48,16},{64,96},{80,112},{96,64},{112,80},{1... | collective-permute-start | bytes 1572872 | tf_op jit(solution)/shard_map/ppermute | solution.py:227
  16.1 22.5 %collective-permute-start = (bf16[512,512]{1,0:T(8,128)(2,1)S(1)}, bf16[512,512]{1,0:T(8,128)(2,1)}, u32[]{:S(2)}, u32[]{:S(2)}) collective-permute-start(bf16[512,512]{1,0:T(8,128)(2,1)S(1)} %copy-done.1), channel_id=1, source_target_pairs={{0,16},{16,0},{32,48},{48,32},{64,80},{80,64},{96,112},{112,96},{1... | collective-permute-start | bytes 1572872 | tf_op jit(solution)/shard_map/ppermute | solution.py:227
  37.8 5.7 %copy-start.2 = (bf16[512,512]{1,0:T(8,128)(2,1)}, bf16[512,512]{1,0:T(8,128)(2,1)S(1)}, u32[]{:S(2)}) copy-start(bf16[512,512]{1,0:T(8,128)(2,1)S(1)} %collective-permute-done.5.refs_6_) | copy-start | bytes 1572868
  37.8 2.0 %collective-permute-start.6 = (bf16[512,512]{1,0:T(8,128)(2,1)S(1)}, bf16[512,512]{1,0:T(8,128)(2,1)}, u32[]{:S(2)}, u32[]{:S(2)}) collective-permute-start(bf16[512,512]{1,0:T(8,128)(2,1)S(1)} %collective-permute-done.5.refs_6_), channel_id=1, source_target_pairs={{0,16},{16,0},{32,48},{48,32},{64,80},{80,64},{96,112},{112,96},{1... | collective-permute-start | bytes 1572872 | tf_op jit(solution)/shard_map/ppermute | solution.py:227
  37.8 3.0 %collective-permute-start.4 = (bf16[512,512]{1,0:T(8,128)(2,1)}, bf16[512,512]{1,0:T(8,128)(2,1)}, u32[]{:S(2)}, u32[]{:S(2)}) collective-permute-start(bf16[512,512]{1,0:T(8,128)(2,1)} %collective-permute-done.3.refs_4_), channel_id=1, source_target_pairs={{0,16},{16,0},{32,48},{48,32},{64,80},{80,64},{96,112},{112,96},{1... | collective-permute-start | bytes 1572872 | tf_op jit(solution)/shard_map/ppermute | solution.py:227
  38.5 3.0 %collective-permute-start.2 = (bf16[512,512]{1,0:T(8,128)(2,1)}, bf16[512,512]{1,0:T(8,128)(2,1)}, u32[]{:S(2)}, u32[]{:S(2)}) collective-permute-start(bf16[512,512]{1,0:T(8,128)(2,1)} %collective-permute-done.1.refs_2_), channel_id=1, source_target_pairs={{0,16},{16,0},{32,48},{48,32},{64,80},{80,64},{96,112},{112,96},{1... | collective-permute-start | bytes 1572872 | tf_op jit(solution)/shard_map/ppermute | solution.py:227
  43.5 1.3 copy-start
  52.2 1.3 collective-permute-start.7
  53.5 5.0 %collective-permute-start.10 = (f32[1,4096]{1,0:T(1,128)S(1)}, f32[1,4096]{1,0:T(1,128)S(1)}, u32[]{:S(2)}, u32[]{:S(2)}) collective-permute-start(f32[1,4096]{1,0:T(1,128)S(1)} %add.9.c0), channel_id=1, source_target_pairs={{0,96},{16,112},{32,64},{48,80},{64,32},{80,48},{96,0},{112,16},{1... | collective-permute-start | bytes 49160 | tf_op jit(solution)/shard_map/ppermute | solution.py:227
  56.4 5.2 %collective-permute-start.9 = (f32[1,4096]{1,0:T(1,128)S(1)}, f32[1,4096]{1,0:T(1,128)S(1)}, u32[]{:S(2)}, u32[]{:S(2)}) collective-permute-start(f32[1,4096]{1,0:T(1,128)S(1)} %add.9.c0), channel_id=1, source_target_pairs={{0,64},{16,80},{32,96},{48,112},{64,0},{80,16},{96,32},{112,48},{1... | collective-permute-start | bytes 49160 | tf_op jit(solution)/shard_map/ppermute | solution.py:227
  57.2 4.5 %collective-permute-start.8 = (f32[1,4096]{1,0:T(1,128)S(1)}, f32[1,4096]{1,0:T(1,128)S(1)}, u32[]{:S(2)}, u32[]{:S(2)}) collective-permute-start(f32[1,4096]{1,0:T(1,128)S(1)} %add.9.c0), channel_id=1, source_target_pairs={{0,32},{16,48},{32,0},{48,16},{64,96},{80,112},{96,64},{112,80},{1... | collective-permute-start | bytes 49160 | tf_op jit(solution)/shard_map/ppermute | solution.py:227
  80.5 1.3 collective-permute-start.11
  81.7 11.8 %collective-permute-start.14 = (f32[1,4096]{1,0:T(1,128)S(1)}, f32[1,4096]{1,0:T(1,128)S(1)}, u32[]{:S(2)}, u32[]{:S(2)}) collective-permute-start(f32[1,4096]{1,0:T(1,128)S(1)} %add.10.c0), channel_id=1, source_target_pairs={{0,96},{16,112},{32,64},{48,80},{64,32},{80,48},{96,0},{112,16},{1... | collective-permute-start | bytes 49160 | tf_op jit(solution)/shard_map/ppermute | solution.py:227
  82.6 11.0 %collective-permute-start.13 = (f32[1,4096]{1,0:T(1,128)S(1)}, f32[1,4096]{1,0:T(1,128)S(1)}, u32[]{:S(2)}, u32[]{:S(2)}) collective-permute-start(f32[1,4096]{1,0:T(1,128)S(1)} %add.10.c0), channel_id=1, source_target_pairs={{0,64},{16,80},{32,96},{48,112},{64,0},{80,16},{96,32},{112,48},{1... | collective-permute-start | bytes 49160 | tf_op jit(solution)/shard_map/ppermute | solution.py:227
  83.9 9.7 %collective-permute-start.12 = (f32[1,4096]{1,0:T(1,128)S(1)}, f32[1,4096]{1,0:T(1,128)S(1)}, u32[]{:S(2)}, u32[]{:S(2)}) collective-permute-start(f32[1,4096]{1,0:T(1,128)S(1)} %add.10.c0), channel_id=1, source_target_pairs={{0,32},{16,48},{32,0},{48,16},{64,96},{80,112},{96,64},{112,80},{1... | collective-permute-start | bytes 49160 | tf_op jit(solution)/shard_map/ppermute | solution.py:227
  111.2 1.3 collective-permute-start.15
  112.5 5.1 %collective-permute-start.18 = (f32[1,4096]{1,0:T(1,128)S(1)}, f32[1,4096]{1,0:T(1,128)S(1)}, u32[]{:S(2)}, u32[]{:S(2)}) collective-permute-start(f32[1,4096]{1,0:T(1,128)S(1)} %add.11.c0), channel_id=1, source_target_pairs={{0,96},{16,112},{32,64},{48,80},{64,32},{80,48},{96,0},{112,16},{1... | collective-permute-start | bytes 49160 | tf_op jit(solution)/shard_map/ppermute | solution.py:227
  113.3 5.2 %collective-permute-start.17 = (f32[1,4096]{1,0:T(1,128)S(1)}, f32[1,4096]{1,0:T(1,128)S(1)}, u32[]{:S(2)}, u32[]{:S(2)}) collective-permute-start(f32[1,4096]{1,0:T(1,128)S(1)} %add.11.c0), channel_id=1, source_target_pairs={{0,64},{16,80},{32,96},{48,112},{64,0},{80,16},{96,32},{112,48},{1... | collective-permute-start | bytes 49160 | tf_op jit(solution)/shard_map/ppermute | solution.py:227
  114.7 3.9 %collective-permute-start.16 = (f32[1,4096]{1,0:T(1,128)S(1)}, f32[1,4096]{1,0:T(1,128)S(1)}, u32[]{:S(2)}, u32[]{:S(2)}) collective-permute-start(f32[1,4096]{1,0:T(1,128)S(1)} %add.11.c0), channel_id=1, source_target_pairs={{0,32},{16,48},{32,0},{48,16},{64,96},{80,112},{96,64},{112,80},{1... | collective-permute-start | bytes 49160 | tf_op jit(solution)/shard_map/ppermute | solution.py:227
  151.8 3.8 %collective-permute-start.19 = (bf16[4,512,256]{2,1,0:T(8,128)(2,1)}, bf16[4,512,256]{2,1,0:T(8,128)(2,1)S(1)}, u32[]{:S(2)}, u32[]{:S(2)}) collective-permute-start(bf16[4,512,256]{2,1,0:T(8,128)(2,1)} %get-tuple-element.31), channel_id=1, source_target_pairs={{0,16},{16,0},{32,48},{48,32},{64,80},{80,64},{96,112},{112,96},{1... | collective-permute-start | bytes 3145736 | tf_op jit(solution)/shard_map/ppermute | solution.py:227
  151.9 23.5 %all-to-all-start.4 = ((bf16[16,128,256]{2,1,0:T(8,128)(2,1)}), bf16[16,128,256]{2,1,0:T(8,128)(2,1)S(1)}, u32[]{:S(2)}, u32[]{:S(2)}) async-start(bf16[16,128,256]{2,1,0:T(8,128)(2,1)} %get-tuple-element.29), calls=%async_computation.4 | async-start | bytes 2097152 | tf_op jit(solution)/shard_map/all_to_all | solution.py:322
  158.0 17.4 %collective-permute-start.20 = (bf16[512,256]{1,0:T(8,128)(2,1)S(1)}, bf16[512,256]{1,0:T(8,128)(2,1)S(1)}, u32[]{:S(2)}, u32[]{:S(2)}) collective-permute-start(bf16[512,256]{1,0:T(8,128)(2,1)S(1)} %get-tuple-element.32), channel_id=1, source_target_pairs={{0,32},{16,48},{32,0},{48,16},{64,96},{80,112},{96,64},{112,80},{1... | collective-permute-start | bytes 786440 | tf_op jit(solution)/shard_map/ppermute | solution.py:227
  159.9 15.6 %collective-permute-start.21 = (bf16[512,256]{1,0:T(8,128)(2,1)S(1)}, bf16[512,256]{1,0:T(8,128)(2,1)S(1)}, u32[]{:S(2)}, u32[]{:S(2)}) collective-permute-start(bf16[512,256]{1,0:T(8,128)(2,1)S(1)} %get-tuple-element.33), channel_id=1, source_target_pairs={{0,64},{16,80},{32,96},{48,112},{64,0},{80,16},{96,32},{112,48},{1... | collective-permute-start | bytes 786440 | tf_op jit(solution)/shard_map/ppermute | solution.py:227
  162.0 15.0 %collective-permute-start.22 = (bf16[512,256]{1,0:T(8,128)(2,1)S(1)}, bf16[512,256]{1,0:T(8,128)(2,1)S(1)}, u32[]{:S(2)}, u32[]{:S(2)}) collective-permute-start(bf16[512,256]{1,0:T(8,128)(2,1)S(1)} %get-tuple-element.34), channel_id=1, source_target_pairs={{0,96},{16,112},{32,64},{48,80},{64,32},{80,48},{96,0},{112,16},{1... | collective-permute-start | bytes 786440 | tf_op jit(solution)/shard_map/ppermute | solution.py:227

commit v6 on v5

--- a/solution.py
+++ b/solution.py
@@ -260,7 +260,7 @@
     for iteration in range(ITERS):
         if iteration:
             c = call(
-                functools.partial(col_kernel, 128, 2048, own),
+                functools.partial(col_kernel, 256, 2048, own),
                 "column_sums",
                 all_cols,
                 [me, e, sums],

time: 180 us -> 180 us (level)
  transfers between devices with their start and end apart: 25 -> 25, of which waited for: 15 -> 16; matrix products, arithmetic and copies ran while one was open for 0% -> 0% of each run, Pallas kernels for 6% -> 6%
where the time goes in v6:
time: 180 us; the launch traced here: 179 us
  Pallas kernels  56.9 us (32%)
  waiting for transfers between devices  50.5 us (28%)
  blocking collectives  35.4 us (20%)
  starting transfers between devices  34.2 us (19%)
    pallas_call x11, Pallas kernels, call(): pl.pallas_call(kernel, out_shape=out_shape, in_specs=[SM] * smem + [whole...  56.9 us
    ppermute x23, waiting for transfers between devices, shards(): lax.ppermute(x, 'batch', [(i, i ^ k) for i in range(nb)])  35.8 us
    all_to_all x3, blocking collectives, shards(): sums = lax.all_to_all(r, 'proto', 0, 0)  35.4 us
    ppermute x23, starting transfers between devices, shards(): lax.ppermute(x, 'batch', [(i, i ^ k) for i in range(nb)])  22.2 us
    all_to_all x1, waiting for transfers between devices, shards(): f, *got = lax.optimization_barrier((lax.all_to_all(f, 'proto', 0, 0), *got))  12.7 us
    all_to_all x1, starting transfers between devices, shards(): feats = lax.all_to_all(feats, 'proto', 0, 0).reshape(rows, 2 * dim)  8.26 us
    all_to_all x1, starting transfers between devices, shards(): f, *got = lax.optimization_barrier((lax.all_to_all(f, 'proto', 0, 0), *got))  3.66 us
  transfers between devices with their start and end apart: 25, of which 16 were waited for; matrix products, arithmetic and copies ran while one was open for 0% of the time, Pallas kernels for 6%

profile of v6, /device:TPU:0, one launch (start us, length us, event | category | flops | bytes accessed | tf_op | source)
XLA Modules:
  0.0 179.2 jit_solution(18002957901807508570)
XLA Ops:
  0.6 3.0 %unit_rows.1 = (bf16[16,128,512]{2,1,0:T(8,128)(2,1)}, bf16[512,512]{1,0:T(8,128)(2,1)}) custom-call(bf16[128,256]{1,0:T(8,128)(2,1)} %tf.1, bf16[128,256]{1,0:T(8,128)(2,1)} %sf.3, bf16[512,256]{1,0:T(8,128)(2,1)} %tp.1, bf16[512,256]{1,0:T(8,128)(2,1)} %sp.3), custom_call_target="tpu_custom_call" | custom-call | tf_op jit(solution)/shard_map/unit_rows/pallas_call | solution.py:215
  3.6 8.3 %all-to-all-start = ((bf16[16,128,512]{2,1,0:T(8,128)(2,1)}), bf16[16,128,512]{2,1,0:T(8,128)(2,1)S(1)}, u32[]{:S(2)}, u32[]{:S(2)}) async-start(bf16[16,128,512]{2,1,0:T(8,128)(2,1)} %get-tuple-element.21), calls=%async_computation | async-start | bytes 4194304 | tf_op jit(solution)/shard_map/all_to_all | solution.py:244
  11.9 2.8 %collective-permute-start.5 = (bf16[512,512]{1,0:T(8,128)(2,1)S(1)}, bf16[512,512]{1,0:T(8,128)(2,1)S(1)}, u32[]{:S(2)}, u32[]{:S(2)}) collective-permute-start(bf16[512,512]{1,0:T(8,128)(2,1)S(1)} %copy-done.1), channel_id=1, source_target_pairs={{0,96},{16,112},{32,64},{48,80},{64,32},{80,48},{96,0},{112,16},{1... | collective-permute-start | bytes 1572872 | tf_op jit(solution)/shard_map/ppermute | solution.py:227
  14.7 0.8 collective-permute-start.3
  15.5 0.5 collective-permute-start.1
  16.1 0.0 collective-permute-start
  16.1 21.7 %collective-permute-done.5.refs_6_ = bf16[512,512]{1,0:T(8,128)(2,1)S(1)} collective-permute-done((bf16[512,512]{1,0:T(8,128)(2,1)S(1)}, bf16[512,512]{1,0:T(8,128)(2,1)S(1)}, u32[]{:S(2)}, u32[]{:S(2)}) %collective-permute-start.5) | collective-permute-done | bytes 524320 | tf_op jit(solution)/shard_map/ppermute | solution.py:227
  37.8 0.0 collective-permute-start.6
  37.8 0.0 collective-permute-done.3.refs_4_
  37.8 0.5 collective-permute-start.4
  38.3 0.2 collective-permute-done.1.refs_2_
  38.5 0.0 collective-permute-start.2
  38.5 0.0 collective-permute-done.refs_1_
  38.5 1.3 collective-permute-done.6.refs_7_
  39.8 1.0 collective-permute-done.4.refs_5_
  40.8 0.7 collective-permute-done.2.refs_3_
  41.5 2.0 %all-to-all-done = bf16[16,128,512]{2,1,0:T(8,128)(2,1)S(1)} async-done(((bf16[16,128,512]{2,1,0:T(8,128)(2,1)}), bf16[16,128,512]{2,1,0:T(8,128)(2,1)S(1)}, u32[]{:S(2)}, u32[]{:S(2)}) %all-to-all-start) | async-done | bytes 2097184 | tf_op jit(solution)/shard_map/all_to_all | solution.py:244
  43.5 1.3 copy-done
  44.9 7.4 %teacher_exp.1 = (f32[2048,4096]{1,0:T(8,128)S(1)}, f32[1,4096]{1,0:T(1,128)S(1)}) custom-call(s32[1]{0:T(128)} %bitcast.me, bf16[2048,512]{1,0:T(8,128)(2,1)} %bitcast.2, bf16[512,512]{1,0:T(8,128)(2,1)} %get-tuple-element.22.refs_0_, bf16[512,512]{1,0:T(8,128)(2,1)} %collective-permute-done.refs_1_, bf16[512,512]{1,0:T(8,128)(2,1)} %collective-permute-done.1.refs_2_, ...), custom_call_target="tpu_custom_call" | custom-call | tf_op jit(solution)/shard_map/teacher_exp/pallas_call | solution.py:215
  52.2 0.1 collective-permute-start.7
  52.3 1.2 collective-permute-done.7
  53.5 2.8 %collective-permute-start.10 = (f32[1,4096]{1,0:T(1,128)S(1)}, f32[1,4096]{1,0:T(1,128)S(1)}, u32[]{:S(2)}, u32[]{:S(2)}) collective-permute-start(f32[1,4096]{1,0:T(1,128)S(1)} %add.9.c0), channel_id=1, source_target_pairs={{0,96},{16,112},{32,64},{48,80},{64,32},{80,48},{96,0},{112,16},{1... | collective-permute-start | bytes 49160 | tf_op jit(solution)/shard_map/ppermute | solution.py:227
  56.4 0.8 collective-permute-start.9
  57.2 0.5 collective-permute-start.8
  57.7 0.9 collective-permute-done.10.c3
  58.6 3.0 %collective-permute-done.9.c2 = f32[1,4096]{1,0:T(1,128)S(1)} collective-permute-done((f32[1,4096]{1,0:T(1,128)S(1)}, f32[1,4096]{1,0:T(1,128)S(1)}, u32[]{:S(2)}, u32[]{:S(2)}) %collective-permute-start.9) | collective-permute-done | bytes 16416 | tf_op jit(solution)/shard_map/ppermute | solution.py:227
  61.6 0.0 collective-permute-done.8.c1
  61.6 3.0 %row_sums.3 = (f32[16,1,2048]{2,1,0:T(1,128)S(1)}, f32[1,4096]{1,0:T(1,128)}) custom-call(s32[1]{0:T(128)} %bitcast.me, f32[2048,4096]{1,0:T(8,128)S(1)} %get-tuple-element.23.e, f32[1,4096]{1,0:T(1,128)S(1)} %add.9.c0, f32[1,4096]{1,0:T(1,128)S(1)} %collective-permute-done.8.c1, f32[1,4096]{1,0:T(1,128)S(1)} %collective-permute-done.9.c2, ...), custom_call_target="tpu_custom_call" | custom-call | tf_op jit(solution)/shard_map/row_sums/pallas_call | solution.py:215
  64.6 12.7 %all_to_all.25.sums = f32[16,1,2048]{2,1,0:T(1,128)S(1)} all-to-all(f32[16,1,2048]{2,1,0:T(1,128)S(1)} %get-tuple-element.25), channel_id=1, replica_groups=mesh['batch'=8,'proto'=16] {'proto'}, dimensions={0} | all-to-all | bytes 262144 | tf_op jit(solution)/shard_map/all_to_all | solution.py:293
  77.3 3.0 %column_sums.2 = f32[1,4096]{1,0:T(1,128)S(1)} custom-call(s32[1]{0:T(128)} %bitcast.me, f32[2048,4096]{1,0:T(8,128)S(1)} %get-tuple-element.23.e, f32[16,1,2048]{2,1,0:T(1,128)S(1)} %all_to_all.25.sums), custom_call_target="tpu_custom_call" | custom-call | tf_op jit(solution)/shard_map/column_sums/pallas_call | solution.py:215
  80.3 0.1 collective-permute-start.11
  80.4 1.2 collective-permute-done.11
  81.6 0.8 collective-permute-start.14
  82.4 1.4 collective-permute-start.13
  83.8 2.0 %collective-permute-start.12 = (f32[1,4096]{1,0:T(1,128)S(1)}, f32[1,4096]{1,0:T(1,128)S(1)}, u32[]{:S(2)}, u32[]{:S(2)}) collective-permute-start(f32[1,4096]{1,0:T(1,128)S(1)} %add.10.c0), channel_id=1, source_target_pairs={{0,32},{16,48},{32,0},{48,16},{64,96},{80,112},{96,64},{112,80},{1... | collective-permute-start | bytes 49160 | tf_op jit(solution)/shard_map/ppermute | solution.py:227
  85.8 7.6 %student_total.1.refs_0_ = f32[1,2048]{1,0:T(1,128)S(1)} custom-call(bf16[2048,512]{1,0:T(8,128)(2,1)} %bitcast.3, bf16[512,512]{1,0:T(8,128)(2,1)} %get-tuple-element.22.refs_0_, bf16[512,512]{1,0:T(8,128)(2,1)} %collective-permute-done.refs_1_, bf16[512,512]{1,0:T(8,128)(2,1)} %collective-permute-done.1.refs_2_, ...), custom_call_target="tpu_custom_call" | custom-call | tf_op jit(solution)/shard_map/student_total/pallas_call | solution.py:215
  93.4 0.0 collective-permute-done.14.c3
  93.5 0.0 collective-permute-done.13.c2
  93.5 0.0 collective-permute-done.12.c1
  93.5 2.8 %row_sums.4 = (f32[16,2,2048]{2,1,0:T(2,128)S(1)}, f32[1,4096]{1,0:T(1,128)}) custom-call(s32[1]{0:T(128)} %bitcast.me, f32[2048,4096]{1,0:T(8,128)S(1)} %get-tuple-element.23.e, f32[1,4096]{1,0:T(1,128)S(1)} %add.10.c0, f32[1,4096]{1,0:T(1,128)S(1)} %collective-permute-done.12.c1, f32[1,4096]{1,0:T(1,128)S(1)} %collective-permute-done.13.c2, ...), custom_call_target="tpu_custom_call" | custom-call | tf_op jit(solution)/shard_map/row_sums/pallas_call | solution.py:215
  96.2 11.8 %all_to_all.26.sums.zsums = f32[16,2,2048]{2,1,0:T(2,128)S(1)} all-to-all(f32[16,2,2048]{2,1,0:T(2,128)S(1)} %get-tuple-element.26), channel_id=1, replica_groups=mesh['batch'=8,'proto'=16] {'proto'}, dimensions={0} | all-to-all | bytes 524288 | tf_op jit(solution)/shard_map/all_to_all | solution.py:293
  108.0 3.0 %column_sums.3 = f32[1,4096]{1,0:T(1,128)S(1)} custom-call(s32[1]{0:T(128)} %bitcast.me, f32[2048,4096]{1,0:T(8,128)S(1)} %get-tuple-element.23.e, f32[16,2,2048]{2,1,0:T(2,128)S(1)} %all_to_all.26.sums.zsums), custom_call_target="tpu_custom_call" | custom-call | tf_op jit(solution)/shard_map/column_sums/pallas_call | solution.py:215
  111.0 0.1 collective-permute-start.15
  111.1 1.2 collective-permute-done.15
  112.3 0.8 collective-permute-start.18
  113.0 1.4 collective-permute-start.17
  114.5 2.0 %collective-permute-start.16 = (f32[1,4096]{1,0:T(1,128)S(1)}, f32[1,4096]{1,0:T(1,128)S(1)}, u32[]{:S(2)}, u32[]{:S(2)}) collective-permute-start(f32[1,4096]{1,0:T(1,128)S(1)} %add.11.c0), channel_id=1, source_target_pairs={{0,32},{16,48},{32,0},{48,16},{64,96},{80,112},{96,64},{112,80},{1... | collective-permute-start | bytes 49160 | tf_op jit(solution)/shard_map/ppermute | solution.py:227
  116.4 0.9 collective-permute-done.18.c3
  117.4 0.9 collective-permute-done.17.c2
  118.3 0.1 collective-permute-done.16.c1
  118.3 2.7 %row_sums.5 = (f32[16,1,2048]{2,1,0:T(1,128)S(1)}, f32[1,4096]{1,0:T(1,128)S(1)}) custom-call(s32[1]{0:T(128)} %bitcast.me, f32[2048,4096]{1,0:T(8,128)S(1)} %get-tuple-element.23.e, f32[1,4096]{1,0:T(1,128)S(1)} %add.11.c0, f32[1,4096]{1,0:T(1,128)S(1)} %collective-permute-done.16.c1, f32[1,4096]{1,0:T(1,128)S(1)} %collective-permute-done.17.c2, ...), custom_call_target="tpu_custom_call" | custom-call | tf_op jit(solution)/shard_map/row_sums/pallas_call | solution.py:215
  121.1 10.9 %all_to_all.27.sums = f32[16,1,2048]{2,1,0:T(1,128)S(1)} all-to-all(f32[16,1,2048]{2,1,0:T(1,128)S(1)} %get-tuple-element.28), channel_id=1, replica_groups=mesh['batch'=8,'proto'=16] {'proto'}, dimensions={0} | all-to-all | bytes 262144 | tf_op jit(solution)/shard_map/all_to_all | solution.py:293
  132.0 19.6 %logit_grad.1 = (bf16[16,128,256]{2,1,0:T(8,128)(2,1)}, f32[4,512,256]{2,1,0:T(8,128)}, bf16[4,512,256]{2,1,0:T(8,128)(2,1)}) custom-call(f32[2048,4096]{1,0:T(8,128)S(1)} %get-tuple-element.23.e, bf16[2048,512]{1,0:T(8,128)(2,1)} %bitcast.4, f32[1,4096]{1,0:T(1,128)S(1)} %get-tuple-element.27.b, f32[16,1,2048]{2,1,0:T(1,128)S(1)} %all_to_all.27.sums, ...), custom_call_target="tpu_custom_call" | custom-call | tf_op jit(solution)/shard_map/logit_grad/pallas_call | solution.py:215
  151.6 0.1 collective-permute-start.19
  151.7 3.7 %all-to-all-start.4 = ((bf16[16,128,256]{2,1,0:T(8,128)(2,1)}), bf16[16,128,256]{2,1,0:T(8,128)(2,1)S(1)}, u32[]{:S(2)}, u32[]{:S(2)}) async-start(bf16[16,128,256]{2,1,0:T(8,128)(2,1)} %get-tuple-element.29), calls=%async_computation.4 | async-start | bytes 2097152 | tf_op jit(solution)/shard_map/all_to_all | solution.py:322
  155.4 2.4 %merge_cores.1 = (f32[512,256]{1,0:T(8,128)}, bf16[512,256]{1,0:T(8,128)(2,1)S(1)}, bf16[512,256]{1,0:T(8,128)(2,1)S(1)}, bf16[512,256]{1,0:T(8,128)(2,1)S(1)}) custom-call(f32[4,512,256]{2,1,0:T(8,128)} %get-tuple-element.30.keep, bf16[4,512,256]{2,1,0:T(8,128)(2,1)S(1)} %collective-permute-done.19.got), custom_call_target="tpu_custom_call" | custom-call | tf_op jit(solution)/shard_map/merge_cores/pallas_call | solution.py:215
  157.8 1.8 %collective-permute-start.20 = (bf16[512,256]{1,0:T(8,128)(2,1)S(1)}, bf16[512,256]{1,0:T(8,128)(2,1)S(1)}, u32[]{:S(2)}, u32[]{:S(2)}) collective-permute-start(bf16[512,256]{1,0:T(8,128)(2,1)S(1)} %get-tuple-element.32), channel_id=1, source_target_pairs={{0,32},{16,48},{32,0},{48,16},{64,96},{80,112},{96,64},{112,80},{1... | collective-permute-start | bytes 786440 | tf_op jit(solution)/shard_map/ppermute | solution.py:227
  159.6 2.1 %collective-permute-start.21 = (bf16[512,256]{1,0:T(8,128)(2,1)S(1)}, bf16[512,256]{1,0:T(8,128)(2,1)S(1)}, u32[]{:S(2)}, u32[]{:S(2)}) collective-permute-start(bf16[512,256]{1,0:T(8,128)(2,1)S(1)} %get-tuple-element.33), channel_id=1, source_target_pairs={{0,64},{16,80},{32,96},{48,112},{64,0},{80,16},{96,32},{112,48},{1... | collective-permute-start | bytes 786440 | tf_op jit(solution)/shard_map/ppermute | solution.py:227
  161.8 0.7 collective-permute-start.22
  162.5 12.7 %all-to-all-done.4.f = bf16[16,128,256]{2,1,0:T(8,128)(2,1)S(1)} async-done(((bf16[16,128,256]{2,1,0:T(8,128)(2,1)}), bf16[16,128,256]{2,1,0:T(8,128)(2,1)S(1)}, u32[]{:S(2)}, u32[]{:S(2)}) %all-to-all-start.4) | async-done | bytes 1048608 | tf_op jit(solution)/shard_map/all_to_all | solution.py:322
  175.2 0.0 collective-permute-done.20.refs_0_
  175.2 0.0 collective-permute-done.21.refs_1_
  175.2 1.5 collective-permute-done.22.refs_2_
  176.7 2.4 %project_back.1 = (f32[128,256]{1,0:T(8,128)}, f32[512,256]{1,0:T(8,128)}) custom-call(bf16[16,128,256]{2,1,0:T(8,128)(2,1)S(1)} %all-to-all-done.4.f, bf16[128,256]{1,0:T(8,128)(2,1)} %sf.3, bf16[512,256]{1,0:T(8,128)(2,1)} %sp.3, f32[512,256]{1,0:T(8,128)} %get-tuple-element.36.half, bf16[512,256]{1,0:T(8,128)(2,1)S(1)} %collective-permute-done.20.refs_0_, ...), custom_call_target="tpu_custom_call" | custom-call | tf_op jit(solution)/shard_map/project_back/pallas_call | solution.py:215
  (9 shorter events, 0.1 us)
Async XLA Ops:
  3.6 8.3 %copy-start.1 = (bf16[512,512]{1,0:T(8,128)(2,1)S(1)}, bf16[512,512]{1,0:T(8,128)(2,1)}, u32[]{:S(2)}) copy-start(bf16[512,512]{1,0:T(8,128)(2,1)} %get-tuple-element.22.refs_0_) | copy-start | bytes 1572868
  3.6 39.9 %all-to-all-start = ((bf16[16,128,512]{2,1,0:T(8,128)(2,1)}), bf16[16,128,512]{2,1,0:T(8,128)(2,1)S(1)}, u32[]{:S(2)}, u32[]{:S(2)}) async-start(bf16[16,128,512]{2,1,0:T(8,128)(2,1)} %get-tuple-element.21), calls=%async_computation | async-start | bytes 4194304 | tf_op jit(solution)/shard_map/all_to_all | solution.py:244
  11.9 25.9 %collective-permute-start.5 = (bf16[512,512]{1,0:T(8,128)(2,1)S(1)}, bf16[512,512]{1,0:T(8,128)(2,1)S(1)}, u32[]{:S(2)}, u32[]{:S(2)}) collective-permute-start(bf16[512,512]{1,0:T(8,128)(2,1)S(1)} %copy-done.1), channel_id=1, source_target_pairs={{0,96},{16,112},{32,64},{48,80},{64,32},{80,48},{96,0},{112,16},{1... | collective-permute-start | bytes 1572872 | tf_op jit(solution)/shard_map/ppermute | solution.py:227
  14.7 23.1 %collective-permute-start.3 = (bf16[512,512]{1,0:T(8,128)(2,1)S(1)}, bf16[512,512]{1,0:T(8,128)(2,1)}, u32[]{:S(2)}, u32[]{:S(2)}) collective-permute-start(bf16[512,512]{1,0:T(8,128)(2,1)S(1)} %copy-done.1), channel_id=1, source_target_pairs={{0,64},{16,80},{32,96},{48,112},{64,0},{80,16},{96,32},{112,48},{1... | collective-permute-start | bytes 1572872 | tf_op jit(solution)/shard_map/ppermute | solution.py:227
  15.5 23.0 %collective-permute-start.1 = (bf16[512,512]{1,0:T(8,128)(2,1)S(1)}, bf16[512,512]{1,0:T(8,128)(2,1)}, u32[]{:S(2)}, u32[]{:S(2)}) collective-permute-start(bf16[512,512]{1,0:T(8,128)(2,1)S(1)} %copy-done.1), channel_id=1, source_target_pairs={{0,32},{16,48},{32,0},{48,16},{64,96},{80,112},{96,64},{112,80},{1... | collective-permute-start | bytes 1572872 | tf_op jit(solution)/shard_map/ppermute | solution.py:227
  16.1 22.5 %collective-permute-start = (bf16[512,512]{1,0:T(8,128)(2,1)S(1)}, bf16[512,512]{1,0:T(8,128)(2,1)}, u32[]{:S(2)}, u32[]{:S(2)}) collective-permute-start(bf16[512,512]{1,0:T(8,128)(2,1)S(1)} %copy-done.1), channel_id=1, source_target_pairs={{0,16},{16,0},{32,48},{48,32},{64,80},{80,64},{96,112},{112,96},{1... | collective-permute-start | bytes 1572872 | tf_op jit(solution)/shard_map/ppermute | solution.py:227
  37.8 5.7 %copy-start.2 = (bf16[512,512]{1,0:T(8,128)(2,1)}, bf16[512,512]{1,0:T(8,128)(2,1)S(1)}, u32[]{:S(2)}) copy-start(bf16[512,512]{1,0:T(8,128)(2,1)S(1)} %collective-permute-done.5.refs_6_) | copy-start | bytes 1572868
  37.8 2.0 %collective-permute-start.6 = (bf16[512,512]{1,0:T(8,128)(2,1)S(1)}, bf16[512,512]{1,0:T(8,128)(2,1)}, u32[]{:S(2)}, u32[]{:S(2)}) collective-permute-start(bf16[512,512]{1,0:T(8,128)(2,1)S(1)} %collective-permute-done.5.refs_6_), channel_id=1, source_target_pairs={{0,16},{16,0},{32,48},{48,32},{64,80},{80,64},{96,112},{112,96},{1... | collective-permute-start | bytes 1572872 | tf_op jit(solution)/shard_map/ppermute | solution.py:227
  37.8 3.0 %collective-permute-start.4 = (bf16[512,512]{1,0:T(8,128)(2,1)}, bf16[512,512]{1,0:T(8,128)(2,1)}, u32[]{:S(2)}, u32[]{:S(2)}) collective-permute-start(bf16[512,512]{1,0:T(8,128)(2,1)} %collective-permute-done.3.refs_4_), channel_id=1, source_target_pairs={{0,16},{16,0},{32,48},{48,32},{64,80},{80,64},{96,112},{112,96},{1... | collective-permute-start | bytes 1572872 | tf_op jit(solution)/shard_map/ppermute | solution.py:227
  38.5 3.0 %collective-permute-start.2 = (bf16[512,512]{1,0:T(8,128)(2,1)}, bf16[512,512]{1,0:T(8,128)(2,1)}, u32[]{:S(2)}, u32[]{:S(2)}) collective-permute-start(bf16[512,512]{1,0:T(8,128)(2,1)} %collective-permute-done.1.refs_2_), channel_id=1, source_target_pairs={{0,16},{16,0},{32,48},{48,32},{64,80},{80,64},{96,112},{112,96},{1... | collective-permute-start | bytes 1572872 | tf_op jit(solution)/shard_map/ppermute | solution.py:227
  43.5 1.3 copy-start
  52.2 1.3 collective-permute-start.7
  53.5 5.0 %collective-permute-start.10 = (f32[1,4096]{1,0:T(1,128)S(1)}, f32[1,4096]{1,0:T(1,128)S(1)}, u32[]{:S(2)}, u32[]{:S(2)}) collective-permute-start(f32[1,4096]{1,0:T(1,128)S(1)} %add.9.c0), channel_id=1, source_target_pairs={{0,96},{16,112},{32,64},{48,80},{64,32},{80,48},{96,0},{112,16},{1... | collective-permute-start | bytes 49160 | tf_op jit(solution)/shard_map/ppermute | solution.py:227
  56.4 5.2 %collective-permute-start.9 = (f32[1,4096]{1,0:T(1,128)S(1)}, f32[1,4096]{1,0:T(1,128)S(1)}, u32[]{:S(2)}, u32[]{:S(2)}) collective-permute-start(f32[1,4096]{1,0:T(1,128)S(1)} %add.9.c0), channel_id=1, source_target_pairs={{0,64},{16,80},{32,96},{48,112},{64,0},{80,16},{96,32},{112,48},{1... | collective-permute-start | bytes 49160 | tf_op jit(solution)/shard_map/ppermute | solution.py:227
  57.2 4.5 %collective-permute-start.8 = (f32[1,4096]{1,0:T(1,128)S(1)}, f32[1,4096]{1,0:T(1,128)S(1)}, u32[]{:S(2)}, u32[]{:S(2)}) collective-permute-start(f32[1,4096]{1,0:T(1,128)S(1)} %add.9.c0), channel_id=1, source_target_pairs={{0,32},{16,48},{32,0},{48,16},{64,96},{80,112},{96,64},{112,80},{1... | collective-permute-start | bytes 49160 | tf_op jit(solution)/shard_map/ppermute | solution.py:227
  80.3 1.3 collective-permute-start.11
  81.6 11.8 %collective-permute-start.14 = (f32[1,4096]{1,0:T(1,128)S(1)}, f32[1,4096]{1,0:T(1,128)S(1)}, u32[]{:S(2)}, u32[]{:S(2)}) collective-permute-start(f32[1,4096]{1,0:T(1,128)S(1)} %add.10.c0), channel_id=1, source_target_pairs={{0,96},{16,112},{32,64},{48,80},{64,32},{80,48},{96,0},{112,16},{1... | collective-permute-start | bytes 49160 | tf_op jit(solution)/shard_map/ppermute | solution.py:227
  82.4 11.0 %collective-permute-start.13 = (f32[1,4096]{1,0:T(1,128)S(1)}, f32[1,4096]{1,0:T(1,128)S(1)}, u32[]{:S(2)}, u32[]{:S(2)}) collective-permute-start(f32[1,4096]{1,0:T(1,128)S(1)} %add.10.c0), channel_id=1, source_target_pairs={{0,64},{16,80},{32,96},{48,112},{64,0},{80,16},{96,32},{112,48},{1... | collective-permute-start | bytes 49160 | tf_op jit(solution)/shard_map/ppermute | solution.py:227
  83.8 9.7 %collective-permute-start.12 = (f32[1,4096]{1,0:T(1,128)S(1)}, f32[1,4096]{1,0:T(1,128)S(1)}, u32[]{:S(2)}, u32[]{:S(2)}) collective-permute-start(f32[1,4096]{1,0:T(1,128)S(1)} %add.10.c0), channel_id=1, source_target_pairs={{0,32},{16,48},{32,0},{48,16},{64,96},{80,112},{96,64},{112,80},{1... | collective-permute-start | bytes 49160 | tf_op jit(solution)/shard_map/ppermute | solution.py:227
  111.0 1.3 collective-permute-start.15
  112.3 5.1 %collective-permute-start.18 = (f32[1,4096]{1,0:T(1,128)S(1)}, f32[1,4096]{1,0:T(1,128)S(1)}, u32[]{:S(2)}, u32[]{:S(2)}) collective-permute-start(f32[1,4096]{1,0:T(1,128)S(1)} %add.11.c0), channel_id=1, source_target_pairs={{0,96},{16,112},{32,64},{48,80},{64,32},{80,48},{96,0},{112,16},{1... | collective-permute-start | bytes 49160 | tf_op jit(solution)/shard_map/ppermute | solution.py:227
  113.0 5.2 %collective-permute-start.17 = (f32[1,4096]{1,0:T(1,128)S(1)}, f32[1,4096]{1,0:T(1,128)S(1)}, u32[]{:S(2)}, u32[]{:S(2)}) collective-permute-start(f32[1,4096]{1,0:T(1,128)S(1)} %add.11.c0), channel_id=1, source_target_pairs={{0,64},{16,80},{32,96},{48,112},{64,0},{80,16},{96,32},{112,48},{1... | collective-permute-start | bytes 49160 | tf_op jit(solution)/shard_map/ppermute | solution.py:227
  114.5 3.9 %collective-permute-start.16 = (f32[1,4096]{1,0:T(1,128)S(1)}, f32[1,4096]{1,0:T(1,128)S(1)}, u32[]{:S(2)}, u32[]{:S(2)}) collective-permute-start(f32[1,4096]{1,0:T(1,128)S(1)} %add.11.c0), channel_id=1, source_target_pairs={{0,32},{16,48},{32,0},{48,16},{64,96},{80,112},{96,64},{112,80},{1... | collective-permute-start | bytes 49160 | tf_op jit(solution)/shard_map/ppermute | solution.py:227
  151.6 3.8 %collective-permute-start.19 = (bf16[4,512,256]{2,1,0:T(8,128)(2,1)}, bf16[4,512,256]{2,1,0:T(8,128)(2,1)S(1)}, u32[]{:S(2)}, u32[]{:S(2)}) collective-permute-start(bf16[4,512,256]{2,1,0:T(8,128)(2,1)} %get-tuple-element.31), channel_id=1, source_target_pairs={{0,16},{16,0},{32,48},{48,32},{64,80},{80,64},{96,112},{112,96},{1... | collective-permute-start | bytes 3145736 | tf_op jit(solution)/shard_map/ppermute | solution.py:227
  151.7 23.5 %all-to-all-start.4 = ((bf16[16,128,256]{2,1,0:T(8,128)(2,1)}), bf16[16,128,256]{2,1,0:T(8,128)(2,1)S(1)}, u32[]{:S(2)}, u32[]{:S(2)}) async-start(bf16[16,128,256]{2,1,0:T(8,128)(2,1)} %get-tuple-element.29), calls=%async_computation.4 | async-start | bytes 2097152 | tf_op jit(solution)/shard_map/all_to_all | solution.py:322
  157.8 17.4 %collective-permute-start.20 = (bf16[512,256]{1,0:T(8,128)(2,1)S(1)}, bf16[512,256]{1,0:T(8,128)(2,1)S(1)}, u32[]{:S(2)}, u32[]{:S(2)}) collective-permute-start(bf16[512,256]{1,0:T(8,128)(2,1)S(1)} %get-tuple-element.32), channel_id=1, source_target_pairs={{0,32},{16,48},{32,0},{48,16},{64,96},{80,112},{96,64},{112,80},{1... | collective-permute-start | bytes 786440 | tf_op jit(solution)/shard_map/ppermute | solution.py:227
  159.6 15.6 %collective-permute-start.21 = (bf16[512,256]{1,0:T(8,128)(2,1)S(1)}, bf16[512,256]{1,0:T(8,128)(2,1)S(1)}, u32[]{:S(2)}, u32[]{:S(2)}) collective-permute-start(bf16[512,256]{1,0:T(8,128)(2,1)S(1)} %get-tuple-element.33), channel_id=1, source_target_pairs={{0,64},{16,80},{32,96},{48,112},{64,0},{80,16},{96,32},{112,48},{1... | collective-permute-start | bytes 786440 | tf_op jit(solution)/shard_map/ppermute | solution.py:227
  161.8 15.0 %collective-permute-start.22 = (bf16[512,256]{1,0:T(8,128)(2,1)S(1)}, bf16[512,256]{1,0:T(8,128)(2,1)S(1)}, u32[]{:S(2)}, u32[]{:S(2)}) collective-permute-start(bf16[512,256]{1,0:T(8,128)(2,1)S(1)} %get-tuple-element.34), channel_id=1, source_target_pairs={{0,96},{16,112},{32,64},{48,80},{64,32},{80,48},{96,0},{112,16},{1... | collective-permute-start | bytes 786440 | tf_op jit(solution)/shard_map/ppermute | solution.py:227
